TPU v7x, 32 devices: a whole 2x2x4 slice. The times are simulated.
32 devices in a mesh: leaf: 8 (over z, y), help: 4 (over x, core).
Axes of the slice: x: 2, y: 2, z: 4, core: 2. Of those that a mesh axis runs over, the one named last changes fastest.
Arguments:
- points: float32 [64, 32768], P(None, ('leaf', 'help')), may hold values from -3 to 3
- weights: float32 [256, 32768], P(None, ('leaf', 'help')), may hold values from -0.12 to 0.12
- interp: float32 [64, 512, 256], P(('leaf', 'help')), may hold values from -0.25 to 0.25
- transfer: float32 [6, 512, 256], replicated, may hold values from -0.25 to 0.25
- near_count: int32 [8, 8], P('leaf', 'help'), may hold values from 1 to 32, 128 in all within a row
- near_src: int32 [64, 32], P(('leaf', 'help')), may hold values from 0 to 63, as said below
- skel_group: int32 [8, 256], P('leaf'), may hold values from 0 to 4095, as said below
- skel_node: int32 [6, 256], replicated, may hold values from 0 to 511, as said below
- far_nodes: int32 [14, 4], replicated, may hold values from 0 to 7, as said below
Outputs:
- product: float32 [256, 32768], P(None, ('leaf', 'help'))
Inputs may be any that keep to these rules, and one draw needn't show every extreme that they name: `near_src`: slot 0 of leaf i names leaf i itself; every source of a leaf of subtree g is a leaf of subtree g - 1, g or g + 1. Slots at or after the leaf's near_count are not used. `near_count`: the 8 counts of one subtree sum to exactly 128. `skel_group`: each row holds 256 distinct indices into its subtree's points, counted from the subtree's first point. `skel_node`: each row holds 256 distinct indices into its two children's skeleton points, the first child's first. `far_nodes`: rows 0 to 7 are the level-0 nodes, the next 4 rows the level-1 nodes, and so on down to the 2 nodes of the highest listed level; each entry is a node number of that row's level. On level 0, the first entry of node k's row is k - 1 (modulo 8) and no other entry is k, k + 1 or k - 1 (modulo 8); on a higher level of c >= 4 nodes, no entry of node k's row is k, k + 1 or k - 1 (modulo c); on the level of 2 nodes, every entry is the other node.
All inputs are finite; a program needn't handle non-finite values. No bound on the sum of `near_count` on one device may be relied on, other than what follows from the above.
Results may differ from a plain program's by a relative error of at most 0.0003.
Values sent between devices are 32-bit elements; how exact they have to be, the bound alone decides.
No kernel may reach another device: no remote copies, remote signals or barrier semaphores. Data moves between devices by JAX's collectives and lax.ppermute only.
A program may use at most 192 MiB of HBM per device.

v0:
```python
import math
from functools import partial

import jax
import jax.numpy as jnp
from jax import lax
from jax.experimental import pallas as pl
from jax.experimental.pallas import tpu as pltpu
from jax.sharding import PartitionSpec as P

F = 64
R = 256
LEAF = 512
SK = 256
FL = 4
EXTRA = 8
SIZES = (128, 128)

BF = jnp.bfloat16
F32 = jnp.float32
LOG2E = 1.0 / math.log(2.0)
SCALE = math.sqrt(0.5 * LOG2E)
BIAS = 0.0625 * F * LOG2E
VMEM_LIMIT = 24 * 1024 * 1024
VMEM_WHOLE = 64 * 1024 * 1024


def dot(a, b):
    return jnp.dot(a, b, preferred_element_type=F32)


def dot_t(a, b):
    return lax.dot_general(a, b, (((1,), (1,)), ((), ())), preferred_element_type=F32)


def halves(x):
    hi = x.astype(BF)
    lo = (x - hi.astype(F32)).astype(BF)
    return hi, lo


def dot3(a, b, mul=dot):
    a_hi, a_lo = halves(a)
    b_hi, b_lo = halves(b)
    return mul(a_hi, b_hi) + mul(a_lo, b_hi) + mul(a_hi, b_lo)


def target_side(x):
    hi, lo = halves(x)
    both = hi.astype(F32) + lo.astype(F32)
    off = BIAS - 0.5 * jnp.sum(both * both, axis=0, keepdims=True)
    return jnp.concatenate([hi, lo, hi, lo], axis=0), off


def source_side(x):
    xt = x.T
    hi, lo = halves(xt)
    both = hi.astype(F32) + lo.astype(F32)
    off = BIAS - 0.5 * jnp.sum(both * both, axis=1, keepdims=True)
    return jnp.concatenate([hi, hi, lo, lo], axis=1), off


def near_body(
    xs, sets, leaves_at, rows, row, nacc, nout, pos_ref, *refs
):
    nset = len(sets)
    start, stop = leaves_at
    msgs, (t_ref, tb_ref), refs = refs[: 2 * xs], refs[2 * xs : 2 * xs + 2], refs[2 * xs + 2 :]
    if nacc:
        s_scr, sb_scr, w_scr, o_scr, k_scr, times_scr, list_ref, times_ref, sems = refs[-9:]
        outs = refs[-9 - nout : -9]
    else:
        o_scr, s_scr, sb_scr, w_scr, k_scr, times_scr, list_ref, times_ref, sems = refs[-9:]
    copies = [
        pltpu.make_async_copy(msgs[b].at[F : F + EXTRA, :128], times_ref.at[b], sems.at[b])
        for b in range(start // 2, stop // 2)
    ]
    for copy in copies:
        copy.start()
    at = 0
    for k, (_, ready, chunks) in enumerate(sets):
        heads = refs[at : at + 1 + ready]
        parts = refs[at + 1 + ready : at + 1 + ready + chunks]
        at += 1 + ready + chunks
        for leaf in range(2):
            cols = slice(leaf * LEAF, (leaf + 1) * LEAF)
            j = 2 * k + leaf
            if ready:
                s_scr[j] = heads[0][leaf]
                sb_scr[j] = heads[1][leaf]
            else:
                side, off = source_side(heads[0][:F, cols] * SCALE)
                s_scr[j] = side
                sb_scr[j] = jnp.broadcast_to(off, (LEAF, 128))
            top = 0
            for part in parts:
                hi, lo = halves(part[:, cols])
                w_scr[j, top : top + part.shape[0], :] = hi
                w_scr[j, rows + top : rows + top + part.shape[0], :] = lo
                top += part.shape[0]
    for t in range(start, stop):
        if nacc:
            o_scr[t - start] = sum(
                ref[t - (4 * xs - ref.shape[0]), row : row + rows, :] for ref in refs[at : at + nacc]
            )
        else:
            o_scr[t - start] = jnp.zeros((rows, LEAF), F32)

    x, core, group, leaves = pos_ref[0], pos_ref[1], pos_ref[2], pos_ref[3]
    odd = group % 2
    column = []
    for kind, _, _ in sets:
        relative = {"own": 1, "pair": 2 - 2 * odd, "next": 2 * odd}[kind]
        column.append(relative * leaves + 2 * (2 * x + core))

    for copy in copies:
        copy.wait()
    count = jnp.int32(0)
    list_ref[0] = 0
    for t in range(start, stop):
        for j in range(2 * nset):
            times = times_ref[t // 2, t % 2, column[j // 2] + j % 2]

            @pl.when(times > 0)
            def _(count=count, t=t, j=j, times=times):
                list_ref[count] = t * 8 + j
                times_scr[count] = times

            count = count + (times > 0).astype(jnp.int32)

    def block(index, slot):
        code = list_ref[jnp.minimum(index, jnp.maximum(count - 1, 0))]
        t, j = code // 8, code % 8
        side = t_ref[t]
        off = tb_ref[t][:1, :]
        for half in range(2):
            part = slice(half * 256, (half + 1) * 256)
            cross = dot(s_scr[j, part, :], side)
            src_off = sb_scr[j, part, :]
            src_off = jnp.concatenate([src_off] * (LEAF // 128), axis=1)
            k_hi, k_lo = halves(jnp.exp2(cross + src_off + off))
            k_scr[slot, part, :] = k_hi
            k_scr[slot, LEAF + half * 256 : LEAF + (half + 1) * 256, :] = k_lo

    def apply(index, slot):
        code = list_ref[index]
        t, j = code // 8 - start, code % 8
        factor = times_scr[index]
        for half in range(2):
            cols = slice(half * 256, (half + 1) * 256)
            both = dot(w_scr[j], k_scr[slot, :LEAF, cols])
            low = dot(w_scr[j, :rows, :], k_scr[slot, LEAF:, cols])
            o_scr[t, :, cols] = o_scr[t, :, cols] + factor * (both[:rows] + both[rows:] + low)

    @pl.when(count > 0)
    def _():
        block(0, 0)

    def pair(index, carry):
        block(2 * index + 1, 1)
        apply(2 * index, 0)

        @pl.when(2 * index + 1 < count)
        def _():
            block(2 * index + 2, 0)
            apply(2 * index + 1, 1)

        return carry

    lax.fori_loop(0, (count + 1) // 2, pair, jnp.int32(0))
    if nacc:
        t, top = 0, 0
        for ref in outs:
            tall = ref.shape[0]
            for leaf in range(2):
                cols = slice(leaf * LEAF, (leaf + 1) * LEAF)
                ref[:, cols] = o_scr[t + leaf, top : top + tall, :]
            t, top = (t, top + tall) if top + tall < rows else (t + 2, 0)


def near_call(name, pos, msgs, targets, leaves_at, sources, rows, row=0, acc=(), after=()):
    nset = len(sources)
    start, stop = leaves_at
    vmem = pl.BlockSpec(memory_space=pltpu.VMEM)
    smem = pl.BlockSpec(memory_space=pltpu.SMEM)
    operands = [a for _, heads, chunks in sources for a in (*heads, *chunks)]
    scratch = [
        pltpu.VMEM((2 * nset, LEAF, 4 * F), BF),
        pltpu.VMEM((2 * nset, LEAF, 128), F32),
        pltpu.VMEM((2 * nset, 2 * rows, LEAF), BF),
        pltpu.VMEM((stop - start, rows, LEAF), F32),
        pltpu.VMEM((2, 2 * LEAF, LEAF), BF),
        pltpu.SMEM((2 * nset * (stop - start),), F32),
        pltpu.SMEM((2 * nset * (stop - start),), jnp.int32),
        pltpu.SMEM((len(msgs), EXTRA, 128), F32),
        pltpu.SemaphoreType.DMA((len(msgs),)),
    ]
    if not acc:
        out = [jax.ShapeDtypeStruct((stop - start, rows, LEAF), F32)]
        scratch.pop(3)
    else:
        operands += list(acc)
        talls = SIZES if rows == R else (rows,)
        out = [jax.ShapeDtypeStruct((tall, 2 * LEAF), F32) for tall in talls] * ((stop - start) // 2)
    sets = tuple((kind, len(heads) - 1, len(chunks)) for kind, heads, chunks in sources)
    return pl.pallas_call(
        partial(
            near_body, len(msgs) // 2, sets, leaves_at, rows, row, len(acc), len(out)
        ),
        name=name,
        out_shape=out,
        in_specs=[smem]
        + [pl.BlockSpec(memory_space=pl.ANY)] * len(msgs)
        + [vmem] * (2 + len(operands))
        + [pl.BlockSpec(memory_space=pl.ANY)] * len(after),
        out_specs=[vmem] * len(out),
        scratch_shapes=scratch,
        compiler_params=pltpu.CompilerParams(vmem_limit_bytes=VMEM_LIMIT),
    )(pos, *msgs, *targets, *operands, *after)


def source_body(pts_ref, side_ref, off_ref):
    for leaf in range(2):
        cols = slice(leaf * LEAF, (leaf + 1) * LEAF)
        side, off = source_side(pts_ref[:F, cols] * SCALE)
        side_ref[leaf] = side
        off_ref[leaf] = jnp.broadcast_to(off, (LEAF, 128))


def source_call(pts):
    vmem = pl.BlockSpec(memory_space=pltpu.VMEM)
    return pl.pallas_call(
        source_body,
        name="source_side",
        out_shape=[
            jax.ShapeDtypeStruct((2, LEAF, 4 * F), BF),
            jax.ShapeDtypeStruct((2, LEAF, 128), F32),
        ],
        in_specs=[vmem],
        out_specs=[vmem, vmem],
        compiler_params=pltpu.CompilerParams(vmem_limit_bytes=VMEM_LIMIT),
    )(pts)


def share_rows(xs):
    return R // (2 * xs) * SK // (2 * LEAF)


def leaf_body(xs, pos_ref, count_ref, src_ref, pts_in, w_in, interp_in, *refs):
    msgs = refs[: 2 * xs]
    pts_ref, w_ref, interp_ref, scr, sems = refs[2 * xs :]
    copies = [
        pltpu.make_async_copy(pts_in, pts_ref, sems.at[0]),
        pltpu.make_async_copy(w_in, w_ref, sems.at[1]),
        pltpu.make_async_copy(interp_in, interp_ref, sems.at[2]),
    ]
    for copy in copies:
        copy.start()
    x, core, group, leaves = pos_ref[0], pos_ref[1], pos_ref[2], pos_ref[3]
    lane = lax.broadcasted_iota(jnp.int32, (1, 128), 1) + (group - 1) * leaves
    times = []
    for leaf in range(2):
        row = jnp.zeros((1, 128), F32)
        for slot in range(src_ref.shape[1]):
            name = jnp.where(slot < count_ref[0, leaf], src_ref[leaf, slot], -1 - 128 * leaves)
            row = row + (lane == name).astype(F32)
        times.append(row)
    times = jnp.concatenate(times + [jnp.zeros((EXTRA - 2, 128), F32)], axis=0)
    for copy in copies:
        copy.wait()
    total = jnp.zeros((R, SK), F32)
    for leaf in range(2):
        total = total + dot3(w_ref[:, leaf * LEAF : (leaf + 1) * LEAF], interp_ref[leaf])
    scr[...] = total
    rows = R // (2 * xs)
    tall = share_rows(xs)
    for n, msg in enumerate(msgs):
        helper = 2 * lax.rem(x + n // 2, xs) + (core if n % 2 == 0 else 1 - core)
        msg[:F, :] = pts_ref[...]
        msg[F : F + EXTRA, :] = jnp.zeros((EXTRA, 2 * LEAF), F32)
        msg[F : F + EXTRA, :128] = times
        for i in range(rows // tall):
            at = pl.multiple_of(helper * rows + i * tall, tall)
            msg[F + EXTRA :, i * SK : (i + 1) * SK] = scr[pl.ds(at, tall), :]


def leaf_call(xs, pos, near_count, near_src, points, weights, interp):
    vmem = pl.BlockSpec(memory_space=pltpu.VMEM)
    smem = pl.BlockSpec(memory_space=pltpu.SMEM)
    anywhere = pl.BlockSpec(memory_space=pl.ANY)
    height = F + EXTRA + share_rows(xs)
    return pl.pallas_call(
        partial(leaf_body, xs),
        name="leaf_up",
        out_shape=[jax.ShapeDtypeStruct((height, 2 * LEAF), F32)] * (2 * xs),
        in_specs=[smem, smem, smem, anywhere, anywhere, anywhere],
        out_specs=[vmem] * (2 * xs),
        scratch_shapes=[
            pltpu.VMEM(points.shape, F32),
            pltpu.VMEM(weights.shape, F32),
            pltpu.VMEM(interp.shape, F32),
            pltpu.VMEM((R, SK), F32),
            pltpu.SemaphoreType.DMA((3,)),
        ],
        compiler_params=pltpu.CompilerParams(vmem_limit_bytes=VMEM_WHOLE),
    )(pos, near_count, near_src, points, weights, interp)


def skel_body(xs, pos_ref, index_ref, *refs):
    msgs, (out_ref, side_ref, off_ref) = refs[:-3], refs[-3:]
    rows = R // (2 * xs)
    tall = share_rows(xs)
    total = jnp.zeros((2 * F, SK), F32)
    value = jnp.zeros((tall, 2 * LEAF), F32)
    spot = lax.broadcasted_iota(jnp.int32, (2 * LEAF, SK), 0)
    x, core = pos_ref[0], pos_ref[1]
    for b, msg in enumerate(msgs):
        helper = 2 * lax.rem(x + b // 2, xs) + (core if b % 2 == 0 else 1 - core)
        side, off = target_side(msg[:F, :] * SCALE)
        for leaf in range(2):
            part = slice(leaf * LEAF, (leaf + 1) * LEAF)
            side_ref[2 * b + leaf] = side[:, part]
            off_ref[2 * b + leaf] = jnp.broadcast_to(off[:, part], (8, LEAF))
        hot = spot + helper * (2 * LEAF) == index_ref[...]
        total = total + dot(side[: 2 * F], hot.astype(F32).astype(BF))
        value = value + msg[F + EXTRA :, :]
    out_ref[:F, :] = total[:F] + total[F:]
    for i in range(rows // tall):
        out_ref[F + i * tall : F + (i + 1) * tall, :] = value[:, i * SK : (i + 1) * SK]


def skel_call(xs, pos, index, msgs):
    rows = R // (2 * xs)
    leaves = 2 * len(msgs)
    vmem = pl.BlockSpec(memory_space=pltpu.VMEM)
    payload, *targets = pl.pallas_call(
        partial(skel_body, xs),
        name="skeleton",
        out_shape=[
            jax.ShapeDtypeStruct((F + rows, SK), F32),
            jax.ShapeDtypeStruct((leaves, 4 * F, LEAF), BF),
            jax.ShapeDtypeStruct((leaves, 8, LEAF), F32),
        ],
        in_specs=[pl.BlockSpec(memory_space=pltpu.SMEM)] + [vmem] * (1 + len(msgs)),
        out_specs=[vmem] * 3,
        compiler_params=pltpu.CompilerParams(vmem_limit_bytes=VMEM_LIMIT),
        cost_estimate=pl.CostEstimate(
            flops=5_000_000_000, bytes_accessed=8_000_000, transcendentals=0
        ),
    )(pos, index, *msgs)
    return payload, targets


def stack_body(*refs):
    for n, ref in enumerate(refs[:-1]):
        refs[-1][n] = ref[...]


def stack_call(pieces):
    vmem = pl.BlockSpec(memory_space=pltpu.VMEM)
    return pl.pallas_call(
        stack_body,
        name="stack",
        out_shape=jax.ShapeDtypeStruct((len(pieces), *pieces[0].shape), F32),
        in_specs=[vmem] * len(pieces),
        out_specs=vmem,
        compiler_params=pltpu.CompilerParams(vmem_limit_bytes=VMEM_LIMIT),
    )(*pieces)


def upper_start(level, groups):
    return sum((groups >> step for step in range(1, level)))


def list_start(level, groups):
    return sum((groups >> step for step in range(level)))


def far_body(groups, rows, pos_ref, far_ref, node_ref, transfer_ref, alike_ref, beside_ref, *refs):
    out_ref, p_scr, u_scr, f_scr = refs[-4:]
    levels = groups.bit_length() - 1
    group = pos_ref[2]
    start = [list_start(level, groups) for level in range(levels)]
    for n in range(groups // 2):
        same, other = group ^ (2 * n), group ^ (2 * n + 1)
        p_scr[same] = alike_ref[n, :F, :]
        u_scr[same] = alike_ref[n, F:, :]
        p_scr[other] = beside_ref[n, :F, :]
        u_scr[other] = beside_ref[n, F:, :]
    spot = lax.broadcasted_iota(jnp.int32, (2 * SK, SK), 0)
    for level in range(1, levels):
        for n in range(groups >> level):
            row = upper_start(level, groups) + n
            left = start[level - 1] + 2 * n
            hot = (spot == node_ref[row : row + 1, :]).astype(F32).astype(BF)
            hi, lo = halves(jnp.concatenate([p_scr[left], p_scr[left + 1]], axis=1))
            both = dot(jnp.concatenate([hi, lo], axis=0), hot)
            p_scr[start[level] + n] = both[:F] + both[F:]
            vals = jnp.concatenate([u_scr[left], u_scr[left + 1]], axis=1)
            u_scr[start[level] + n] = dot3(vals, transfer_ref[row])
    for level in range(levels):
        node = group >> level
        side, off = target_side(p_scr[start[level] + node])
        f_scr[level] = jnp.zeros((rows, SK), F32)

        def one(n, carry, level=level, node=node, side=side, off=off):
            hits = jnp.int32(0)
            for slot in range(FL):
                hits = hits + (far_ref[slot, start[level] + node] == n).astype(jnp.int32)

            @pl.when(hits > 0)
            def _():
                src, src_off = source_side(p_scr[start[level] + n])
                block = jnp.exp2(dot(src, side) + src_off + off)
                term = dot3(u_scr[start[level] + n], block)
                f_scr[level] = f_scr[level] + hits.astype(F32) * term

            return carry

        lax.fori_loop(0, groups >> level, one, jnp.int32(0))
    local = f_scr[levels - 1]
    for level in range(levels - 1, 0, -1):
        row = upper_start(level, groups) + (group >> level)
        bit = (group >> (level - 1)) & 1
        matrix = transfer_ref[row, pl.ds(pl.multiple_of(bit * SK, SK), SK), :]
        local = f_scr[level - 1] + dot3(local, matrix, dot_t)
    out_ref[...] = local


def far_call(groups, pos, far_nodes, skel_node, transfer, alike, beside, after):
    rows = alike.shape[1] - F
    vmem = pl.BlockSpec(memory_space=pltpu.VMEM)
    smem = pl.BlockSpec(memory_space=pltpu.SMEM)
    nodes = 2 * groups
    return pl.pallas_call(
        partial(far_body, groups, rows),
        name="far",
        out_shape=jax.ShapeDtypeStruct((rows, SK), F32),
        in_specs=[smem, smem, vmem, vmem, vmem, vmem]
        + [pl.BlockSpec(memory_space=pl.ANY)] * len(after),
        out_specs=vmem,
        scratch_shapes=[
            pltpu.VMEM((nodes, F, SK), F32),
            pltpu.VMEM((nodes, rows, SK), F32),
            pltpu.VMEM((groups.bit_length(), rows, SK), F32),
        ],
        compiler_params=pltpu.CompilerParams(vmem_limit_bytes=VMEM_LIMIT),
    )(pos, far_nodes.T, skel_node, transfer, alike, beside, *after)


def final_body(xs, pos_ref, interp_ref, *refs):
    values, sums = refs[: 2 * xs], refs[2 * xs : -2]
    out_ref, v_scr = refs[-2:]
    rows = R // (2 * xs)
    x, core = pos_ref[0], pos_ref[1]
    for n, ref in enumerate(values):
        helper = 2 * lax.rem(x + n // 2, xs) + (core if n % 2 == 0 else 1 - core)
        v_scr[pl.ds(pl.multiple_of(helper * rows, rows), rows), :] = ref[...]
    value = v_scr[...]
    for leaf in range(2):
        cols = slice(leaf * LEAF, (leaf + 1) * LEAF)
        total = dot3(value, interp_ref[leaf], dot_t)
        for c in range(2):
            part = slice(c * SIZES[0], SIZES[0] + c * SIZES[1])
            out_ref[part, cols] = total[part] + sums[c][:, cols] + sums[2 + c][:, cols]


def add_body(count, *refs):
    for n, out_ref in enumerate(refs[-(len(refs) // (count + 1)) :]):
        total = refs[n * count][...]
        for ref in refs[n * count + 1 : (n + 1) * count]:
            total = total + ref[...]
        out_ref[...] = total


def add_call(*sums):
    vmem = pl.BlockSpec(memory_space=pltpu.VMEM)
    operands = [value for terms in sums for value in terms]
    return pl.pallas_call(
        partial(add_body, len(sums[0])),
        name="add_parts",
        out_shape=[jax.ShapeDtypeStruct(terms[0].shape, F32) for terms in sums],
        in_specs=[vmem] * len(operands),
        out_specs=[vmem] * len(sums),
        compiler_params=pltpu.CompilerParams(vmem_limit_bytes=VMEM_LIMIT),
    )(*operands)


def final_call(xs, pos, interp, home, mate, values):
    vmem = pl.BlockSpec(memory_space=pltpu.VMEM)
    return pl.pallas_call(
        partial(final_body, xs),
        name="join",
        out_shape=jax.ShapeDtypeStruct((R, 2 * LEAF), F32),
        in_specs=[pl.BlockSpec(memory_space=pltpu.SMEM)] + [vmem] * (1 + 2 * xs + 4),
        out_specs=vmem,
        scratch_shapes=[pltpu.VMEM((R, SK), F32)],
        compiler_params=pltpu.CompilerParams(vmem_limit_bytes=VMEM_LIMIT),
    )(pos, interp, *values, *home, *mate)


def help_pairs(xs, dx, dc):
    return [
        (2 * ((x + dx) % xs) + (core ^ dc), 2 * x + core) for x in range(xs) for core in range(2)
    ]


def shards(
    points, weights, interp, transfer, near_count, near_src, skel_group, skel_node, far_nodes
):
    helpers = lax.axis_size("help")
    groups = lax.axis_size("leaf")
    xs = helpers // 2
    helper = lax.axis_index("help")
    group = lax.axis_index("leaf")
    x, core = helper // 2, helper % 2
    leaves = 2 * helpers
    pos = jnp.stack([x, core, group, jnp.int32(leaves)]).astype(jnp.int32)
    rows = R // 2

    def from_help(value, dx, dc):
        return lax.ppermute(value, "help", help_pairs(xs, dx, dc))

    def to_help(value, dx):
        return lax.ppermute(value, "help", help_pairs(xs, -dx, 0))

    def together(*values):
        return lax.optimization_barrier(values)

    beside = [(i, i ^ 1) for i in range(groups)]
    across = [(i, i + 2) for i in range(0, groups - 2, 2)]
    across += [(i, i - 2) for i in range(3, groups, 2)]
    order = [(dx, dc) for dx in range(xs) for dc in range(2)]

    cut = SIZES[0]
    pts_y = lax.ppermute(points, "leaf", beside)
    w_y = [lax.ppermute(chunk, "leaf", beside) for chunk in (weights[:cut], weights[cut:])]
    sent = leaf_call(xs, pos, near_count, near_src, points, weights, interp)
    got = [
        lax.ppermute(sent[n], "help", help_pairs(xs, -dx, dc))
        for n, (dx, dc) in enumerate(order)
        if n
    ]
    pts_z = lax.ppermute(pts_y, "leaf", across)
    pts_z, w_y[0] = together(pts_z, w_y[0])
    w_z = [lax.ppermute(w_y[0], "leaf", across)]
    msgs = [sent[0]] + [got[order.index((-dx % xs, dc)) - 1] for dx, dc in order[1:]]
    payload, targets = skel_call(xs, pos, skel_group, msgs)
    pieces = [payload]
    for mask in range(2, groups, 2):
        pieces.append(lax.ppermute(payload, "leaf", [(i, i ^ mask) for i in range(groups)]))

    payload, w_y[1] = together(payload, w_y[1])
    every, away, home = (0, 2 * helpers), (4, 2 * helpers), (0, 4)
    (own,) = near_call("near_own", pos, msgs, targets, every, [("own", (points,), [weights])], R)
    w_z.append(lax.ppermute(w_y[1], "leaf", across))
    pair_src = ("pair", (pts_y,), w_y)
    (pair,) = near_call("near_pair", pos, msgs, targets, away, [pair_src], R, after=[own])
    z_side = source_call(pts_z)
    sums, part = [], [pair]
    for c in range(2):
        if c == 1:
            pieces, part = together(pieces, part)
            alike = stack_call(pieces)
            side = lax.ppermute(alike, "leaf", beside)
            part = [alike]
        part = near_call(
            "near_next_away", pos, msgs, targets, away, [("next", z_side, w_z[c : c + 1])],
            SIZES[c], c * SIZES[0], [own, pair], part[:1],
        )
        kept, given = part[::2], part[1::2]
        sums.append((kept, [from_help(value, 0, 1) for value in given]))
    parts = []
    for c in range(2):
        kept, mates = sums[c]
        if c == 1:
            mates, side = together(mates, side)
        both = add_call(*zip(kept, mates))
        parts.append([to_help(value, dx + 1) for dx, value in enumerate(both)])
    v_own = far_call(groups, pos, far_nodes, skel_node, transfer, alike, side, both[:1])
    values = [v_own] + [from_help(v_own, dx, dc) for dx, dc in order[1:]]
    sources = [pair_src, ("next", z_side, w_z)]
    home = near_call("near_home", pos, msgs, targets, home, sources, R, 0, [own], [v_own])
    mate = [from_help(value, 0, 1) for value in home[2:]]
    mine = add_call(*[[home[c], *parts[c]] for c in range(2)])
    return final_call(xs, pos, interp, mine, mate, values)


def solution(mesh):
    placed = (
        P(None, ("leaf", "help")),
        P(None, ("leaf", "help")),
        P(("leaf", "help"), None, None),
        P(),
        P("leaf", "help"),
        P(("leaf", "help"), None),
        P("leaf", None),
        P(),
        P(),
    )
    return jax.shard_map(
        shards, mesh=mesh, in_specs=placed, out_specs=P(None, ("leaf", "help")), check_vma=False
    )
```

profile of v0, /device:TPU:21, one launch (start us, length us, event | category | flops | bytes accessed | tf_op | source)
XLA Modules:
  0.0 107.2 jit_solution(12003118260759520180)
XLA Ops:
  0.2 2.3 %fusion = (f32[128,1024]{1,0:T(8,128)}, f32[128,1024]{1,0:T(8,128)}) fusion(f32[256,1024]{1,0:T(8,128)} %refs_7_.1), kind=kLoop, calls=%fused_computation.1 | loop fusion | bytes 2097152 | tf_op jit(solution)/shard_map/slice | solution.py:537
  4.4 4.1 %leaf_up.1 = (f32[88,1024]{1,0:T(8,128)}, f32[88,1024]{1,0:T(8,128)}, f32[88,1024]{1,0:T(8,128)}, f32[88,1024]{1,0:T(8,128)}) custom-call(s32[4]{0:T(128)} %pad_add_fusion.pos_ref, s32[1,2]{1,0:T(1,128)} %count_ref.1, s32[2,32]{1,0:T(2,128)} %src_ref.1, f32[64,1024]{1,0:T(8,128)} %refs_6_.1, f32[256,1024]{1,0:T(8,128)} %refs_7_.1, f32[2,512,256]{2,1,0:T(8,128)} %interp_ref.1), custom_call_target="tpu_custom_call" | custom-call | tf_op jit(solution)/shard_map/leaf_up/pallas_call | solution.py:292
  8.5 1.3 %collective-permute-start = (f32[88,1024]{1,0:T(8,128)}, f32[88,1024]{1,0:T(8,128)S(1)}, u32[]{:S(2)}, u32[]{:S(2)}) collective-permute-start(f32[88,1024]{1,0:T(8,128)} %get-tuple-element.34), channel_id=1, source_target_pairs={{1,0},{0,1},{3,2},{2,3},{5,4},{4,5},{7,6},{6,7},{9,8},{8,9},{11,10... | collective-permute-start | bytes 1081352 | tf_op jit(solution)/shard_map/ppermute | solution.py:540
  11.5 2.1 %collective-permute-start.7 = (f32[64,1024]{1,0:T(8,128)}, f32[64,1024]{1,0:T(8,128)S(1)}, u32[]{:S(2)}, u32[]{:S(2)}) collective-permute-start(f32[64,1024]{1,0:T(8,128)} %collective-permute-done.6.refs_6_), channel_id=1, source_target_pairs={{0,8},{8,16},{16,24},{12,4},{20,12},{28,20},{1,9},{9,17},{17,25},{... | collective-permute-start | bytes 786440 | tf_op jit(solution)/shard_map/ppermute | solution.py:544
  13.6 7.8 %collective-permute-done.7.pts_ref = f32[64,1024]{1,0:T(8,128)S(1)} collective-permute-done((f32[64,1024]{1,0:T(8,128)}, f32[64,1024]{1,0:T(8,128)S(1)}, u32[]{:S(2)}, u32[]{:S(2)}) %collective-permute-start.7) | collective-permute-done | bytes 262176 | tf_op jit(solution)/shard_map/ppermute | solution.py:544
  21.6 2.1 %collective-permute-start.9 = (f32[128,1024]{1,0:T(8,128)}, f32[128,1024]{1,0:T(8,128)S(1)}, u32[]{:S(2)}, u32[]{:S(2)}) collective-permute-start(f32[128,1024]{1,0:T(8,128)} %collective-permute-done.8.refs_7_), channel_id=1, source_target_pairs={{0,8},{8,16},{16,24},{12,4},{20,12},{28,20},{1,9},{9,17},{17,25},{... | collective-permute-start | bytes 1572872 | tf_op jit(solution)/shard_map/ppermute | solution.py:546
  23.7 4.5 %collective-permute-done.2.refs_3_ = f32[88,1024]{1,0:T(8,128)S(1)} collective-permute-done((f32[88,1024]{1,0:T(8,128)}, f32[88,1024]{1,0:T(8,128)S(1)}, u32[]{:S(2)}, u32[]{:S(2)}) %collective-permute-start.2) | collective-permute-done | bytes 360480 | tf_op jit(solution)/shard_map/ppermute | solution.py:540
  30.5 1.3 %skeleton.1 = (f32[128,256]{1,0:T(8,128)S(1)}, bf16[8,256,512]{2,1,0:T(8,128)(2,1)S(1)}, f32[8,8,512]{2,1,0:T(8,128)S(1)}) custom-call(s32[4]{0:T(128)S(1)} %copy-done.6, s32[1,256]{1,0:T(1,128)S(1)} %copy-done.10, f32[88,1024]{1,0:T(8,128)S(1)} %copy-done.1, f32[88,1024]{1,0:T(8,128)S(1)} %collective-permute-done.refs_1_, ...), custom_call_target="tpu_custom_call" | custom-call | flops 5000000000 | bytes 8000000 | tf_op jit(solution)/shard_map/skeleton/pallas_call | solution.py:336
  31.8 2.2 %collective-permute-done.10.refs_8_ = f32[128,1024]{1,0:T(8,128)S(1)} collective-permute-done((f32[128,1024]{1,0:T(8,128)}, f32[128,1024]{1,0:T(8,128)S(1)}, u32[]{:S(2)}, u32[]{:S(2)}) %collective-permute-start.10) | collective-permute-done | bytes 524320 | tf_op jit(solution)/shard_map/ppermute | solution.py:537
  34.0 2.1 %collective-permute-start.11 = (f32[128,1024]{1,0:T(8,128)S(1)}, f32[128,1024]{1,0:T(8,128)S(1)}, u32[]{:S(2)}, u32[]{:S(2)}) collective-permute-start(f32[128,1024]{1,0:T(8,128)S(1)} %collective-permute-done.10.refs_8_), channel_id=1, source_target_pairs={{0,8},{8,16},{16,24},{12,4},{20,12},{28,20},{1,9},{9,17},{17,25},{... | collective-permute-start | bytes 1572872 | tf_op jit(solution)/shard_map/ppermute | solution.py:556
  36.1 1.4 %collective-permute-start.3 = (f32[128,256]{1,0:T(8,128)S(1)}, f32[128,256]{1,0:T(8,128)S(1)}, u32[]{:S(2)}, u32[]{:S(2)}) collective-permute-start(f32[128,256]{1,0:T(8,128)S(1)} %get-tuple-element.47.refs_0_), channel_id=1, source_target_pairs={{0,8},{4,12},{8,0},{12,4},{16,24},{20,28},{24,16},{28,20},{1,9},{5... | collective-permute-start | bytes 393224 | tf_op jit(solution)/shard_map/ppermute | solution.py:551
  38.8 8.3 %near_own.1.refs_9_.refs_13_ = f32[8,256,512]{2,1,0:T(8,128)S(1)} custom-call(s32[4]{0:T(128)S(1)} %copy-done.6, f32[88,1024]{1,0:T(8,128)S(1)} %copy-done.2, f32[88,1024]{1,0:T(8,128)S(1)} %collective-permute-done.refs_1_, f32[88,1024]{1,0:T(8,128)S(1)} %collective-permute-done.1.refs_2_, f32[88,1024]{1,0:T(8,128)S(1)} %collective-permute-done.2.refs_3_, ...), custom_call_target="tpu_custom_call" | custom-call | tf_op jit(solution)/shard_map/near_own/pallas_call | solution.py:206
  47.7 3.2 %near_pair.1.refs_10_.refs_11_ = f32[4,256,512]{2,1,0:T(8,128)S(1)} custom-call(s32[4]{0:T(128)S(1)} %copy-done.6, f32[88,1024]{1,0:T(8,128)S(1)} %copy-done.2, f32[88,1024]{1,0:T(8,128)S(1)} %collective-permute-done.refs_1_, f32[88,1024]{1,0:T(8,128)S(1)} %collective-permute-done.1.refs_2_, f32[88,1024]{1,0:T(8,128)S(1)} %collective-permute-done.2.refs_3_, ...), custom_call_target="tpu_custom_call" | custom-call | tf_op jit(solution)/shard_map/near_pair/pallas_call | solution.py:206
  50.9 2.8 %near_next_away.2 = (f32[128,1024]{1,0:T(8,128)S(1)}, f32[128,1024]{1,0:T(8,128)S(1)}) custom-call(s32[4]{0:T(128)S(1)} %copy-done.6, f32[88,1024]{1,0:T(8,128)S(1)} %copy-done.2, f32[88,1024]{1,0:T(8,128)S(1)} %collective-permute-done.refs_1_, f32[88,1024]{1,0:T(8,128)S(1)} %collective-permute-done.1.refs_2_, ...), custom_call_target="tpu_custom_call" | custom-call | tf_op jit(solution)/shard_map/near_next_away/pallas_call | solution.py:206
  53.7 8.5 %collective-permute-start.17 = (f32[128,1024]{1,0:T(8,128)S(1)}, f32[128,1024]{1,0:T(8,128)S(1)}, u32[]{:S(2)}, u32[]{:S(2)}) collective-permute-start(f32[128,1024]{1,0:T(8,128)S(1)} %get-tuple-element.46), channel_id=1, source_target_pairs={{1,0},{0,1},{3,2},{2,3},{5,4},{4,5},{7,6},{6,7},{9,8},{8,9},{11,10... | collective-permute-start | bytes 1572872 | tf_op jit(solution)/shard_map/ppermute | solution.py:522
  62.3 3.0 %near_next_away.3 = (f32[128,1024]{1,0:T(8,128)S(1)}, f32[128,1024]{1,0:T(8,128)S(1)}) custom-call(s32[4]{0:T(128)S(1)} %copy-done.6, f32[88,1024]{1,0:T(8,128)S(1)} %copy-done.2, f32[88,1024]{1,0:T(8,128)S(1)} %collective-permute-done.refs_1_, f32[88,1024]{1,0:T(8,128)S(1)} %collective-permute-done.1.refs_2_, ...), custom_call_target="tpu_custom_call" | custom-call | tf_op jit(solution)/shard_map/near_next_away/pallas_call | solution.py:206
  65.4 1.7 %collective-permute-start.12 = (f32[128,1024]{1,0:T(8,128)S(1)}, f32[128,1024]{1,0:T(8,128)S(1)}, u32[]{:S(2)}, u32[]{:S(2)}) collective-permute-start(f32[128,1024]{1,0:T(8,128)S(1)} %get-tuple-element.51), channel_id=1, source_target_pairs={{1,0},{0,1},{3,2},{2,3},{5,4},{4,5},{7,6},{6,7},{9,8},{8,9},{11,10... | collective-permute-start | bytes 1572872 | tf_op jit(solution)/shard_map/ppermute | solution.py:522
  68.6 12.0 %collective-permute-done.13.beside_ref = f32[4,128,256]{2,1,0:T(8,128)S(1)} collective-permute-done((f32[4,128,256]{2,1,0:T(8,128)S(1)}, f32[4,128,256]{2,1,0:T(8,128)S(1)}, u32[]{:S(2)}, u32[]{:S(2)}) %collective-permute-start.13) | collective-permute-done | bytes 524320 | tf_op jit(solution)/shard_map/ppermute | solution.py:565
  80.8 6.5 %far.1.refs_14_.refs_0_ = f32[64,256]{1,0:T(8,128)S(1)} custom-call(s32[4]{0:T(128)S(1)} %copy-done.7, s32[4,14]{1,0:T(4,128)S(1)} %bitcast.4, s32[6,256]{1,0:T(8,128)S(1)} %copy-done.8, f32[6,512,256]{2,1,0:T(8,128)S(1)} %copy-done.4, f32[4,128,256]{2,1,0:T(8,128)S(1)} %stack.17.refs_11_.alike_ref, f32[4,128,256]{2,1,0:T(8,128)S(1)} %collective-permute-done.13.beside_ref, ...), custom_call_target="tpu_custom_call" | custom-call | tf_op jit(solution)/shard_map/far/pallas_call | solution.py:435
  87.3 9.8 %near_home.1 = (f32[128,1024]{1,0:T(8,128)S(1)}, f32[128,1024]{1,0:T(8,128)S(1)}, f32[128,1024]{1,0:T(8,128)S(1)}, f32[128,1024]{1,0:T(8,128)S(1)}) custom-call(s32[4]{0:T(128)S(1)} %copy-done.7, f32[88,1024]{1,0:T(8,128)S(1)} %copy-done.2, f32[88,1024]{1,0:T(8,128)S(1)} %collective-permute-done.refs_1_, f32[88,1024]{1,0:T(8,128)S(1)} %collective-permute-done.1.refs_2_, ...), custom_call_target="tpu_custom_call" | custom-call | tf_op jit(solution)/shard_map/near_home/pallas_call | solution.py:206
  97.7 3.2 %collective-permute-start.15 = (f32[64,256]{1,0:T(8,128)S(1)}, f32[64,256]{1,0:T(8,128)S(1)}, u32[]{:S(2)}, u32[]{:S(2)}) collective-permute-start(f32[64,256]{1,0:T(8,128)S(1)} %far.1.refs_14_.refs_0_), channel_id=1, source_target_pairs={{2,0},{3,1},{0,2},{1,3},{6,4},{7,5},{4,6},{5,7},{10,8},{11,9},{8,1... | collective-permute-start | bytes 196616 | tf_op jit(solution)/shard_map/ppermute | solution.py:522
  101.1 2.2 %collective-permute-done.15.refs_2_ = f32[64,256]{1,0:T(8,128)S(1)} collective-permute-done((f32[64,256]{1,0:T(8,128)S(1)}, f32[64,256]{1,0:T(8,128)S(1)}, u32[]{:S(2)}, u32[]{:S(2)}) %collective-permute-start.15) | collective-permute-done | bytes 65568 | tf_op jit(solution)/shard_map/ppermute | solution.py:522
  103.4 1.7 %collective-permute-done.16.refs_3_ = f32[64,256]{1,0:T(8,128)S(1)} collective-permute-done((f32[64,256]{1,0:T(8,128)S(1)}, f32[64,256]{1,0:T(8,128)S(1)}, u32[]{:S(2)}, u32[]{:S(2)}) %collective-permute-start.16) | collective-permute-done | bytes 65568 | tf_op jit(solution)/shard_map/ppermute | solution.py:522
  105.0 2.2 %join.1 = f32[256,1024]{1,0:T(8,128)} custom-call(s32[4]{0:T(128)S(1)} %copy-done.7, f32[2,512,256]{2,1,0:T(8,128)S(1)} %copy-done.3, f32[64,256]{1,0:T(8,128)S(1)} %far.1.refs_14_.refs_0_, f32[64,256]{1,0:T(8,128)S(1)} %collective-permute-done.14.refs_1_, f32[64,256]{1,0:T(8,128)S(1)} %collective-permute-done.15.refs_2_, ...), custom_call_target="tpu_custom_call" | custom-call | tf_op jit(solution)/shard_map/join/pallas_call | solution.py:491
  (58 shorter events, 10.8 us)
Async XLA Ops:
  0.0 11.5 %collective-permute-start.6 = (f32[64,1024]{1,0:T(8,128)}, f32[64,1024]{1,0:T(8,128)}, u32[]{:S(2)}, u32[]{:S(2)}) collective-permute-start(f32[64,1024]{1,0:T(8,128)} %refs_6_.1), channel_id=1, source_target_pairs={{0,4},{4,0},{8,12},{12,8},{16,20},{20,16},{24,28},{28,24},{1,5},{5... | collective-permute-start | bytes 786440 | tf_op jit(solution)/shard_map/ppermute | solution.py:536
  2.5 19.1 %collective-permute-start.8 = (f32[128,1024]{1,0:T(8,128)}, f32[128,1024]{1,0:T(8,128)}, u32[]{:S(2)}, u32[]{:S(2)}) collective-permute-start(f32[128,1024]{1,0:T(8,128)} %get-tuple-element.62), channel_id=1, source_target_pairs={{0,4},{4,0},{8,12},{12,8},{16,20},{20,16},{24,28},{28,24},{1,5},{5... | collective-permute-start | bytes 1572872 | tf_op jit(solution)/shard_map/ppermute | solution.py:537
  8.5 15.2 %collective-permute-start = (f32[88,1024]{1,0:T(8,128)}, f32[88,1024]{1,0:T(8,128)S(1)}, u32[]{:S(2)}, u32[]{:S(2)}) collective-permute-start(f32[88,1024]{1,0:T(8,128)} %get-tuple-element.34), channel_id=1, source_target_pairs={{1,0},{0,1},{3,2},{2,3},{5,4},{4,5},{7,6},{6,7},{9,8},{8,9},{11,10... | collective-permute-start | bytes 1081352 | tf_op jit(solution)/shard_map/ppermute | solution.py:540
  9.8 13.9 %collective-permute-start.1 = (f32[88,1024]{1,0:T(8,128)}, f32[88,1024]{1,0:T(8,128)S(1)}, u32[]{:S(2)}, u32[]{:S(2)}) collective-permute-start(f32[88,1024]{1,0:T(8,128)} %get-tuple-element.35), channel_id=1, source_target_pairs={{2,0},{3,1},{0,2},{1,3},{6,4},{7,5},{4,6},{5,7},{10,8},{11,9},{8,1... | collective-permute-start | bytes 1081352 | tf_op jit(solution)/shard_map/ppermute | solution.py:540
  11.0 17.2 %collective-permute-start.2 = (f32[88,1024]{1,0:T(8,128)}, f32[88,1024]{1,0:T(8,128)S(1)}, u32[]{:S(2)}, u32[]{:S(2)}) collective-permute-start(f32[88,1024]{1,0:T(8,128)} %get-tuple-element.36), channel_id=1, source_target_pairs={{3,0},{2,1},{1,2},{0,3},{7,4},{6,5},{5,6},{4,7},{11,8},{10,9},{9,1... | collective-permute-start | bytes 1081352 | tf_op jit(solution)/shard_map/ppermute | solution.py:540
  11.5 9.8 %collective-permute-start.7 = (f32[64,1024]{1,0:T(8,128)}, f32[64,1024]{1,0:T(8,128)S(1)}, u32[]{:S(2)}, u32[]{:S(2)}) collective-permute-start(f32[64,1024]{1,0:T(8,128)} %collective-permute-done.6.refs_6_), channel_id=1, source_target_pairs={{0,8},{8,16},{16,24},{12,4},{20,12},{28,20},{1,9},{9,17},{17,25},{... | collective-permute-start | bytes 786440 | tf_op jit(solution)/shard_map/ppermute | solution.py:544
  21.4 12.7 %collective-permute-start.10 = (f32[128,1024]{1,0:T(8,128)}, f32[128,1024]{1,0:T(8,128)S(1)}, u32[]{:S(2)}, u32[]{:S(2)}) collective-permute-start(f32[128,1024]{1,0:T(8,128)} %get-tuple-element.61), channel_id=1, source_target_pairs={{0,4},{4,0},{8,12},{12,8},{16,20},{20,16},{24,28},{28,24},{1,5},{5... | collective-permute-start | bytes 1572872 | tf_op jit(solution)/shard_map/ppermute | solution.py:537
  21.6 29.3 %collective-permute-start.9 = (f32[128,1024]{1,0:T(8,128)}, f32[128,1024]{1,0:T(8,128)S(1)}, u32[]{:S(2)}, u32[]{:S(2)}) collective-permute-start(f32[128,1024]{1,0:T(8,128)} %collective-permute-done.8.refs_7_), channel_id=1, source_target_pairs={{0,8},{8,16},{16,24},{12,4},{20,12},{28,20},{1,9},{9,17},{17,25},{... | collective-permute-start | bytes 1572872 | tf_op jit(solution)/shard_map/ppermute | solution.py:546
  34.0 28.3 %collective-permute-start.11 = (f32[128,1024]{1,0:T(8,128)S(1)}, f32[128,1024]{1,0:T(8,128)S(1)}, u32[]{:S(2)}, u32[]{:S(2)}) collective-permute-start(f32[128,1024]{1,0:T(8,128)S(1)} %collective-permute-done.10.refs_8_), channel_id=1, source_target_pairs={{0,8},{8,16},{16,24},{12,4},{20,12},{28,20},{1,9},{9,17},{17,25},{... | collective-permute-start | bytes 1572872 | tf_op jit(solution)/shard_map/ppermute | solution.py:556
  36.1 26.1 %collective-permute-start.3 = (f32[128,256]{1,0:T(8,128)S(1)}, f32[128,256]{1,0:T(8,128)S(1)}, u32[]{:S(2)}, u32[]{:S(2)}) collective-permute-start(f32[128,256]{1,0:T(8,128)S(1)} %get-tuple-element.47.refs_0_), channel_id=1, source_target_pairs={{0,8},{4,12},{8,0},{12,4},{16,24},{20,28},{24,16},{28,20},{1,9},{5... | collective-permute-start | bytes 393224 | tf_op jit(solution)/shard_map/ppermute | solution.py:551
  37.5 24.7 %collective-permute-start.4 = (f32[128,256]{1,0:T(8,128)S(1)}, f32[128,256]{1,0:T(8,128)S(1)}, u32[]{:S(2)}, u32[]{:S(2)}) collective-permute-start(f32[128,256]{1,0:T(8,128)S(1)} %get-tuple-element.47.refs_0_), channel_id=1, source_target_pairs={{0,16},{4,20},{8,24},{12,28},{16,0},{20,4},{24,8},{28,12},{1,17},{... | collective-permute-start | bytes 393224 | tf_op jit(solution)/shard_map/ppermute | solution.py:551
  37.5 24.7 %collective-permute-start.5 = (f32[128,256]{1,0:T(8,128)S(1)}, f32[128,256]{1,0:T(8,128)S(1)}, u32[]{:S(2)}, u32[]{:S(2)}) collective-permute-start(f32[128,256]{1,0:T(8,128)S(1)} %get-tuple-element.47.refs_0_), channel_id=1, source_target_pairs={{0,24},{4,28},{8,16},{12,20},{16,8},{20,12},{24,0},{28,4},{1,25},{... | collective-permute-start | bytes 393224 | tf_op jit(solution)/shard_map/ppermute | solution.py:551
  53.7 13.4 %collective-permute-start.17 = (f32[128,1024]{1,0:T(8,128)S(1)}, f32[128,1024]{1,0:T(8,128)S(1)}, u32[]{:S(2)}, u32[]{:S(2)}) collective-permute-start(f32[128,1024]{1,0:T(8,128)S(1)} %get-tuple-element.46), channel_id=1, source_target_pairs={{1,0},{0,1},{3,2},{2,3},{5,4},{4,5},{7,6},{6,7},{9,8},{8,9},{11,10... | collective-permute-start | bytes 1572872 | tf_op jit(solution)/shard_map/ppermute | solution.py:522
  62.3 18.5 %copy-start.8 = (s32[6,256]{1,0:T(8,128)S(1)}, s32[6,256]{1,0:T(8,128)}, u32[]{:S(2)}) copy-start(s32[6,256]{1,0:T(8,128)} %node_ref.1) | copy-start | bytes 18436
  65.4 3.3 %collective-permute-start.12 = (f32[128,1024]{1,0:T(8,128)S(1)}, f32[128,1024]{1,0:T(8,128)S(1)}, u32[]{:S(2)}, u32[]{:S(2)}) collective-permute-start(f32[128,1024]{1,0:T(8,128)S(1)} %get-tuple-element.51), channel_id=1, source_target_pairs={{1,0},{0,1},{3,2},{2,3},{5,4},{4,5},{7,6},{6,7},{9,8},{8,9},{11,10... | collective-permute-start | bytes 1572872 | tf_op jit(solution)/shard_map/ppermute | solution.py:522
  67.1 13.5 %collective-permute-start.13 = (f32[4,128,256]{2,1,0:T(8,128)S(1)}, f32[4,128,256]{2,1,0:T(8,128)S(1)}, u32[]{:S(2)}, u32[]{:S(2)}) collective-permute-start(f32[4,128,256]{2,1,0:T(8,128)S(1)} %stack.17.refs_11_.alike_ref), channel_id=1, source_target_pairs={{0,4},{4,0},{8,12},{12,8},{16,20},{20,16},{24,28},{28,24},{1,5},{5... | collective-permute-start | bytes 1572872 | tf_op jit(solution)/shard_map/ppermute | solution.py:565
  67.2 30.6 %collective-permute-start.18 = (f32[128,1024]{1,0:T(8,128)S(1)}, f32[128,1024]{1,0:T(8,128)S(1)}, u32[]{:S(2)}, u32[]{:S(2)}) collective-permute-start(f32[128,1024]{1,0:T(8,128)S(1)} %add_parts.4), channel_id=1, source_target_pairs={{2,0},{3,1},{0,2},{1,3},{6,4},{7,5},{4,6},{5,7},{10,8},{11,9},{8,1... | collective-permute-start | bytes 1572872 | tf_op jit(solution)/shard_map/ppermute | solution.py:525
  80.7 20.3 %collective-permute-start.19 = (f32[128,1024]{1,0:T(8,128)S(1)}, f32[128,1024]{1,0:T(8,128)S(1)}, u32[]{:S(2)}, u32[]{:S(2)}) collective-permute-start(f32[128,1024]{1,0:T(8,128)S(1)} %add_parts.3.refs_0_), channel_id=1, source_target_pairs={{2,0},{3,1},{0,2},{1,3},{6,4},{7,5},{4,6},{5,7},{10,8},{11,9},{8,1... | collective-permute-start | bytes 1572872 | tf_op jit(solution)/shard_map/ppermute | solution.py:525
  87.3 17.7 %copy-start.3 = (f32[2,512,256]{2,1,0:T(8,128)S(1)}, f32[2,512,256]{2,1,0:T(8,128)}, u32[]{:S(2)}) copy-start(f32[2,512,256]{2,1,0:T(8,128)} %interp_ref.1) | copy-start | bytes 3145732
  97.1 8.0 %collective-permute-start.20 = (f32[128,1024]{1,0:T(8,128)S(1)}, f32[128,1024]{1,0:T(8,128)S(1)}, u32[]{:S(2)}, u32[]{:S(2)}) collective-permute-start(f32[128,1024]{1,0:T(8,128)S(1)} %get-tuple-element.59), channel_id=1, source_target_pairs={{1,0},{0,1},{3,2},{2,3},{5,4},{4,5},{7,6},{6,7},{9,8},{8,9},{11,10... | collective-permute-start | bytes 1572872 | tf_op jit(solution)/shard_map/ppermute | solution.py:522
  97.2 7.9 %collective-permute-start.21 = (f32[128,1024]{1,0:T(8,128)S(1)}, f32[128,1024]{1,0:T(8,128)S(1)}, u32[]{:S(2)}, u32[]{:S(2)}) collective-permute-start(f32[128,1024]{1,0:T(8,128)S(1)} %get-tuple-element.60), channel_id=1, source_target_pairs={{1,0},{0,1},{3,2},{2,3},{5,4},{4,5},{7,6},{6,7},{9,8},{8,9},{11,10... | collective-permute-start | bytes 1572872 | tf_op jit(solution)/shard_map/ppermute | solution.py:522
  97.7 3.5 %collective-permute-start.14 = (f32[64,256]{1,0:T(8,128)S(1)}, f32[64,256]{1,0:T(8,128)S(1)}, u32[]{:S(2)}, u32[]{:S(2)}) collective-permute-start(f32[64,256]{1,0:T(8,128)S(1)} %far.1.refs_14_.refs_0_), channel_id=1, source_target_pairs={{1,0},{0,1},{3,2},{2,3},{5,4},{4,5},{7,6},{6,7},{9,8},{8,9},{11,10... | collective-permute-start | bytes 196616 | tf_op jit(solution)/shard_map/ppermute | solution.py:522
  97.7 5.6 %collective-permute-start.15 = (f32[64,256]{1,0:T(8,128)S(1)}, f32[64,256]{1,0:T(8,128)S(1)}, u32[]{:S(2)}, u32[]{:S(2)}) collective-permute-start(f32[64,256]{1,0:T(8,128)S(1)} %far.1.refs_14_.refs_0_), channel_id=1, source_target_pairs={{2,0},{3,1},{0,2},{1,3},{6,4},{7,5},{4,6},{5,7},{10,8},{11,9},{8,1... | collective-permute-start | bytes 196616 | tf_op jit(solution)/shard_map/ppermute | solution.py:522
  101.0 4.0 %collective-permute-start.16 = (f32[64,256]{1,0:T(8,128)S(1)}, f32[64,256]{1,0:T(8,128)S(1)}, u32[]{:S(2)}, u32[]{:S(2)}) collective-permute-start(f32[64,256]{1,0:T(8,128)S(1)} %far.1.refs_14_.refs_0_), channel_id=1, source_target_pairs={{3,0},{2,1},{1,2},{0,3},{7,4},{6,5},{5,6},{4,7},{11,8},{10,9},{9,1... | collective-permute-start | bytes 196616 | tf_op jit(solution)/shard_map/ppermute | solution.py:522
  (9 other events, 73.5 us)
where the time goes:
time: 107 us
  Pallas kernels  42 us (39%)
  waiting for transfers between devices  31.1 us (29%)
  starting transfers between devices  28.6 us (27%)
  local copies, waits for them, and re-layouts  4.67 us (4%)
    pallas_call x5, Pallas kernels, near_call(): pl.pallas_call(partial(near_body, len(msgs) // 2, sets, leaves_at, rows,...  27.1 us
    ppermute x7, starting transfers between devices, from_help(): return lax.ppermute(value, 'help', help_pairs(xs, dx, dc))  14.1 us
    ppermute x1, waiting for transfers between devices, shards(): side = lax.ppermute(alike, 'leaf', beside)  12 us
    ppermute x1, waiting for transfers between devices, shards(): pts_z = lax.ppermute(pts_y, 'leaf', across)  7.77 us
    pallas_call x1, Pallas kernels, far_call(): pl.pallas_call(partial(far_body, groups, rows), name='far', out_shape=jax...  6.51 us
    ppermute x7, waiting for transfers between devices, from_help(): return lax.ppermute(value, 'help', help_pairs(xs, dx, dc))  4.62 us
    ppermute x3, waiting for transfers between devices, shards(): lax.ppermute(sent[n], 'help', help_pairs(xs, -dx, dc))  4.51 us
    pallas_call x1, Pallas kernels, leaf_call(): pl.pallas_call(partial(leaf_body, xs), name='leaf_up', out_shape=[jax.Sha...  4.07 us
  transfers between devices with their start and end apart: 22, of which 7 were waited for; matrix products, arithmetic and copies ran while one was open for 3% of the time, Pallas kernels for 37%

commit v1 on v0

--- a/solution.py
+++ b/solution.py
@@ -573,14 +573,12 @@
     parts = []
     for c in range(2):
         kept, mates = sums[c]
-        if c == 1:
-            mates, side = together(mates, side)
         both = add_call(*zip(kept, mates))
         parts.append([to_help(value, dx + 1) for dx, value in enumerate(both)])
-    v_own = far_call(groups, pos, far_nodes, skel_node, transfer, alike, side, both[:1])
+    sources = [pair_src, ("next", z_side, w_z)]
+    home = near_call("near_home", pos, msgs, targets, home, sources, R, 0, [own], both[:1])
+    v_own = far_call(groups, pos, far_nodes, skel_node, transfer, alike, side, home[:1])
     values = [v_own] + [from_help(v_own, dx, dc) for dx, dc in order[1:]]
-    sources = [pair_src, ("next", z_side, w_z)]
-    home = near_call("near_home", pos, msgs, targets, home, sources, R, 0, [own], [v_own])
     mate = [from_help(value, 0, 1) for value in home[2:]]
     mine = add_call(*[[home[c], *parts[c]] for c in range(2)])
     return final_call(xs, pos, interp, mine, mate, values)

time: 107 us -> 100 us (0.935)
  the two profiles are of different devices: /device:TPU:21 before, /device:TPU:0 now
where the time goes in v1:
time: 100 us; the launch traced here: 99.2 us
  Pallas kernels  36.9 us (37%)
  starting transfers between devices  31.9 us (32%)
  waiting for transfers between devices  24.7 us (25%)
  local copies, waits for them, and re-layouts  4.67 us (5%)
    pallas_call x5, Pallas kernels, near_call(): pl.pallas_call(partial(near_body, len(msgs) // 2, sets, leaves_at, rows,...  22.1 us
    pallas_call x1, Pallas kernels, far_call(): pl.pallas_call(partial(far_body, groups, rows), name='far', out_shape=jax...  6.51 us
    ppermute x1, waiting for transfers between devices, shards(): pts_z = lax.ppermute(pts_y, 'leaf', across)  6.36 us
    ppermute x2, waiting for transfers between devices, to_help(): return lax.ppermute(value, 'help', help_pairs(xs, -dx, 0))  5.35 us
    ppermute x3, starting transfers between devices, shards(): lax.ppermute(payload, 'leaf', [(i, i ^ mask) for i in range(groups)])  4.45 us
    ppermute x7, waiting for transfers between devices, from_help(): return lax.ppermute(value, 'help', help_pairs(xs, dx, dc))  4.23 us
    ppermute x1, waiting for transfers between devices, shards(): side = lax.ppermute(alike, 'leaf', beside)  4.14 us
    pallas_call x1, Pallas kernels, leaf_call(): pl.pallas_call(partial(leaf_body, xs), name='leaf_up', out_shape=[jax.Sha...  4.07 us
  transfers between devices with their start and end apart: 22, of which 7 were waited for; matrix products, arithmetic and copies ran while one was open for 3% of the time, Pallas kernels for 35%

profile of v1, /device:TPU:0, one launch (start us, length us, event | category | flops | bytes accessed | tf_op | source)
XLA Modules:
  0.0 99.2 jit_solution(3245745141783003486)
XLA Ops:
  0.0 3.0 %collective-permute-start.6 = (f32[64,1024]{1,0:T(8,128)}, f32[64,1024]{1,0:T(8,128)}, u32[]{:S(2)}, u32[]{:S(2)}) collective-permute-start(f32[64,1024]{1,0:T(8,128)} %refs_6_.1), channel_id=1, source_target_pairs={{0,4},{4,0},{8,12},{12,8},{16,20},{20,16},{24,28},{28,24},{1,5},{5... | collective-permute-start | bytes 786440 | tf_op jit(solution)/shard_map/ppermute | solution.py:536
  3.0 2.3 %fusion = (f32[128,1024]{1,0:T(8,128)}, f32[128,1024]{1,0:T(8,128)}) fusion(f32[256,1024]{1,0:T(8,128)} %refs_7_.1), kind=kLoop, calls=%fused_computation.1 | loop fusion | bytes 2097152 | tf_op jit(solution)/shard_map/slice | solution.py:537
  5.9 4.1 %leaf_up.1 = (f32[88,1024]{1,0:T(8,128)}, f32[88,1024]{1,0:T(8,128)}, f32[88,1024]{1,0:T(8,128)}, f32[88,1024]{1,0:T(8,128)}) custom-call(s32[4]{0:T(128)} %pad_add_fusion.pos_ref, s32[1,2]{1,0:T(1,128)} %count_ref.1, s32[2,32]{1,0:T(2,128)} %src_ref.1, f32[64,1024]{1,0:T(8,128)} %refs_6_.1, f32[256,1024]{1,0:T(8,128)} %refs_7_.1, f32[2,512,256]{2,1,0:T(8,128)} %interp_ref.1), custom_call_target="tpu_custom_call" | custom-call | tf_op jit(solution)/shard_map/leaf_up/pallas_call | solution.py:292
  10.1 2.1 %collective-permute-start.1 = (f32[88,1024]{1,0:T(8,128)}, f32[88,1024]{1,0:T(8,128)S(1)}, u32[]{:S(2)}, u32[]{:S(2)}) collective-permute-start(f32[88,1024]{1,0:T(8,128)} %get-tuple-element.33), channel_id=1, source_target_pairs={{2,0},{3,1},{0,2},{1,3},{6,4},{7,5},{4,6},{5,7},{10,8},{11,9},{8,1... | collective-permute-start | bytes 1081352 | tf_op jit(solution)/shard_map/ppermute | solution.py:540
  12.2 3.7 %collective-permute-start.7 = (f32[64,1024]{1,0:T(8,128)}, f32[64,1024]{1,0:T(8,128)S(1)}, u32[]{:S(2)}, u32[]{:S(2)}) collective-permute-start(f32[64,1024]{1,0:T(8,128)} %collective-permute-done.6.refs_6_), channel_id=1, source_target_pairs={{0,8},{8,16},{16,24},{12,4},{20,12},{28,20},{1,9},{9,17},{17,25},{... | collective-permute-start | bytes 786440 | tf_op jit(solution)/shard_map/ppermute | solution.py:544
  15.9 6.4 %collective-permute-done.7.pts_ref = f32[64,1024]{1,0:T(8,128)S(1)} collective-permute-done((f32[64,1024]{1,0:T(8,128)}, f32[64,1024]{1,0:T(8,128)S(1)}, u32[]{:S(2)}, u32[]{:S(2)}) %collective-permute-start.7) | collective-permute-done | bytes 262176 | tf_op jit(solution)/shard_map/ppermute | solution.py:544
  22.3 2.3 %collective-permute-start.10 = (f32[128,1024]{1,0:T(8,128)}, f32[128,1024]{1,0:T(8,128)S(1)}, u32[]{:S(2)}, u32[]{:S(2)}) collective-permute-start(f32[128,1024]{1,0:T(8,128)} %get-tuple-element.57), channel_id=1, source_target_pairs={{0,4},{4,0},{8,12},{12,8},{16,20},{20,16},{24,28},{28,24},{1,5},{5... | collective-permute-start | bytes 1572872 | tf_op jit(solution)/shard_map/ppermute | solution.py:537
  24.6 3.5 %collective-permute-start.9 = (f32[128,1024]{1,0:T(8,128)}, f32[128,1024]{1,0:T(8,128)S(1)}, u32[]{:S(2)}, u32[]{:S(2)}) collective-permute-start(f32[128,1024]{1,0:T(8,128)} %collective-permute-done.8.refs_7_), channel_id=1, source_target_pairs={{0,8},{8,16},{16,24},{12,4},{20,12},{28,20},{1,9},{9,17},{17,25},{... | collective-permute-start | bytes 1572872 | tf_op jit(solution)/shard_map/ppermute | solution.py:546
  32.5 4.0 %collective-permute-done.10.refs_8_ = f32[128,1024]{1,0:T(8,128)S(1)} collective-permute-done((f32[128,1024]{1,0:T(8,128)}, f32[128,1024]{1,0:T(8,128)S(1)}, u32[]{:S(2)}, u32[]{:S(2)}) %collective-permute-start.10) | collective-permute-done | bytes 524320 | tf_op jit(solution)/shard_map/ppermute | solution.py:537
  36.5 3.7 %collective-permute-start.12 = (f32[128,1024]{1,0:T(8,128)S(1)}, f32[128,1024]{1,0:T(8,128)S(1)}, u32[]{:S(2)}, u32[]{:S(2)}) collective-permute-start(f32[128,1024]{1,0:T(8,128)S(1)} %collective-permute-done.10.refs_8_), channel_id=1, source_target_pairs={{0,8},{8,16},{16,24},{12,4},{20,12},{28,20},{1,9},{9,17},{17,25},{... | collective-permute-start | bytes 1572872 | tf_op jit(solution)/shard_map/ppermute | solution.py:556
  40.2 1.6 %collective-permute-start.3 = (f32[128,256]{1,0:T(8,128)S(1)}, f32[128,256]{1,0:T(8,128)S(1)}, u32[]{:S(2)}, u32[]{:S(2)}) collective-permute-start(f32[128,256]{1,0:T(8,128)S(1)} %get-tuple-element.45.refs_0_), channel_id=1, source_target_pairs={{0,8},{4,12},{8,0},{12,4},{16,24},{20,28},{24,16},{28,20},{1,9},{5... | collective-permute-start | bytes 393224 | tf_op jit(solution)/shard_map/ppermute | solution.py:551
  42.9 1.7 %collective-permute-start.5 = (f32[128,256]{1,0:T(8,128)S(1)}, f32[128,256]{1,0:T(8,128)S(1)}, u32[]{:S(2)}, u32[]{:S(2)}) collective-permute-start(f32[128,256]{1,0:T(8,128)S(1)} %get-tuple-element.45.refs_0_), channel_id=1, source_target_pairs={{0,24},{4,28},{8,16},{12,20},{16,8},{20,12},{24,0},{28,4},{1,25},{... | collective-permute-start | bytes 393224 | tf_op jit(solution)/shard_map/ppermute | solution.py:551
  44.6 10.6 %near_own.1.refs_9_.refs_13_ = f32[8,256,512]{2,1,0:T(8,128)S(1)} custom-call(s32[4]{0:T(128)S(1)} %copy-done.6, f32[88,1024]{1,0:T(8,128)S(1)} %copy-done.2, f32[88,1024]{1,0:T(8,128)S(1)} %collective-permute-done.refs_1_, f32[88,1024]{1,0:T(8,128)S(1)} %collective-permute-done.1.refs_2_, f32[88,1024]{1,0:T(8,128)S(1)} %collective-permute-done.2.refs_3_, ...), custom_call_target="tpu_custom_call" | custom-call | tf_op jit(solution)/shard_map/near_own/pallas_call | solution.py:206
  55.7 3.2 %near_pair.1.refs_10_.refs_11_ = f32[4,256,512]{2,1,0:T(8,128)S(1)} custom-call(s32[4]{0:T(128)S(1)} %copy-done.6, f32[88,1024]{1,0:T(8,128)S(1)} %copy-done.2, f32[88,1024]{1,0:T(8,128)S(1)} %collective-permute-done.refs_1_, f32[88,1024]{1,0:T(8,128)S(1)} %collective-permute-done.1.refs_2_, f32[88,1024]{1,0:T(8,128)S(1)} %collective-permute-done.2.refs_3_, ...), custom_call_target="tpu_custom_call" | custom-call | tf_op jit(solution)/shard_map/near_pair/pallas_call | solution.py:206
  61.7 1.5 %near_next_away.3 = (f32[128,1024]{1,0:T(8,128)S(1)}, f32[128,1024]{1,0:T(8,128)S(1)}) custom-call(s32[4]{0:T(128)S(1)} %copy-done.6, f32[88,1024]{1,0:T(8,128)S(1)} %copy-done.2, f32[88,1024]{1,0:T(8,128)S(1)} %collective-permute-done.refs_1_, f32[88,1024]{1,0:T(8,128)S(1)} %collective-permute-done.1.refs_2_, ...), custom_call_target="tpu_custom_call" | custom-call | tf_op jit(solution)/shard_map/near_next_away/pallas_call | solution.py:206
  63.4 3.2 %collective-permute-start.11 = (f32[4,128,256]{2,1,0:T(8,128)S(1)}, f32[4,128,256]{2,1,0:T(8,128)S(1)}, u32[]{:S(2)}, u32[]{:S(2)}) collective-permute-start(f32[4,128,256]{2,1,0:T(8,128)S(1)} %stack.17.refs_11_.alike_ref), channel_id=1, source_target_pairs={{0,4},{4,0},{8,12},{12,8},{16,20},{20,16},{24,28},{28,24},{1,5},{5... | collective-permute-start | bytes 1572872 | tf_op jit(solution)/shard_map/ppermute | solution.py:565
  66.7 1.6 %collective-permute-start.18 = (f32[128,1024]{1,0:T(8,128)S(1)}, f32[128,1024]{1,0:T(8,128)S(1)}, u32[]{:S(2)}, u32[]{:S(2)}) collective-permute-start(f32[128,1024]{1,0:T(8,128)S(1)} %add_parts.4), channel_id=1, source_target_pairs={{2,0},{3,1},{0,2},{1,3},{6,4},{7,5},{4,6},{5,7},{10,8},{11,9},{8,1... | collective-permute-start | bytes 1572872 | tf_op jit(solution)/shard_map/ppermute | solution.py:525
  68.9 5.5 %near_home.1 = (f32[128,1024]{1,0:T(8,128)S(1)}, f32[128,1024]{1,0:T(8,128)S(1)}, f32[128,1024]{1,0:T(8,128)S(1)}, f32[128,1024]{1,0:T(8,128)S(1)}) custom-call(s32[4]{0:T(128)S(1)} %copy-done.7, f32[88,1024]{1,0:T(8,128)S(1)} %copy-done.2, f32[88,1024]{1,0:T(8,128)S(1)} %collective-permute-done.refs_1_, f32[88,1024]{1,0:T(8,128)S(1)} %collective-permute-done.1.refs_2_, ...), custom_call_target="tpu_custom_call" | custom-call | tf_op jit(solution)/shard_map/near_home/pallas_call | solution.py:206
  75.0 4.1 %collective-permute-done.11.beside_ref = f32[4,128,256]{2,1,0:T(8,128)S(1)} collective-permute-done((f32[4,128,256]{2,1,0:T(8,128)S(1)}, f32[4,128,256]{2,1,0:T(8,128)S(1)}, u32[]{:S(2)}, u32[]{:S(2)}) %collective-permute-start.11) | collective-permute-done | bytes 524320 | tf_op jit(solution)/shard_map/ppermute | solution.py:565
  79.1 6.5 %far.1.refs_0_ = f32[64,256]{1,0:T(8,128)S(1)} custom-call(s32[4]{0:T(128)S(1)} %copy-done.7, s32[4,14]{1,0:T(4,128)S(1)} %bitcast.4, s32[6,256]{1,0:T(8,128)S(1)} %copy-done.8, f32[6,512,256]{2,1,0:T(8,128)S(1)} %copy-done.4, f32[4,128,256]{2,1,0:T(8,128)S(1)} %stack.17.refs_11_.alike_ref, f32[4,128,256]{2,1,0:T(8,128)S(1)} %collective-permute-done.11.beside_ref, ...), custom_call_target="tpu_custom_call" | custom-call | tf_op jit(solution)/shard_map/far/pallas_call | solution.py:435
  85.8 1.6 %collective-permute-start.15 = (f32[64,256]{1,0:T(8,128)S(1)}, f32[64,256]{1,0:T(8,128)S(1)}, u32[]{:S(2)}, u32[]{:S(2)}) collective-permute-start(f32[64,256]{1,0:T(8,128)S(1)} %far.1.refs_0_), channel_id=1, source_target_pairs={{2,0},{3,1},{0,2},{1,3},{6,4},{7,5},{4,6},{5,7},{10,8},{11,9},{8,1... | collective-permute-start | bytes 196616 | tf_op jit(solution)/shard_map/ppermute | solution.py:522
  87.3 5.3 %collective-permute-done.19.refs_3_ = f32[128,1024]{1,0:T(8,128)S(1)} collective-permute-done((f32[128,1024]{1,0:T(8,128)S(1)}, f32[128,1024]{1,0:T(8,128)S(1)}, u32[]{:S(2)}, u32[]{:S(2)}) %collective-permute-start.19) | collective-permute-done | bytes 524320 | tf_op jit(solution)/shard_map/ppermute | solution.py:525
  93.4 3.6 %collective-permute-done.16.refs_3_ = f32[64,256]{1,0:T(8,128)S(1)} collective-permute-done((f32[64,256]{1,0:T(8,128)S(1)}, f32[64,256]{1,0:T(8,128)S(1)}, u32[]{:S(2)}, u32[]{:S(2)}) %collective-permute-start.16) | collective-permute-done | bytes 65568 | tf_op jit(solution)/shard_map/ppermute | solution.py:522
  97.0 2.2 %join.1 = f32[256,1024]{1,0:T(8,128)} custom-call(s32[4]{0:T(128)S(1)} %copy-done.7, f32[2,512,256]{2,1,0:T(8,128)S(1)} %copy-done.3, f32[64,256]{1,0:T(8,128)S(1)} %far.1.refs_0_, f32[64,256]{1,0:T(8,128)S(1)} %collective-permute-done.14.refs_1_, f32[64,256]{1,0:T(8,128)S(1)} %collective-permute-done.15.refs_2_, ...), custom_call_target="tpu_custom_call" | custom-call | tf_op jit(solution)/shard_map/join/pallas_call | solution.py:491
  (58 shorter events, 11.6 us)
Async XLA Ops:
  0.0 12.2 %collective-permute-start.6 = (f32[64,1024]{1,0:T(8,128)}, f32[64,1024]{1,0:T(8,128)}, u32[]{:S(2)}, u32[]{:S(2)}) collective-permute-start(f32[64,1024]{1,0:T(8,128)} %refs_6_.1), channel_id=1, source_target_pairs={{0,4},{4,0},{8,12},{12,8},{16,20},{20,16},{24,28},{28,24},{1,5},{5... | collective-permute-start | bytes 786440 | tf_op jit(solution)/shard_map/ppermute | solution.py:536
  5.3 19.4 %collective-permute-start.8 = (f32[128,1024]{1,0:T(8,128)}, f32[128,1024]{1,0:T(8,128)}, u32[]{:S(2)}, u32[]{:S(2)}) collective-permute-start(f32[128,1024]{1,0:T(8,128)} %get-tuple-element.58), channel_id=1, source_target_pairs={{0,4},{4,0},{8,12},{12,8},{16,20},{20,16},{24,28},{28,24},{1,5},{5... | collective-permute-start | bytes 1572872 | tf_op jit(solution)/shard_map/ppermute | solution.py:537
  10.0 18.1 %collective-permute-start = (f32[88,1024]{1,0:T(8,128)}, f32[88,1024]{1,0:T(8,128)S(1)}, u32[]{:S(2)}, u32[]{:S(2)}) collective-permute-start(f32[88,1024]{1,0:T(8,128)} %get-tuple-element.32), channel_id=1, source_target_pairs={{1,0},{0,1},{3,2},{2,3},{5,4},{4,5},{7,6},{6,7},{9,8},{8,9},{11,10... | collective-permute-start | bytes 1081352 | tf_op jit(solution)/shard_map/ppermute | solution.py:540
  10.1 18.1 %collective-permute-start.1 = (f32[88,1024]{1,0:T(8,128)}, f32[88,1024]{1,0:T(8,128)S(1)}, u32[]{:S(2)}, u32[]{:S(2)}) collective-permute-start(f32[88,1024]{1,0:T(8,128)} %get-tuple-element.33), channel_id=1, source_target_pairs={{2,0},{3,1},{0,2},{1,3},{6,4},{7,5},{4,6},{5,7},{10,8},{11,9},{8,1... | collective-permute-start | bytes 1081352 | tf_op jit(solution)/shard_map/ppermute | solution.py:540
  12.1 16.7 %collective-permute-start.2 = (f32[88,1024]{1,0:T(8,128)}, f32[88,1024]{1,0:T(8,128)S(1)}, u32[]{:S(2)}, u32[]{:S(2)}) collective-permute-start(f32[88,1024]{1,0:T(8,128)} %get-tuple-element.34), channel_id=1, source_target_pairs={{3,0},{2,1},{1,2},{0,3},{7,4},{6,5},{5,6},{4,7},{11,8},{10,9},{9,1... | collective-permute-start | bytes 1081352 | tf_op jit(solution)/shard_map/ppermute | solution.py:540
  12.2 10.1 %collective-permute-start.7 = (f32[64,1024]{1,0:T(8,128)}, f32[64,1024]{1,0:T(8,128)S(1)}, u32[]{:S(2)}, u32[]{:S(2)}) collective-permute-start(f32[64,1024]{1,0:T(8,128)} %collective-permute-done.6.refs_6_), channel_id=1, source_target_pairs={{0,8},{8,16},{16,24},{12,4},{20,12},{28,20},{1,9},{9,17},{17,25},{... | collective-permute-start | bytes 786440 | tf_op jit(solution)/shard_map/ppermute | solution.py:544
  22.3 14.2 %collective-permute-start.10 = (f32[128,1024]{1,0:T(8,128)}, f32[128,1024]{1,0:T(8,128)S(1)}, u32[]{:S(2)}, u32[]{:S(2)}) collective-permute-start(f32[128,1024]{1,0:T(8,128)} %get-tuple-element.57), channel_id=1, source_target_pairs={{0,4},{4,0},{8,12},{12,8},{16,20},{20,16},{24,28},{28,24},{1,5},{5... | collective-permute-start | bytes 1572872 | tf_op jit(solution)/shard_map/ppermute | solution.py:537
  24.6 34.4 %collective-permute-start.9 = (f32[128,1024]{1,0:T(8,128)}, f32[128,1024]{1,0:T(8,128)S(1)}, u32[]{:S(2)}, u32[]{:S(2)}) collective-permute-start(f32[128,1024]{1,0:T(8,128)} %collective-permute-done.8.refs_7_), channel_id=1, source_target_pairs={{0,8},{8,16},{16,24},{12,4},{20,12},{28,20},{1,9},{9,17},{17,25},{... | collective-permute-start | bytes 1572872 | tf_op jit(solution)/shard_map/ppermute | solution.py:546
  31.1 13.5 %copy-start.5 = (f32[64,1024]{1,0:T(8,128)S(1)}, f32[64,1024]{1,0:T(8,128)}, u32[]{:S(2)}) copy-start(f32[64,1024]{1,0:T(8,128)} %refs_6_.1) | copy-start | bytes 786436
  36.5 25.3 %collective-permute-start.12 = (f32[128,1024]{1,0:T(8,128)S(1)}, f32[128,1024]{1,0:T(8,128)S(1)}, u32[]{:S(2)}, u32[]{:S(2)}) collective-permute-start(f32[128,1024]{1,0:T(8,128)S(1)} %collective-permute-done.10.refs_8_), channel_id=1, source_target_pairs={{0,8},{8,16},{16,24},{12,4},{20,12},{28,20},{1,9},{9,17},{17,25},{... | collective-permute-start | bytes 1572872 | tf_op jit(solution)/shard_map/ppermute | solution.py:556
  40.2 21.5 %collective-permute-start.3 = (f32[128,256]{1,0:T(8,128)S(1)}, f32[128,256]{1,0:T(8,128)S(1)}, u32[]{:S(2)}, u32[]{:S(2)}) collective-permute-start(f32[128,256]{1,0:T(8,128)S(1)} %get-tuple-element.45.refs_0_), channel_id=1, source_target_pairs={{0,8},{4,12},{8,0},{12,4},{16,24},{20,28},{24,16},{28,20},{1,9},{5... | collective-permute-start | bytes 393224 | tf_op jit(solution)/shard_map/ppermute | solution.py:551
  41.8 19.9 %collective-permute-start.4 = (f32[128,256]{1,0:T(8,128)S(1)}, f32[128,256]{1,0:T(8,128)S(1)}, u32[]{:S(2)}, u32[]{:S(2)}) collective-permute-start(f32[128,256]{1,0:T(8,128)S(1)} %get-tuple-element.45.refs_0_), channel_id=1, source_target_pairs={{0,16},{4,20},{8,24},{12,28},{16,0},{20,4},{24,8},{28,12},{1,17},{... | collective-permute-start | bytes 393224 | tf_op jit(solution)/shard_map/ppermute | solution.py:551
  42.9 18.8 %collective-permute-start.5 = (f32[128,256]{1,0:T(8,128)S(1)}, f32[128,256]{1,0:T(8,128)S(1)}, u32[]{:S(2)}, u32[]{:S(2)}) collective-permute-start(f32[128,256]{1,0:T(8,128)S(1)} %get-tuple-element.45.refs_0_), channel_id=1, source_target_pairs={{0,24},{4,28},{8,16},{12,20},{16,8},{20,12},{24,0},{28,4},{1,25},{... | collective-permute-start | bytes 393224 | tf_op jit(solution)/shard_map/ppermute | solution.py:551
  60.3 6.3 %collective-permute-start.17 = (f32[128,1024]{1,0:T(8,128)S(1)}, f32[128,1024]{1,0:T(8,128)S(1)}, u32[]{:S(2)}, u32[]{:S(2)}) collective-permute-start(f32[128,1024]{1,0:T(8,128)S(1)} %get-tuple-element.44), channel_id=1, source_target_pairs={{1,0},{0,1},{3,2},{2,3},{5,4},{4,5},{7,6},{6,7},{9,8},{8,9},{11,10... | collective-permute-start | bytes 1572872 | tf_op jit(solution)/shard_map/ppermute | solution.py:522
  63.3 5.0 %collective-permute-start.13 = (f32[128,1024]{1,0:T(8,128)S(1)}, f32[128,1024]{1,0:T(8,128)S(1)}, u32[]{:S(2)}, u32[]{:S(2)}) collective-permute-start(f32[128,1024]{1,0:T(8,128)S(1)} %get-tuple-element.50), channel_id=1, source_target_pairs={{1,0},{0,1},{3,2},{2,3},{5,4},{4,5},{7,6},{6,7},{9,8},{8,9},{11,10... | collective-permute-start | bytes 1572872 | tf_op jit(solution)/shard_map/ppermute | solution.py:522
  63.4 15.8 %collective-permute-start.11 = (f32[4,128,256]{2,1,0:T(8,128)S(1)}, f32[4,128,256]{2,1,0:T(8,128)S(1)}, u32[]{:S(2)}, u32[]{:S(2)}) collective-permute-start(f32[4,128,256]{2,1,0:T(8,128)S(1)} %stack.17.refs_11_.alike_ref), channel_id=1, source_target_pairs={{0,4},{4,0},{8,12},{12,8},{16,20},{20,16},{24,28},{28,24},{1,5},{5... | collective-permute-start | bytes 1572872 | tf_op jit(solution)/shard_map/ppermute | solution.py:565
  66.7 19.1 %collective-permute-start.18 = (f32[128,1024]{1,0:T(8,128)S(1)}, f32[128,1024]{1,0:T(8,128)S(1)}, u32[]{:S(2)}, u32[]{:S(2)}) collective-permute-start(f32[128,1024]{1,0:T(8,128)S(1)} %add_parts.4), channel_id=1, source_target_pairs={{2,0},{3,1},{0,2},{1,3},{6,4},{7,5},{4,6},{5,7},{10,8},{11,9},{8,1... | collective-permute-start | bytes 1572872 | tf_op jit(solution)/shard_map/ppermute | solution.py:525
  68.3 24.3 %collective-permute-start.19 = (f32[128,1024]{1,0:T(8,128)S(1)}, f32[128,1024]{1,0:T(8,128)S(1)}, u32[]{:S(2)}, u32[]{:S(2)}) collective-permute-start(f32[128,1024]{1,0:T(8,128)S(1)} %add_parts.3.refs_14_), channel_id=1, source_target_pairs={{2,0},{3,1},{0,2},{1,3},{6,4},{7,5},{4,6},{5,7},{10,8},{11,9},{8,1... | collective-permute-start | bytes 1572872 | tf_op jit(solution)/shard_map/ppermute | solution.py:525
  74.4 22.6 %collective-permute-start.20 = (f32[128,1024]{1,0:T(8,128)S(1)}, f32[128,1024]{1,0:T(8,128)S(1)}, u32[]{:S(2)}, u32[]{:S(2)}) collective-permute-start(f32[128,1024]{1,0:T(8,128)S(1)} %get-tuple-element.55), channel_id=1, source_target_pairs={{1,0},{0,1},{3,2},{2,3},{5,4},{4,5},{7,6},{6,7},{9,8},{8,9},{11,10... | collective-permute-start | bytes 1572872 | tf_op jit(solution)/shard_map/ppermute | solution.py:522
  74.5 22.5 %collective-permute-start.21 = (f32[128,1024]{1,0:T(8,128)S(1)}, f32[128,1024]{1,0:T(8,128)S(1)}, u32[]{:S(2)}, u32[]{:S(2)}) collective-permute-start(f32[128,1024]{1,0:T(8,128)S(1)} %get-tuple-element.56), channel_id=1, source_target_pairs={{1,0},{0,1},{3,2},{2,3},{5,4},{4,5},{7,6},{6,7},{9,8},{8,9},{11,10... | collective-permute-start | bytes 1572872 | tf_op jit(solution)/shard_map/ppermute | solution.py:522
  79.1 17.9 %copy-start.3 = (f32[2,512,256]{2,1,0:T(8,128)S(1)}, f32[2,512,256]{2,1,0:T(8,128)}, u32[]{:S(2)}) copy-start(f32[2,512,256]{2,1,0:T(8,128)} %interp_ref.1) | copy-start | bytes 3145732
  85.7 7.1 %collective-permute-start.14 = (f32[64,256]{1,0:T(8,128)S(1)}, f32[64,256]{1,0:T(8,128)S(1)}, u32[]{:S(2)}, u32[]{:S(2)}) collective-permute-start(f32[64,256]{1,0:T(8,128)S(1)} %far.1.refs_0_), channel_id=1, source_target_pairs={{1,0},{0,1},{3,2},{2,3},{5,4},{4,5},{7,6},{6,7},{9,8},{8,9},{11,10... | collective-permute-start | bytes 196616 | tf_op jit(solution)/shard_map/ppermute | solution.py:522
  85.8 7.6 %collective-permute-start.15 = (f32[64,256]{1,0:T(8,128)S(1)}, f32[64,256]{1,0:T(8,128)S(1)}, u32[]{:S(2)}, u32[]{:S(2)}) collective-permute-start(f32[64,256]{1,0:T(8,128)S(1)} %far.1.refs_0_), channel_id=1, source_target_pairs={{2,0},{3,1},{0,2},{1,3},{6,4},{7,5},{4,6},{5,7},{10,8},{11,9},{8,1... | collective-permute-start | bytes 196616 | tf_op jit(solution)/shard_map/ppermute | solution.py:522
  92.7 4.3 %collective-permute-start.16 = (f32[64,256]{1,0:T(8,128)S(1)}, f32[64,256]{1,0:T(8,128)S(1)}, u32[]{:S(2)}, u32[]{:S(2)}) collective-permute-start(f32[64,256]{1,0:T(8,128)S(1)} %far.1.refs_0_), channel_id=1, source_target_pairs={{3,0},{2,1},{1,2},{0,3},{7,4},{6,5},{5,6},{4,7},{11,8},{10,9},{9,1... | collective-permute-start | bytes 196616 | tf_op jit(solution)/shard_map/ppermute | solution.py:522
  (9 other events, 67.5 us)

commit v2 on v1

--- a/solution.py
+++ b/solution.py
@@ -449,13 +449,14 @@
 
 
 def final_body(xs, pos_ref, interp_ref, *refs):
-    values, sums = refs[: 2 * xs], refs[2 * xs : -2]
+    values, sums = refs[:xs], refs[xs:-2]
     out_ref, v_scr = refs[-2:]
     rows = R // (2 * xs)
     x, core = pos_ref[0], pos_ref[1]
-    for n, ref in enumerate(values):
-        helper = 2 * lax.rem(x + n // 2, xs) + (core if n % 2 == 0 else 1 - core)
-        v_scr[pl.ds(pl.multiple_of(helper * rows, rows), rows), :] = ref[...]
+    for dx, ref in enumerate(values):
+        for dc in range(2):
+            helper = 2 * lax.rem(x + dx, xs) + (core if dc == 0 else 1 - core)
+            v_scr[pl.ds(pl.multiple_of(helper * rows, rows), rows), :] = ref[dc]
     value = v_scr[...]
     for leaf in range(2):
         cols = slice(leaf * LEAF, (leaf + 1) * LEAF)
@@ -492,7 +493,7 @@
         partial(final_body, xs),
         name="join",
         out_shape=jax.ShapeDtypeStruct((R, 2 * LEAF), F32),
-        in_specs=[pl.BlockSpec(memory_space=pltpu.SMEM)] + [vmem] * (1 + 2 * xs + 4),
+        in_specs=[pl.BlockSpec(memory_space=pltpu.SMEM)] + [vmem] * (1 + xs + 4),
         out_specs=vmem,
         scratch_shapes=[pltpu.VMEM((R, SK), F32)],
         compiler_params=pltpu.CompilerParams(vmem_limit_bytes=VMEM_LIMIT),
@@ -542,7 +543,7 @@
         if n
     ]
     pts_z = lax.ppermute(pts_y, "leaf", across)
-    pts_z, w_y[0] = together(pts_z, w_y[0])
+    got, pts_z = together(got, pts_z)
     w_z = [lax.ppermute(w_y[0], "leaf", across)]
     msgs = [sent[0]] + [got[order.index((-dx % xs, dc)) - 1] for dx, dc in order[1:]]
     payload, targets = skel_call(xs, pos, skel_group, msgs)
@@ -578,7 +579,8 @@
     sources = [pair_src, ("next", z_side, w_z)]
     home = near_call("near_home", pos, msgs, targets, home, sources, R, 0, [own], both[:1])
     v_own = far_call(groups, pos, far_nodes, skel_node, transfer, alike, side, home[:1])
-    values = [v_own] + [from_help(v_own, dx, dc) for dx, dc in order[1:]]
+    v_pair = stack_call([v_own, from_help(v_own, 0, 1)])
+    values = [v_pair] + [from_help(v_pair, dx, 0) for dx in range(1, xs)]
     mate = [from_help(value, 0, 1) for value in home[2:]]
     mine = add_call(*[[home[c], *parts[c]] for c in range(2)])
     return final_call(xs, pos, interp, mine, mate, values)

time: 100 us -> 104 us (1.040)
  starting transfers between devices: 31.9 us -> 34.2 us
  Pallas kernels: 36.9 us -> 38.3 us
    ppermute x3, waiting for transfers between devices: 0.65 us -> 12.8 us  [shards(): lax.ppermute(sent[n], 'help', help_pairs(xs, -dx, dc))]
    ppermute x1, waiting for transfers between devices: 6.36 us -> 0.01 us  [shards(): pts_z = lax.ppermute(pts_y, 'leaf', across)]
    ppermute x2, waiting for transfers between devices: 4.01 us -> 0.01 us  [shards(): lax.ppermute(chunk, 'leaf', beside)]
    ppermute x3, waiting for transfers between devices: 0.01 us -> 3.69 us  [shards(): lax.ppermute(payload, 'leaf', [(i, i ^ mask) for i in range(groups)])]
    ppermute x1, starting transfers between devices: 3.24 us -> 6.28 us  [shards(): side = lax.ppermute(alike, 'leaf', beside)]
    ppermute x2, starting transfers between devices: 2.32 us -> 0.07 us  [shards(): lax.ppermute(chunk, 'leaf', beside)]
    ppermute x1, waiting for transfers between devices: 4.14 us -> 2.07 us  [shards(): side = lax.ppermute(alike, 'leaf', beside)]
    ppermute x2, waiting for transfers between devices: 5.35 us -> 3.84 us  [to_help(): return lax.ppermute(value, 'help', help_pairs(xs, -dx, 0))]
  transfers between devices with their start and end apart: 22 -> 21, of which waited for: 7 -> 8; matrix products, arithmetic and copies ran while one was open for 3% -> 3% of each run, Pallas kernels for 35% -> 35%
where the time goes in v2:
time: 104 us
  Pallas kernels  38.3 us (37%)
  starting transfers between devices  34.2 us (33%)
  waiting for transfers between devices  25.6 us (25%)
  local copies, waits for them, and re-layouts  4.59 us (4%)
    pallas_call x5, Pallas kernels, near_call(): pl.pallas_call(partial(near_body, len(msgs) // 2, sets, leaves_at, rows,...  23.5 us
    ppermute x3, waiting for transfers between devices, shards(): lax.ppermute(sent[n], 'help', help_pairs(xs, -dx, dc))  12.8 us
    pallas_call x1, Pallas kernels, far_call(): pl.pallas_call(partial(far_body, groups, rows), name='far', out_shape=jax...  6.51 us
    ppermute x1, starting transfers between devices, shards(): side = lax.ppermute(alike, 'leaf', beside)  6.28 us
    ppermute x3, starting transfers between devices, shards(): lax.ppermute(payload, 'leaf', [(i, i ^ mask) for i in range(groups)])  4.45 us
    ppermute x6, starting transfers between devices, from_help(): return lax.ppermute(value, 'help', help_pairs(xs, dx, dc))  4.12 us
    pallas_call x1, Pallas kernels, leaf_call(): pl.pallas_call(partial(leaf_body, xs), name='leaf_up', out_shape=[jax.Sha...  4.06 us
    ppermute x2, waiting for transfers between devices, to_help(): return lax.ppermute(value, 'help', help_pairs(xs, -dx, 0))  3.84 us
  transfers between devices with their start and end apart: 21, of which 8 were waited for; matrix products, arithmetic and copies ran while one was open for 3% of the time, Pallas kernels for 35%

profile of v2, /device:TPU:0, one launch (start us, length us, event | category | flops | bytes accessed | tf_op | source)
XLA Modules:
  0.0 103.6 jit_solution(17623029715951151216)
XLA Ops:
  0.0 3.0 %collective-permute-start.3 = (f32[64,1024]{1,0:T(8,128)}, f32[64,1024]{1,0:T(8,128)}, u32[]{:S(2)}, u32[]{:S(2)}) collective-permute-start(f32[64,1024]{1,0:T(8,128)} %refs_6_.1), channel_id=1, source_target_pairs={{0,4},{4,0},{8,12},{12,8},{16,20},{20,16},{24,28},{28,24},{1,5},{5... | collective-permute-start | bytes 786440 | tf_op jit(solution)/shard_map/ppermute | solution.py:537
  3.0 2.3 %fusion = (f32[128,1024]{1,0:T(8,128)}, f32[128,1024]{1,0:T(8,128)}) fusion(f32[256,1024]{1,0:T(8,128)} %refs_7_.1), kind=kLoop, calls=%fused_computation.1 | loop fusion | bytes 2097152 | tf_op jit(solution)/shard_map/slice | solution.py:538
  5.9 4.1 %leaf_up.1 = (f32[88,1024]{1,0:T(8,128)}, f32[88,1024]{1,0:T(8,128)}, f32[88,1024]{1,0:T(8,128)}, f32[88,1024]{1,0:T(8,128)}) custom-call(s32[4]{0:T(128)} %pad_add_fusion.pos_ref, s32[1,2]{1,0:T(1,128)} %count_ref.1, s32[2,32]{1,0:T(2,128)} %src_ref.1, f32[64,1024]{1,0:T(8,128)} %refs_6_.1, f32[256,1024]{1,0:T(8,128)} %refs_7_.1, f32[2,512,256]{2,1,0:T(8,128)} %interp_ref.1), custom_call_target="tpu_custom_call" | custom-call | tf_op jit(solution)/shard_map/leaf_up/pallas_call | solution.py:292
  10.0 2.1 %collective-permute-start.1 = (f32[88,1024]{1,0:T(8,128)}, f32[88,1024]{1,0:T(8,128)S(1)}, u32[]{:S(2)}, u32[]{:S(2)}) collective-permute-start(f32[88,1024]{1,0:T(8,128)} %get-tuple-element.35), channel_id=1, source_target_pairs={{2,0},{3,1},{0,2},{1,3},{6,4},{7,5},{4,6},{5,7},{10,8},{11,9},{8,1... | collective-permute-start | bytes 1081352 | tf_op jit(solution)/shard_map/ppermute | solution.py:541
  12.1 3.7 %collective-permute-start.4 = (f32[64,1024]{1,0:T(8,128)}, f32[64,1024]{1,0:T(8,128)S(1)}, u32[]{:S(2)}, u32[]{:S(2)}) collective-permute-start(f32[64,1024]{1,0:T(8,128)} %collective-permute-done.3.refs_6_), channel_id=1, source_target_pairs={{0,8},{8,16},{16,24},{12,4},{20,12},{28,20},{1,9},{9,17},{17,25},{... | collective-permute-start | bytes 786440 | tf_op jit(solution)/shard_map/ppermute | solution.py:545
  16.0 5.6 %collective-permute-done.1.refs_2_ = f32[88,1024]{1,0:T(8,128)S(1)} collective-permute-done((f32[88,1024]{1,0:T(8,128)}, f32[88,1024]{1,0:T(8,128)S(1)}, u32[]{:S(2)}, u32[]{:S(2)}) %collective-permute-start.1) | collective-permute-done | bytes 360480 | tf_op jit(solution)/shard_map/ppermute | solution.py:541
  21.6 7.1 %collective-permute-done.2.refs_3_ = f32[88,1024]{1,0:T(8,128)S(1)} collective-permute-done((f32[88,1024]{1,0:T(8,128)}, f32[88,1024]{1,0:T(8,128)S(1)}, u32[]{:S(2)}, u32[]{:S(2)}) %collective-permute-start.2) | collective-permute-done | bytes 360480 | tf_op jit(solution)/shard_map/ppermute | solution.py:541
  28.7 3.6 %collective-permute-start.9 = (f32[128,1024]{1,0:T(8,128)}, f32[128,1024]{1,0:T(8,128)S(1)}, u32[]{:S(2)}, u32[]{:S(2)}) collective-permute-start(f32[128,1024]{1,0:T(8,128)} %collective-permute-done.8.refs_7_), channel_id=1, source_target_pairs={{0,8},{8,16},{16,24},{12,4},{20,12},{28,20},{1,9},{9,17},{17,25},{... | collective-permute-start | bytes 1572872 | tf_op jit(solution)/shard_map/ppermute | solution.py:547
  35.9 3.5 %collective-permute-start.12 = (f32[128,1024]{1,0:T(8,128)S(1)}, f32[128,1024]{1,0:T(8,128)S(1)}, u32[]{:S(2)}, u32[]{:S(2)}) collective-permute-start(f32[128,1024]{1,0:T(8,128)S(1)} %collective-permute-done.10.refs_8_), channel_id=1, source_target_pairs={{0,8},{8,16},{16,24},{12,4},{20,12},{28,20},{1,9},{9,17},{17,25},{... | collective-permute-start | bytes 1572872 | tf_op jit(solution)/shard_map/ppermute | solution.py:557
  39.4 1.6 %collective-permute-start.5 = (f32[128,256]{1,0:T(8,128)S(1)}, f32[128,256]{1,0:T(8,128)S(1)}, u32[]{:S(2)}, u32[]{:S(2)}) collective-permute-start(f32[128,256]{1,0:T(8,128)S(1)} %get-tuple-element.49.refs_0_), channel_id=1, source_target_pairs={{0,8},{4,12},{8,0},{12,4},{16,24},{20,28},{24,16},{28,20},{1,9},{5... | collective-permute-start | bytes 393224 | tf_op jit(solution)/shard_map/ppermute | solution.py:552
  41.0 2.8 %collective-permute-start.7 = (f32[128,256]{1,0:T(8,128)S(1)}, f32[128,256]{1,0:T(8,128)S(1)}, u32[]{:S(2)}, u32[]{:S(2)}) collective-permute-start(f32[128,256]{1,0:T(8,128)S(1)} %get-tuple-element.49.refs_0_), channel_id=1, source_target_pairs={{0,24},{4,28},{8,16},{12,20},{16,8},{20,12},{24,0},{28,4},{1,25},{... | collective-permute-start | bytes 393224 | tf_op jit(solution)/shard_map/ppermute | solution.py:552
  44.4 9.8 %near_own.1.refs_9_.refs_13_ = f32[8,256,512]{2,1,0:T(8,128)S(1)} custom-call(s32[4]{0:T(128)S(1)} %copy-done.6, f32[88,1024]{1,0:T(8,128)S(1)} %copy-done.2, f32[88,1024]{1,0:T(8,128)S(1)} %collective-permute-done.refs_1_, f32[88,1024]{1,0:T(8,128)S(1)} %collective-permute-done.1.refs_2_, f32[88,1024]{1,0:T(8,128)S(1)} %collective-permute-done.2.refs_3_, ...), custom_call_target="tpu_custom_call" | custom-call | tf_op jit(solution)/shard_map/near_own/pallas_call | solution.py:206
  54.3 4.7 %near_pair.1.refs_10_.refs_11_ = f32[4,256,512]{2,1,0:T(8,128)S(1)} custom-call(s32[4]{0:T(128)S(1)} %copy-done.6, f32[88,1024]{1,0:T(8,128)S(1)} %copy-done.2, f32[88,1024]{1,0:T(8,128)S(1)} %collective-permute-done.refs_1_, f32[88,1024]{1,0:T(8,128)S(1)} %collective-permute-done.1.refs_2_, f32[88,1024]{1,0:T(8,128)S(1)} %collective-permute-done.2.refs_3_, ...), custom_call_target="tpu_custom_call" | custom-call | tf_op jit(solution)/shard_map/near_pair/pallas_call | solution.py:206
  61.6 2.5 %collective-permute-done.7.refs_3_ = f32[128,256]{1,0:T(8,128)S(1)} collective-permute-done((f32[128,256]{1,0:T(8,128)S(1)}, f32[128,256]{1,0:T(8,128)S(1)}, u32[]{:S(2)}, u32[]{:S(2)}) %collective-permute-start.7) | collective-permute-done | bytes 131104 | tf_op jit(solution)/shard_map/ppermute | solution.py:552
  64.2 1.5 %near_next_away.3 = (f32[128,1024]{1,0:T(8,128)S(1)}, f32[128,1024]{1,0:T(8,128)S(1)}) custom-call(s32[4]{0:T(128)S(1)} %copy-done.6, f32[88,1024]{1,0:T(8,128)S(1)} %copy-done.2, f32[88,1024]{1,0:T(8,128)S(1)} %collective-permute-done.refs_1_, f32[88,1024]{1,0:T(8,128)S(1)} %collective-permute-done.1.refs_2_, ...), custom_call_target="tpu_custom_call" | custom-call | tf_op jit(solution)/shard_map/near_next_away/pallas_call | solution.py:206
  65.8 6.3 %collective-permute-start.11 = (f32[4,128,256]{2,1,0:T(8,128)S(1)}, f32[4,128,256]{2,1,0:T(8,128)S(1)}, u32[]{:S(2)}, u32[]{:S(2)}) collective-permute-start(f32[4,128,256]{2,1,0:T(8,128)S(1)} %stack.18.refs_11_.alike_ref), channel_id=1, source_target_pairs={{0,4},{4,0},{8,12},{12,8},{16,20},{20,16},{24,28},{28,24},{1,5},{5... | collective-permute-start | bytes 1572872 | tf_op jit(solution)/shard_map/ppermute | solution.py:566
  72.1 3.2 %collective-permute-start.17 = (f32[128,1024]{1,0:T(8,128)S(1)}, f32[128,1024]{1,0:T(8,128)S(1)}, u32[]{:S(2)}, u32[]{:S(2)}) collective-permute-start(f32[128,1024]{1,0:T(8,128)S(1)} %add_parts.4), channel_id=1, source_target_pairs={{2,0},{3,1},{0,2},{1,3},{6,4},{7,5},{4,6},{5,7},{10,8},{11,9},{8,1... | collective-permute-start | bytes 1572872 | tf_op jit(solution)/shard_map/ppermute | solution.py:526
  75.5 6.1 %near_home.1 = (f32[128,1024]{1,0:T(8,128)S(1)}, f32[128,1024]{1,0:T(8,128)S(1)}, f32[128,1024]{1,0:T(8,128)S(1)}, f32[128,1024]{1,0:T(8,128)S(1)}) custom-call(s32[4]{0:T(128)S(1)} %copy-done.7, f32[88,1024]{1,0:T(8,128)S(1)} %copy-done.2, f32[88,1024]{1,0:T(8,128)S(1)} %collective-permute-done.refs_1_, f32[88,1024]{1,0:T(8,128)S(1)} %collective-permute-done.1.refs_2_, ...), custom_call_target="tpu_custom_call" | custom-call | tf_op jit(solution)/shard_map/near_home/pallas_call | solution.py:206
  82.2 2.1 %collective-permute-done.11.beside_ref = f32[4,128,256]{2,1,0:T(8,128)S(1)} collective-permute-done((f32[4,128,256]{2,1,0:T(8,128)S(1)}, f32[4,128,256]{2,1,0:T(8,128)S(1)}, u32[]{:S(2)}, u32[]{:S(2)}) %collective-permute-start.11) | collective-permute-done | bytes 524320 | tf_op jit(solution)/shard_map/ppermute | solution.py:566
  84.3 6.5 %far.1.refs_0_ = f32[64,256]{1,0:T(8,128)S(1)} custom-call(s32[4]{0:T(128)S(1)} %copy-done.7, s32[4,14]{1,0:T(4,128)S(1)} %bitcast.4, s32[6,256]{1,0:T(8,128)S(1)} %copy-done.8, f32[6,512,256]{2,1,0:T(8,128)S(1)} %copy-done.4, f32[4,128,256]{2,1,0:T(8,128)S(1)} %stack.18.refs_11_.alike_ref, f32[4,128,256]{2,1,0:T(8,128)S(1)} %collective-permute-done.11.beside_ref, ...), custom_call_target="tpu_custom_call" | custom-call | tf_op jit(solution)/shard_map/far/pallas_call | solution.py:435
  92.1 3.3 %collective-permute-start.15 = (f32[2,64,256]{2,1,0:T(8,128)S(1)}, f32[2,64,256]{2,1,0:T(8,128)S(1)}, u32[]{:S(2)}, u32[]{:S(2)}) collective-permute-start(f32[2,64,256]{2,1,0:T(8,128)S(1)} %stack.19.refs_0_), channel_id=1, source_target_pairs={{2,0},{3,1},{0,2},{1,3},{6,4},{7,5},{4,6},{5,7},{10,8},{11,9},{8,1... | collective-permute-start | bytes 393224 | tf_op jit(solution)/shard_map/ppermute | solution.py:523
  95.5 3.8 %collective-permute-done.18.refs_3_ = f32[128,1024]{1,0:T(8,128)S(1)} collective-permute-done((f32[128,1024]{1,0:T(8,128)S(1)}, f32[128,1024]{1,0:T(8,128)S(1)}, u32[]{:S(2)}, u32[]{:S(2)}) %collective-permute-start.18) | collective-permute-done | bytes 524320 | tf_op jit(solution)/shard_map/ppermute | solution.py:526
  99.4 2.0 %collective-permute-done.15.refs_1_ = f32[2,64,256]{2,1,0:T(8,128)S(1)} collective-permute-done((f32[2,64,256]{2,1,0:T(8,128)S(1)}, f32[2,64,256]{2,1,0:T(8,128)S(1)}, u32[]{:S(2)}, u32[]{:S(2)}) %collective-permute-start.15) | collective-permute-done | bytes 131104 | tf_op jit(solution)/shard_map/ppermute | solution.py:523
  101.4 2.2 %join.1 = f32[256,1024]{1,0:T(8,128)} custom-call(s32[4]{0:T(128)S(1)} %copy-done.7, f32[2,512,256]{2,1,0:T(8,128)S(1)} %copy-done.3, f32[2,64,256]{2,1,0:T(8,128)S(1)} %stack.19.refs_0_, f32[2,64,256]{2,1,0:T(8,128)S(1)} %collective-permute-done.15.refs_1_, f32[128,1024]{1,0:T(8,128)S(1)} %get-tuple-element.57.refs_2_, ...), custom_call_target="tpu_custom_call" | custom-call | tf_op jit(solution)/shard_map/join/pallas_call | solution.py:492
  (57 shorter events, 9.9 us)
Async XLA Ops:
  0.0 12.1 %collective-permute-start.3 = (f32[64,1024]{1,0:T(8,128)}, f32[64,1024]{1,0:T(8,128)}, u32[]{:S(2)}, u32[]{:S(2)}) collective-permute-start(f32[64,1024]{1,0:T(8,128)} %refs_6_.1), channel_id=1, source_target_pairs={{0,4},{4,0},{8,12},{12,8},{16,20},{20,16},{24,28},{28,24},{1,5},{5... | collective-permute-start | bytes 786440 | tf_op jit(solution)/shard_map/ppermute | solution.py:537
  5.3 23.5 %collective-permute-start.8 = (f32[128,1024]{1,0:T(8,128)}, f32[128,1024]{1,0:T(8,128)}, u32[]{:S(2)}, u32[]{:S(2)}) collective-permute-start(f32[128,1024]{1,0:T(8,128)} %get-tuple-element.62), channel_id=1, source_target_pairs={{0,4},{4,0},{8,12},{12,8},{16,20},{20,16},{24,28},{28,24},{1,5},{5... | collective-permute-start | bytes 1572872 | tf_op jit(solution)/shard_map/ppermute | solution.py:538
  9.9 5.9 %collective-permute-start = (f32[88,1024]{1,0:T(8,128)}, f32[88,1024]{1,0:T(8,128)S(1)}, u32[]{:S(2)}, u32[]{:S(2)}) collective-permute-start(f32[88,1024]{1,0:T(8,128)} %get-tuple-element.34), channel_id=1, source_target_pairs={{1,0},{0,1},{3,2},{2,3},{5,4},{4,5},{7,6},{6,7},{9,8},{8,9},{11,10... | collective-permute-start | bytes 1081352 | tf_op jit(solution)/shard_map/ppermute | solution.py:541
  10.0 11.6 %collective-permute-start.1 = (f32[88,1024]{1,0:T(8,128)}, f32[88,1024]{1,0:T(8,128)S(1)}, u32[]{:S(2)}, u32[]{:S(2)}) collective-permute-start(f32[88,1024]{1,0:T(8,128)} %get-tuple-element.35), channel_id=1, source_target_pairs={{2,0},{3,1},{0,2},{1,3},{6,4},{7,5},{4,6},{5,7},{10,8},{11,9},{8,1... | collective-permute-start | bytes 1081352 | tf_op jit(solution)/shard_map/ppermute | solution.py:541
  12.1 16.7 %collective-permute-start.2 = (f32[88,1024]{1,0:T(8,128)}, f32[88,1024]{1,0:T(8,128)S(1)}, u32[]{:S(2)}, u32[]{:S(2)}) collective-permute-start(f32[88,1024]{1,0:T(8,128)} %get-tuple-element.36), channel_id=1, source_target_pairs={{3,0},{2,1},{1,2},{0,3},{7,4},{6,5},{5,6},{4,7},{11,8},{10,9},{9,1... | collective-permute-start | bytes 1081352 | tf_op jit(solution)/shard_map/ppermute | solution.py:541
  12.1 16.6 %collective-permute-start.4 = (f32[64,1024]{1,0:T(8,128)}, f32[64,1024]{1,0:T(8,128)S(1)}, u32[]{:S(2)}, u32[]{:S(2)}) collective-permute-start(f32[64,1024]{1,0:T(8,128)} %collective-permute-done.3.refs_6_), channel_id=1, source_target_pairs={{0,8},{8,16},{16,24},{12,4},{20,12},{28,20},{1,9},{9,17},{17,25},{... | collective-permute-start | bytes 786440 | tf_op jit(solution)/shard_map/ppermute | solution.py:545
  15.9 20.0 %collective-permute-start.10 = (f32[128,1024]{1,0:T(8,128)}, f32[128,1024]{1,0:T(8,128)S(1)}, u32[]{:S(2)}, u32[]{:S(2)}) collective-permute-start(f32[128,1024]{1,0:T(8,128)} %get-tuple-element.61), channel_id=1, source_target_pairs={{0,4},{4,0},{8,12},{12,8},{16,20},{20,16},{24,28},{28,24},{1,5},{5... | collective-permute-start | bytes 1572872 | tf_op jit(solution)/shard_map/ppermute | solution.py:538
  28.7 30.3 %collective-permute-start.9 = (f32[128,1024]{1,0:T(8,128)}, f32[128,1024]{1,0:T(8,128)S(1)}, u32[]{:S(2)}, u32[]{:S(2)}) collective-permute-start(f32[128,1024]{1,0:T(8,128)} %collective-permute-done.8.refs_7_), channel_id=1, source_target_pairs={{0,8},{8,16},{16,24},{12,4},{20,12},{28,20},{1,9},{9,17},{17,25},{... | collective-permute-start | bytes 1572872 | tf_op jit(solution)/shard_map/ppermute | solution.py:547
  34.6 9.8 %copy-start.2 = (f32[88,1024]{1,0:T(8,128)S(1)}, f32[88,1024]{1,0:T(8,128)}, u32[]{:S(2)}) copy-start(f32[88,1024]{1,0:T(8,128)} %get-tuple-element.33.refs_0_) | copy-start | bytes 1081348
  34.6 9.8 %copy-start.5 = (f32[64,1024]{1,0:T(8,128)S(1)}, f32[64,1024]{1,0:T(8,128)}, u32[]{:S(2)}) copy-start(f32[64,1024]{1,0:T(8,128)} %refs_6_.1) | copy-start | bytes 786436
  35.9 28.2 %collective-permute-start.12 = (f32[128,1024]{1,0:T(8,128)S(1)}, f32[128,1024]{1,0:T(8,128)S(1)}, u32[]{:S(2)}, u32[]{:S(2)}) collective-permute-start(f32[128,1024]{1,0:T(8,128)S(1)} %collective-permute-done.10.refs_8_), channel_id=1, source_target_pairs={{0,8},{8,16},{16,24},{12,4},{20,12},{28,20},{1,9},{9,17},{17,25},{... | collective-permute-start | bytes 1572872 | tf_op jit(solution)/shard_map/ppermute | solution.py:557
  39.4 21.0 %collective-permute-start.5 = (f32[128,256]{1,0:T(8,128)S(1)}, f32[128,256]{1,0:T(8,128)S(1)}, u32[]{:S(2)}, u32[]{:S(2)}) collective-permute-start(f32[128,256]{1,0:T(8,128)S(1)} %get-tuple-element.49.refs_0_), channel_id=1, source_target_pairs={{0,8},{4,12},{8,0},{12,4},{16,24},{20,28},{24,16},{28,20},{1,9},{5... | collective-permute-start | bytes 393224 | tf_op jit(solution)/shard_map/ppermute | solution.py:552
  41.0 20.6 %collective-permute-start.6 = (f32[128,256]{1,0:T(8,128)S(1)}, f32[128,256]{1,0:T(8,128)S(1)}, u32[]{:S(2)}, u32[]{:S(2)}) collective-permute-start(f32[128,256]{1,0:T(8,128)S(1)} %get-tuple-element.49.refs_0_), channel_id=1, source_target_pairs={{0,16},{4,20},{8,24},{12,28},{16,0},{20,4},{24,8},{28,12},{1,17},{... | collective-permute-start | bytes 393224 | tf_op jit(solution)/shard_map/ppermute | solution.py:552
  41.0 23.1 %collective-permute-start.7 = (f32[128,256]{1,0:T(8,128)S(1)}, f32[128,256]{1,0:T(8,128)S(1)}, u32[]{:S(2)}, u32[]{:S(2)}) collective-permute-start(f32[128,256]{1,0:T(8,128)S(1)} %get-tuple-element.49.refs_0_), channel_id=1, source_target_pairs={{0,24},{4,28},{8,16},{12,20},{16,8},{20,12},{24,0},{28,4},{1,25},{... | collective-permute-start | bytes 393224 | tf_op jit(solution)/shard_map/ppermute | solution.py:552
  60.4 11.7 %collective-permute-start.16 = (f32[128,1024]{1,0:T(8,128)S(1)}, f32[128,1024]{1,0:T(8,128)S(1)}, u32[]{:S(2)}, u32[]{:S(2)}) collective-permute-start(f32[128,1024]{1,0:T(8,128)S(1)} %get-tuple-element.48), channel_id=1, source_target_pairs={{1,0},{0,1},{3,2},{2,3},{5,4},{4,5},{7,6},{6,7},{9,8},{8,9},{11,10... | collective-permute-start | bytes 1572872 | tf_op jit(solution)/shard_map/ppermute | solution.py:523
  65.7 9.6 %collective-permute-start.13 = (f32[128,1024]{1,0:T(8,128)S(1)}, f32[128,1024]{1,0:T(8,128)S(1)}, u32[]{:S(2)}, u32[]{:S(2)}) collective-permute-start(f32[128,1024]{1,0:T(8,128)S(1)} %get-tuple-element.54), channel_id=1, source_target_pairs={{1,0},{0,1},{3,2},{2,3},{5,4},{4,5},{7,6},{6,7},{9,8},{8,9},{11,10... | collective-permute-start | bytes 1572872 | tf_op jit(solution)/shard_map/ppermute | solution.py:523
  65.8 18.4 %collective-permute-start.11 = (f32[4,128,256]{2,1,0:T(8,128)S(1)}, f32[4,128,256]{2,1,0:T(8,128)S(1)}, u32[]{:S(2)}, u32[]{:S(2)}) collective-permute-start(f32[4,128,256]{2,1,0:T(8,128)S(1)} %stack.18.refs_11_.alike_ref), channel_id=1, source_target_pairs={{0,4},{4,0},{8,12},{12,8},{16,20},{20,16},{24,28},{28,24},{1,5},{5... | collective-permute-start | bytes 1572872 | tf_op jit(solution)/shard_map/ppermute | solution.py:566
  72.1 23.3 %collective-permute-start.17 = (f32[128,1024]{1,0:T(8,128)S(1)}, f32[128,1024]{1,0:T(8,128)S(1)}, u32[]{:S(2)}, u32[]{:S(2)}) collective-permute-start(f32[128,1024]{1,0:T(8,128)S(1)} %add_parts.4), channel_id=1, source_target_pairs={{2,0},{3,1},{0,2},{1,3},{6,4},{7,5},{4,6},{5,7},{10,8},{11,9},{8,1... | collective-permute-start | bytes 1572872 | tf_op jit(solution)/shard_map/ppermute | solution.py:526
  75.4 23.9 %collective-permute-start.18 = (f32[128,1024]{1,0:T(8,128)S(1)}, f32[128,1024]{1,0:T(8,128)S(1)}, u32[]{:S(2)}, u32[]{:S(2)}) collective-permute-start(f32[128,1024]{1,0:T(8,128)S(1)} %add_parts.3.refs_14_), channel_id=1, source_target_pairs={{2,0},{3,1},{0,2},{1,3},{6,4},{7,5},{4,6},{5,7},{10,8},{11,9},{8,1... | collective-permute-start | bytes 1572872 | tf_op jit(solution)/shard_map/ppermute | solution.py:526
  81.6 19.8 %collective-permute-start.19 = (f32[128,1024]{1,0:T(8,128)S(1)}, f32[128,1024]{1,0:T(8,128)S(1)}, u32[]{:S(2)}, u32[]{:S(2)}) collective-permute-start(f32[128,1024]{1,0:T(8,128)S(1)} %get-tuple-element.59), channel_id=1, source_target_pairs={{1,0},{0,1},{3,2},{2,3},{5,4},{4,5},{7,6},{6,7},{9,8},{8,9},{11,10... | collective-permute-start | bytes 1572872 | tf_op jit(solution)/shard_map/ppermute | solution.py:523
  81.7 19.7 %collective-permute-start.20 = (f32[128,1024]{1,0:T(8,128)S(1)}, f32[128,1024]{1,0:T(8,128)S(1)}, u32[]{:S(2)}, u32[]{:S(2)}) collective-permute-start(f32[128,1024]{1,0:T(8,128)S(1)} %get-tuple-element.60), channel_id=1, source_target_pairs={{1,0},{0,1},{3,2},{2,3},{5,4},{4,5},{7,6},{6,7},{9,8},{8,9},{11,10... | collective-permute-start | bytes 1572872 | tf_op jit(solution)/shard_map/ppermute | solution.py:523
  84.3 17.2 %copy-start.3 = (f32[2,512,256]{2,1,0:T(8,128)S(1)}, f32[2,512,256]{2,1,0:T(8,128)}, u32[]{:S(2)}) copy-start(f32[2,512,256]{2,1,0:T(8,128)} %interp_ref.1) | copy-start | bytes 3145732
  90.8 1.3 %collective-permute-start.14 = (f32[64,256]{1,0:T(8,128)S(1)}, f32[64,256]{1,0:T(8,128)S(1)}, u32[]{:S(2)}, u32[]{:S(2)}) collective-permute-start(f32[64,256]{1,0:T(8,128)S(1)} %far.1.refs_0_), channel_id=1, source_target_pairs={{1,0},{0,1},{3,2},{2,3},{5,4},{4,5},{7,6},{6,7},{9,8},{8,9},{11,10... | collective-permute-start | bytes 196616 | tf_op jit(solution)/shard_map/ppermute | solution.py:523
  92.1 9.3 %collective-permute-start.15 = (f32[2,64,256]{2,1,0:T(8,128)S(1)}, f32[2,64,256]{2,1,0:T(8,128)S(1)}, u32[]{:S(2)}, u32[]{:S(2)}) collective-permute-start(f32[2,64,256]{2,1,0:T(8,128)S(1)} %stack.19.refs_0_), channel_id=1, source_target_pairs={{2,0},{3,1},{0,2},{1,3},{6,4},{7,5},{4,6},{5,7},{10,8},{11,9},{8,1... | collective-permute-start | bytes 393224 | tf_op jit(solution)/shard_map/ppermute | solution.py:523
  (8 other events, 48.4 us)

commit v3 on v2

--- a/solution.py
+++ b/solution.py
@@ -61,7 +61,7 @@
 
 
 def near_body(
-    xs, sets, leaves_at, rows, row, nacc, nout, pos_ref, *refs
+    xs, sets, leaves_at, rows, row, nacc, nout, *refs
 ):
     nset = len(sets)
     start, stop = leaves_at
@@ -106,7 +106,8 @@
         else:
             o_scr[t - start] = jnp.zeros((rows, LEAF), F32)
 
-    x, core, group, leaves = pos_ref[0], pos_ref[1], pos_ref[2], pos_ref[3]
+    x, core, group = place()
+    leaves = 4 * xs
     odd = group % 2
     column = []
     for kind, _, _ in sets:
@@ -178,11 +179,10 @@
             t, top = (t, top + tall) if top + tall < rows else (t + 2, 0)
 
 
-def near_call(name, pos, msgs, targets, leaves_at, sources, rows, row=0, acc=(), after=()):
+def near_call(name, msgs, targets, leaves_at, sources, rows, row=0, acc=(), after=()):
     nset = len(sources)
     start, stop = leaves_at
     vmem = pl.BlockSpec(memory_space=pltpu.VMEM)
-    smem = pl.BlockSpec(memory_space=pltpu.SMEM)
     operands = [a for _, heads, chunks in sources for a in (*heads, *chunks)]
     scratch = [
         pltpu.VMEM((2 * nset, LEAF, 4 * F), BF),
@@ -209,14 +209,13 @@
         ),
         name=name,
         out_shape=out,
-        in_specs=[smem]
-        + [pl.BlockSpec(memory_space=pl.ANY)] * len(msgs)
+        in_specs=[pl.BlockSpec(memory_space=pl.ANY)] * len(msgs)
         + [vmem] * (2 + len(operands))
         + [pl.BlockSpec(memory_space=pl.ANY)] * len(after),
         out_specs=[vmem] * len(out),
         scratch_shapes=scratch,
         compiler_params=pltpu.CompilerParams(vmem_limit_bytes=VMEM_LIMIT),
-    )(pos, *msgs, *targets, *operands, *after)
+    )(*msgs, *targets, *operands, *after)
 
 
 def source_body(pts_ref, side_ref, off_ref):
@@ -242,11 +241,16 @@
     )(pts)
 
 
+def place():
+    helper = lax.axis_index("help")
+    return helper // 2, helper % 2, lax.axis_index("leaf")
+
+
 def share_rows(xs):
     return R // (2 * xs) * SK // (2 * LEAF)
 
 
-def leaf_body(xs, pos_ref, count_ref, src_ref, pts_in, w_in, interp_in, *refs):
+def leaf_body(xs, count_ref, src_ref, pts_in, w_in, interp_in, *refs):
     msgs = refs[: 2 * xs]
     pts_ref, w_ref, interp_ref, scr, sems = refs[2 * xs :]
     copies = [
@@ -256,7 +260,8 @@
     ]
     for copy in copies:
         copy.start()
-    x, core, group, leaves = pos_ref[0], pos_ref[1], pos_ref[2], pos_ref[3]
+    x, core, group = place()
+    leaves = 4 * xs
     lane = lax.broadcasted_iota(jnp.int32, (1, 128), 1) + (group - 1) * leaves
     times = []
     for leaf in range(2):
@@ -284,7 +289,7 @@
             msg[F + EXTRA :, i * SK : (i + 1) * SK] = scr[pl.ds(at, tall), :]
 
 
-def leaf_call(xs, pos, near_count, near_src, points, weights, interp):
+def leaf_call(xs, near_count, near_src, points, weights, interp):
     vmem = pl.BlockSpec(memory_space=pltpu.VMEM)
     smem = pl.BlockSpec(memory_space=pltpu.SMEM)
     anywhere = pl.BlockSpec(memory_space=pl.ANY)
@@ -293,7 +298,7 @@
         partial(leaf_body, xs),
         name="leaf_up",
         out_shape=[jax.ShapeDtypeStruct((height, 2 * LEAF), F32)] * (2 * xs),
-        in_specs=[smem, smem, smem, anywhere, anywhere, anywhere],
+        in_specs=[smem, smem, anywhere, anywhere, anywhere],
         out_specs=[vmem] * (2 * xs),
         scratch_shapes=[
             pltpu.VMEM(points.shape, F32),
@@ -303,17 +308,17 @@
             pltpu.SemaphoreType.DMA((3,)),
         ],
         compiler_params=pltpu.CompilerParams(vmem_limit_bytes=VMEM_WHOLE),
-    )(pos, near_count, near_src, points, weights, interp)
-
-
-def skel_body(xs, pos_ref, index_ref, *refs):
+    )(near_count, near_src, points, weights, interp)
+
+
+def skel_body(xs, index_ref, *refs):
     msgs, (out_ref, side_ref, off_ref) = refs[:-3], refs[-3:]
     rows = R // (2 * xs)
     tall = share_rows(xs)
     total = jnp.zeros((2 * F, SK), F32)
     value = jnp.zeros((tall, 2 * LEAF), F32)
     spot = lax.broadcasted_iota(jnp.int32, (2 * LEAF, SK), 0)
-    x, core = pos_ref[0], pos_ref[1]
+    x, core, _ = place()
     for b, msg in enumerate(msgs):
         helper = 2 * lax.rem(x + b // 2, xs) + (core if b % 2 == 0 else 1 - core)
         side, off = target_side(msg[:F, :] * SCALE)
@@ -329,7 +334,7 @@
         out_ref[F + i * tall : F + (i + 1) * tall, :] = value[:, i * SK : (i + 1) * SK]
 
 
-def skel_call(xs, pos, index, msgs):
+def skel_call(xs, index, msgs):
     rows = R // (2 * xs)
     leaves = 2 * len(msgs)
     vmem = pl.BlockSpec(memory_space=pltpu.VMEM)
@@ -341,13 +346,13 @@
             jax.ShapeDtypeStruct((leaves, 4 * F, LEAF), BF),
             jax.ShapeDtypeStruct((leaves, 8, LEAF), F32),
         ],
-        in_specs=[pl.BlockSpec(memory_space=pltpu.SMEM)] + [vmem] * (1 + len(msgs)),
+        in_specs=[vmem] * (1 + len(msgs)),
         out_specs=[vmem] * 3,
         compiler_params=pltpu.CompilerParams(vmem_limit_bytes=VMEM_LIMIT),
         cost_estimate=pl.CostEstimate(
             flops=5_000_000_000, bytes_accessed=8_000_000, transcendentals=0
         ),
-    )(pos, index, *msgs)
+    )(index, *msgs)
     return payload, targets
 
 
@@ -376,10 +381,10 @@
     return sum((groups >> step for step in range(level)))
 
 
-def far_body(groups, rows, pos_ref, far_ref, node_ref, transfer_ref, alike_ref, beside_ref, *refs):
+def far_body(groups, rows, far_ref, node_ref, transfer_ref, alike_ref, beside_ref, *refs):
     out_ref, p_scr, u_scr, f_scr = refs[-4:]
     levels = groups.bit_length() - 1
-    group = pos_ref[2]
+    group = place()[2]
     start = [list_start(level, groups) for level in range(levels)]
     for n in range(groups // 2):
         same, other = group ^ (2 * n), group ^ (2 * n + 1)
@@ -427,7 +432,7 @@
     out_ref[...] = local
 
 
-def far_call(groups, pos, far_nodes, skel_node, transfer, alike, beside, after):
+def far_call(groups, far_nodes, skel_node, transfer, alike, beside, after):
     rows = alike.shape[1] - F
     vmem = pl.BlockSpec(memory_space=pltpu.VMEM)
     smem = pl.BlockSpec(memory_space=pltpu.SMEM)
@@ -436,7 +441,7 @@
         partial(far_body, groups, rows),
         name="far",
         out_shape=jax.ShapeDtypeStruct((rows, SK), F32),
-        in_specs=[smem, smem, vmem, vmem, vmem, vmem]
+        in_specs=[smem, vmem, vmem, vmem, vmem]
         + [pl.BlockSpec(memory_space=pl.ANY)] * len(after),
         out_specs=vmem,
         scratch_shapes=[
@@ -445,14 +450,14 @@
             pltpu.VMEM((groups.bit_length(), rows, SK), F32),
         ],
         compiler_params=pltpu.CompilerParams(vmem_limit_bytes=VMEM_LIMIT),
-    )(pos, far_nodes.T, skel_node, transfer, alike, beside, *after)
-
-
-def final_body(xs, pos_ref, interp_ref, *refs):
+    )(far_nodes.T, skel_node, transfer, alike, beside, *after)
+
+
+def final_body(xs, interp_ref, *refs):
     values, sums = refs[:xs], refs[xs:-2]
     out_ref, v_scr = refs[-2:]
     rows = R // (2 * xs)
-    x, core = pos_ref[0], pos_ref[1]
+    x, core, _ = place()
     for dx, ref in enumerate(values):
         for dc in range(2):
             helper = 2 * lax.rem(x + dx, xs) + (core if dc == 0 else 1 - core)
@@ -487,17 +492,17 @@
     )(*operands)
 
 
-def final_call(xs, pos, interp, home, mate, values):
+def final_call(xs, interp, home, mate, values):
     vmem = pl.BlockSpec(memory_space=pltpu.VMEM)
     return pl.pallas_call(
         partial(final_body, xs),
         name="join",
         out_shape=jax.ShapeDtypeStruct((R, 2 * LEAF), F32),
-        in_specs=[pl.BlockSpec(memory_space=pltpu.SMEM)] + [vmem] * (1 + xs + 4),
+        in_specs=[vmem] * (1 + xs + 4),
         out_specs=vmem,
         scratch_shapes=[pltpu.VMEM((R, SK), F32)],
         compiler_params=pltpu.CompilerParams(vmem_limit_bytes=VMEM_LIMIT),
-    )(pos, interp, *values, *home, *mate)
+    )(interp, *values, *home, *mate)
 
 
 def help_pairs(xs, dx, dc):
@@ -512,13 +517,6 @@
     helpers = lax.axis_size("help")
     groups = lax.axis_size("leaf")
     xs = helpers // 2
-    helper = lax.axis_index("help")
-    group = lax.axis_index("leaf")
-    x, core = helper // 2, helper % 2
-    leaves = 2 * helpers
-    pos = jnp.stack([x, core, group, jnp.int32(leaves)]).astype(jnp.int32)
-    rows = R // 2
-
     def from_help(value, dx, dc):
         return lax.ppermute(value, "help", help_pairs(xs, dx, dc))
 
@@ -536,27 +534,27 @@
     cut = SIZES[0]
     pts_y = lax.ppermute(points, "leaf", beside)
     w_y = [lax.ppermute(chunk, "leaf", beside) for chunk in (weights[:cut], weights[cut:])]
-    sent = leaf_call(xs, pos, near_count, near_src, points, weights, interp)
+    sent = leaf_call(xs, near_count, near_src, points, weights, interp)
     got = [
         lax.ppermute(sent[n], "help", help_pairs(xs, -dx, dc))
         for n, (dx, dc) in enumerate(order)
         if n
     ]
     pts_z = lax.ppermute(pts_y, "leaf", across)
-    got, pts_z = together(got, pts_z)
+    pts_z, w_y[0] = together(pts_z, w_y[0])
     w_z = [lax.ppermute(w_y[0], "leaf", across)]
     msgs = [sent[0]] + [got[order.index((-dx % xs, dc)) - 1] for dx, dc in order[1:]]
-    payload, targets = skel_call(xs, pos, skel_group, msgs)
+    payload, targets = skel_call(xs, skel_group, msgs)
     pieces = [payload]
     for mask in range(2, groups, 2):
         pieces.append(lax.ppermute(payload, "leaf", [(i, i ^ mask) for i in range(groups)]))
 
     payload, w_y[1] = together(payload, w_y[1])
     every, away, home = (0, 2 * helpers), (4, 2 * helpers), (0, 4)
-    (own,) = near_call("near_own", pos, msgs, targets, every, [("own", (points,), [weights])], R)
+    (own,) = near_call("near_own", msgs, targets, every, [("own", (points,), [weights])], R)
     w_z.append(lax.ppermute(w_y[1], "leaf", across))
     pair_src = ("pair", (pts_y,), w_y)
-    (pair,) = near_call("near_pair", pos, msgs, targets, away, [pair_src], R, after=[own])
+    (pair,) = near_call("near_pair", msgs, targets, away, [pair_src], R, after=[own])
     z_side = source_call(pts_z)
     sums, part = [], [pair]
     for c in range(2):
@@ -566,7 +564,7 @@
             side = lax.ppermute(alike, "leaf", beside)
             part = [alike]
         part = near_call(
-            "near_next_away", pos, msgs, targets, away, [("next", z_side, w_z[c : c + 1])],
+            "near_next_away", msgs, targets, away, [("next", z_side, w_z[c : c + 1])],
             SIZES[c], c * SIZES[0], [own, pair], part[:1],
         )
         kept, given = part[::2], part[1::2]
@@ -577,13 +575,13 @@
         both = add_call(*zip(kept, mates))
         parts.append([to_help(value, dx + 1) for dx, value in enumerate(both)])
     sources = [pair_src, ("next", z_side, w_z)]
-    home = near_call("near_home", pos, msgs, targets, home, sources, R, 0, [own], both[:1])
-    v_own = far_call(groups, pos, far_nodes, skel_node, transfer, alike, side, home[:1])
+    home = near_call("near_home", msgs, targets, home, sources, R, 0, [own], both[:1])
+    v_own = far_call(groups, far_nodes, skel_node, transfer, alike, side, home[:1])
     v_pair = stack_call([v_own, from_help(v_own, 0, 1)])
     values = [v_pair] + [from_help(v_pair, dx, 0) for dx in range(1, xs)]
     mate = [from_help(value, 0, 1) for value in home[2:]]
     mine = add_call(*[[home[c], *parts[c]] for c in range(2)])
-    return final_call(xs, pos, interp, mine, mate, values)
+    return final_call(xs, interp, mine, mate, values)
 
 
 def solution(mesh):

time: 104 us -> 97.8 us (0.940)
  waiting for transfers between devices: 25.6 us -> 22.4 us
  starting transfers between devices: 34.2 us -> 31.8 us
    ppermute x3, waiting for transfers between devices: 12.8 us -> 0.65 us  [shards(): lax.ppermute(sent[n], 'help', help_pairs(xs, -dx, dc))]
    ppermute x1, waiting for transfers between devices: 0.01 us -> 6.36 us  [shards(): pts_z = lax.ppermute(pts_y, 'leaf', across)]
    ppermute x2, waiting for transfers between devices: 0.01 us -> 5.21 us  [shards(): lax.ppermute(chunk, 'leaf', beside)]
    ppermute x3, waiting for transfers between devices: 3.69 us -> 0.01 us  [shards(): lax.ppermute(payload, 'leaf', [(i, i ^ mask) for i in range(groups)])]
    ppermute x2, starting transfers between devices: 0.07 us -> 2.32 us  [shards(): lax.ppermute(chunk, 'leaf', beside)]
    ppermute x6, starting transfers between devices: 4.12 us -> 2.27 us  [from_help(): return lax.ppermute(value, 'help', help_pairs(xs, dx, dc))]
    pallas_call x5, Pallas kernels: 23.5 us -> 25.3 us  [near_call(): pl.pallas_call(partial(near_body, len(msgs) // 2, sets, leaves_at, rows,...]
    ppermute x1, starting transfers between devices: 6.28 us -> 4.48 us  [shards(): side = lax.ppermute(alike, 'leaf', beside)]
  transfers between devices with their start and end apart: 21 -> 21, of which waited for: 8 -> 7; matrix products, arithmetic and copies ran while one was open for 3% -> 2% of each run, Pallas kernels for 35% -> 38%
where the time goes in v3:
time: 97.8 us; the launch traced here: 97.3 us
  Pallas kernels  38.9 us (40%)
  starting transfers between devices  31.8 us (33%)
  waiting for transfers between devices  22.4 us (23%)
  local copies, waits for them, and re-layouts  3.99 us (4%)
    pallas_call x5, Pallas kernels, near_call(): pl.pallas_call(partial(near_body, len(msgs) // 2, sets, leaves_at, rows,...  25.3 us
    pallas_call x1, Pallas kernels, far_call(): pl.pallas_call(partial(far_body, groups, rows), name='far', out_shape=jax...  6.39 us
    ppermute x1, waiting for transfers between devices, shards(): pts_z = lax.ppermute(pts_y, 'leaf', across)  6.36 us
    ppermute x2, waiting for transfers between devices, shards(): lax.ppermute(chunk, 'leaf', beside)  5.21 us
    ppermute x2, waiting for transfers between devices, to_help(): return lax.ppermute(value, 'help', help_pairs(xs, -dx, 0))  4.84 us
    ppermute x1, starting transfers between devices, shards(): side = lax.ppermute(alike, 'leaf', beside)  4.48 us
    ppermute x3, starting transfers between devices, shards(): lax.ppermute(payload, 'leaf', [(i, i ^ mask) for i in range(groups)])  4.45 us
    pallas_call x1, Pallas kernels, leaf_call(): pl.pallas_call(partial(leaf_body, xs), name='leaf_up', out_shape=[jax.Sha...  4.06 us
  transfers between devices with their start and end apart: 21, of which 7 were waited for; matrix products, arithmetic and copies ran while one was open for 2% of the time, Pallas kernels for 38%

profile of v3, /device:TPU:0, one launch (start us, length us, event | category | flops | bytes accessed | tf_op | source)
XLA Modules:
  0.0 97.3 jit_solution(9683909388317482289)
XLA Ops:
  0.0 3.0 %collective-permute-start.6 = (f32[64,1024]{1,0:T(8,128)}, f32[64,1024]{1,0:T(8,128)}, u32[]{:S(2)}, u32[]{:S(2)}) collective-permute-start(f32[64,1024]{1,0:T(8,128)} %refs_6_.1), channel_id=1, source_target_pairs={{0,4},{4,0},{8,12},{12,8},{16,20},{20,16},{24,28},{28,24},{1,5},{5... | collective-permute-start | bytes 786440 | tf_op jit(solution)/shard_map/ppermute | solution.py:535
  3.0 2.3 %fusion = (f32[128,1024]{1,0:T(8,128)}, f32[128,1024]{1,0:T(8,128)}) fusion(f32[256,1024]{1,0:T(8,128)} %refs_7_.1), kind=kLoop, calls=%fused_computation | loop fusion | bytes 2097152 | tf_op jit(solution)/shard_map/slice | solution.py:536
  5.3 4.1 %leaf_up.1 = (f32[88,1024]{1,0:T(8,128)}, f32[88,1024]{1,0:T(8,128)}, f32[88,1024]{1,0:T(8,128)}, f32[88,1024]{1,0:T(8,128)}) custom-call(s32[1,2]{1,0:T(1,128)} %count_ref.1, s32[2,32]{1,0:T(2,128)} %src_ref.1, f32[64,1024]{1,0:T(8,128)} %refs_6_.1, f32[256,1024]{1,0:T(8,128)} %refs_7_.1, f32[2,512,256]{2,1,0:T(8,128)} %interp_ref.1), custom_call_target="tpu_custom_call" | custom-call | tf_op jit(solution)/shard_map/leaf_up/pallas_call | solution.py:297
  9.4 2.1 %collective-permute-start.1 = (f32[88,1024]{1,0:T(8,128)}, f32[88,1024]{1,0:T(8,128)S(1)}, u32[]{:S(2)}, u32[]{:S(2)}) collective-permute-start(f32[88,1024]{1,0:T(8,128)} %get-tuple-element.33), channel_id=1, source_target_pairs={{2,0},{3,1},{0,2},{1,3},{6,4},{7,5},{4,6},{5,7},{10,8},{11,9},{8,1... | collective-permute-start | bytes 1081352 | tf_op jit(solution)/shard_map/ppermute | solution.py:539
  11.5 3.7 %collective-permute-start.7 = (f32[64,1024]{1,0:T(8,128)}, f32[64,1024]{1,0:T(8,128)S(1)}, u32[]{:S(2)}, u32[]{:S(2)}) collective-permute-start(f32[64,1024]{1,0:T(8,128)} %collective-permute-done.6.refs_6_), channel_id=1, source_target_pairs={{0,8},{8,16},{16,24},{12,4},{20,12},{28,20},{1,9},{9,17},{17,25},{... | collective-permute-start | bytes 786440 | tf_op jit(solution)/shard_map/ppermute | solution.py:543
  15.3 6.4 %collective-permute-done.7.pts_ref = f32[64,1024]{1,0:T(8,128)S(1)} collective-permute-done((f32[64,1024]{1,0:T(8,128)}, f32[64,1024]{1,0:T(8,128)S(1)}, u32[]{:S(2)}, u32[]{:S(2)}) %collective-permute-start.7) | collective-permute-done | bytes 262176 | tf_op jit(solution)/shard_map/ppermute | solution.py:543
  21.6 2.3 %collective-permute-start.10 = (f32[128,1024]{1,0:T(8,128)}, f32[128,1024]{1,0:T(8,128)S(1)}, u32[]{:S(2)}, u32[]{:S(2)}) collective-permute-start(f32[128,1024]{1,0:T(8,128)} %get-tuple-element.57), channel_id=1, source_target_pairs={{0,4},{4,0},{8,12},{12,8},{16,20},{20,16},{24,28},{28,24},{1,5},{5... | collective-permute-start | bytes 1572872 | tf_op jit(solution)/shard_map/ppermute | solution.py:536
  23.9 3.5 %collective-permute-start.9 = (f32[128,1024]{1,0:T(8,128)}, f32[128,1024]{1,0:T(8,128)S(1)}, u32[]{:S(2)}, u32[]{:S(2)}) collective-permute-start(f32[128,1024]{1,0:T(8,128)} %collective-permute-done.8.refs_7_), channel_id=1, source_target_pairs={{0,8},{8,16},{16,24},{12,4},{20,12},{28,20},{1,9},{9,17},{17,25},{... | collective-permute-start | bytes 1572872 | tf_op jit(solution)/shard_map/ppermute | solution.py:545
  30.6 5.2 %collective-permute-done.10.refs_8_ = f32[128,1024]{1,0:T(8,128)S(1)} collective-permute-done((f32[128,1024]{1,0:T(8,128)}, f32[128,1024]{1,0:T(8,128)S(1)}, u32[]{:S(2)}, u32[]{:S(2)}) %collective-permute-start.10) | collective-permute-done | bytes 524320 | tf_op jit(solution)/shard_map/ppermute | solution.py:536
  35.8 3.7 %collective-permute-start.12 = (f32[128,1024]{1,0:T(8,128)S(1)}, f32[128,1024]{1,0:T(8,128)S(1)}, u32[]{:S(2)}, u32[]{:S(2)}) collective-permute-start(f32[128,1024]{1,0:T(8,128)S(1)} %collective-permute-done.10.refs_8_), channel_id=1, source_target_pairs={{0,8},{8,16},{16,24},{12,4},{20,12},{28,20},{1,9},{9,17},{17,25},{... | collective-permute-start | bytes 1572872 | tf_op jit(solution)/shard_map/ppermute | solution.py:555
  39.5 1.6 %collective-permute-start.3 = (f32[128,256]{1,0:T(8,128)S(1)}, f32[128,256]{1,0:T(8,128)S(1)}, u32[]{:S(2)}, u32[]{:S(2)}) collective-permute-start(f32[128,256]{1,0:T(8,128)S(1)} %get-tuple-element.45.refs_0_), channel_id=1, source_target_pairs={{0,8},{4,12},{8,0},{12,4},{16,24},{20,28},{24,16},{28,20},{1,9},{5... | collective-permute-start | bytes 393224 | tf_op jit(solution)/shard_map/ppermute | solution.py:550
  41.1 1.1 %collective-permute-start.4 = (f32[128,256]{1,0:T(8,128)S(1)}, f32[128,256]{1,0:T(8,128)S(1)}, u32[]{:S(2)}, u32[]{:S(2)}) collective-permute-start(f32[128,256]{1,0:T(8,128)S(1)} %get-tuple-element.45.refs_0_), channel_id=1, source_target_pairs={{0,16},{4,20},{8,24},{12,28},{16,0},{20,4},{24,8},{28,12},{1,17},{... | collective-permute-start | bytes 393224 | tf_op jit(solution)/shard_map/ppermute | solution.py:550
  42.2 1.7 %collective-permute-start.5 = (f32[128,256]{1,0:T(8,128)S(1)}, f32[128,256]{1,0:T(8,128)S(1)}, u32[]{:S(2)}, u32[]{:S(2)}) collective-permute-start(f32[128,256]{1,0:T(8,128)S(1)} %get-tuple-element.45.refs_0_), channel_id=1, source_target_pairs={{0,24},{4,28},{8,16},{12,20},{16,8},{20,12},{24,0},{28,4},{1,25},{... | collective-permute-start | bytes 393224 | tf_op jit(solution)/shard_map/ppermute | solution.py:550
  44.0 10.8 %near_own.1.refs_9_.refs_13_ = f32[8,256,512]{2,1,0:T(8,128)S(1)} custom-call(f32[88,1024]{1,0:T(8,128)S(1)} %copy-done.2, f32[88,1024]{1,0:T(8,128)S(1)} %collective-permute-done.refs_1_, f32[88,1024]{1,0:T(8,128)S(1)} %collective-permute-done.1.refs_2_, f32[88,1024]{1,0:T(8,128)S(1)} %collective-permute-done.2.refs_3_, ...), custom_call_target="tpu_custom_call" | custom-call | tf_op jit(solution)/shard_map/near_own/pallas_call | solution.py:206
  55.3 5.3 %near_pair.1.refs_10_.refs_11_ = f32[4,256,512]{2,1,0:T(8,128)S(1)} custom-call(f32[88,1024]{1,0:T(8,128)S(1)} %copy-done.2, f32[88,1024]{1,0:T(8,128)S(1)} %collective-permute-done.refs_1_, f32[88,1024]{1,0:T(8,128)S(1)} %collective-permute-done.1.refs_2_, f32[88,1024]{1,0:T(8,128)S(1)} %collective-permute-done.2.refs_3_, ...), custom_call_target="tpu_custom_call" | custom-call | tf_op jit(solution)/shard_map/near_pair/pallas_call | solution.py:206
  63.1 4.5 %collective-permute-start.11 = (f32[4,128,256]{2,1,0:T(8,128)S(1)}, f32[4,128,256]{2,1,0:T(8,128)S(1)}, u32[]{:S(2)}, u32[]{:S(2)}) collective-permute-start(f32[4,128,256]{2,1,0:T(8,128)S(1)} %stack.2.refs_11_.alike_ref), channel_id=1, source_target_pairs={{0,4},{4,0},{8,12},{12,8},{16,20},{20,16},{24,28},{28,24},{1,5},{5... | collective-permute-start | bytes 1572872 | tf_op jit(solution)/shard_map/ppermute | solution.py:564
  68.7 1.1 %collective-permute-start.18 = (f32[128,1024]{1,0:T(8,128)S(1)}, f32[128,1024]{1,0:T(8,128)S(1)}, u32[]{:S(2)}, u32[]{:S(2)}) collective-permute-start(f32[128,1024]{1,0:T(8,128)S(1)} %add_parts.3.refs_14_), channel_id=1, source_target_pairs={{2,0},{3,1},{0,2},{1,3},{6,4},{7,5},{4,6},{5,7},{10,8},{11,9},{8,1... | collective-permute-start | bytes 1572872 | tf_op jit(solution)/shard_map/ppermute | solution.py:524
  69.9 7.5 %near_home.1 = (f32[128,1024]{1,0:T(8,128)S(1)}, f32[128,1024]{1,0:T(8,128)S(1)}, f32[128,1024]{1,0:T(8,128)S(1)}, f32[128,1024]{1,0:T(8,128)S(1)}) custom-call(f32[88,1024]{1,0:T(8,128)S(1)} %copy-done.2, f32[88,1024]{1,0:T(8,128)S(1)} %collective-permute-done.refs_1_, f32[88,1024]{1,0:T(8,128)S(1)} %collective-permute-done.1.refs_2_, ...), custom_call_target="tpu_custom_call" | custom-call | tf_op jit(solution)/shard_map/near_home/pallas_call | solution.py:206
  78.0 2.1 %collective-permute-done.11.beside_ref = f32[4,128,256]{2,1,0:T(8,128)S(1)} collective-permute-done((f32[4,128,256]{2,1,0:T(8,128)S(1)}, f32[4,128,256]{2,1,0:T(8,128)S(1)}, u32[]{:S(2)}, u32[]{:S(2)}) %collective-permute-start.11) | collective-permute-done | bytes 524320 | tf_op jit(solution)/shard_map/ppermute | solution.py:564
  80.1 6.4 %far.1.refs_0_ = f32[64,256]{1,0:T(8,128)S(1)} custom-call(s32[4,14]{1,0:T(4,128)S(1)} %bitcast.1, s32[6,256]{1,0:T(8,128)S(1)} %copy-done.6, f32[6,512,256]{2,1,0:T(8,128)S(1)} %copy-done.4, f32[4,128,256]{2,1,0:T(8,128)S(1)} %stack.2.refs_11_.alike_ref, f32[4,128,256]{2,1,0:T(8,128)S(1)} %collective-permute-done.11.beside_ref, ...), custom_call_target="tpu_custom_call" | custom-call | tf_op jit(solution)/shard_map/far/pallas_call | solution.py:440
  86.6 1.2 %collective-permute-done.14.refs_1_ = f32[64,256]{1,0:T(8,128)S(1)} collective-permute-done((f32[64,256]{1,0:T(8,128)S(1)}, f32[64,256]{1,0:T(8,128)S(1)}, u32[]{:S(2)}, u32[]{:S(2)}) %collective-permute-start.14) | collective-permute-done | bytes 65568 | tf_op jit(solution)/shard_map/ppermute | solution.py:521
  88.9 4.8 %collective-permute-done.18.refs_3_ = f32[128,1024]{1,0:T(8,128)S(1)} collective-permute-done((f32[128,1024]{1,0:T(8,128)S(1)}, f32[128,1024]{1,0:T(8,128)S(1)}, u32[]{:S(2)}, u32[]{:S(2)}) %collective-permute-start.18) | collective-permute-done | bytes 524320 | tf_op jit(solution)/shard_map/ppermute | solution.py:524
  93.8 1.9 %collective-permute-done.15.refs_1_ = f32[2,64,256]{2,1,0:T(8,128)S(1)} collective-permute-done((f32[2,64,256]{2,1,0:T(8,128)S(1)}, f32[2,64,256]{2,1,0:T(8,128)S(1)}, u32[]{:S(2)}, u32[]{:S(2)}) %collective-permute-start.15) | collective-permute-done | bytes 131104 | tf_op jit(solution)/shard_map/ppermute | solution.py:521
  95.7 1.6 %join.1 = f32[256,1024]{1,0:T(8,128)} custom-call(f32[2,512,256]{2,1,0:T(8,128)S(1)} %copy-done.3, f32[2,64,256]{2,1,0:T(8,128)S(1)} %stack.3.refs_0_, f32[2,64,256]{2,1,0:T(8,128)S(1)} %collective-permute-done.15.refs_1_, f32[128,1024]{1,0:T(8,128)S(1)} %get-tuple-element.53.refs_2_, f32[128,1024]{1,0:T(8,128)S(1)} %get-tuple-element.54.refs_3_, ...), custom_call_target="tpu_custom_call" | custom-call | tf_op jit(solution)/shard_map/join/pallas_call | solution.py:497
  (52 shorter events, 9.2 us)
Async XLA Ops:
  0.0 11.5 %collective-permute-start.6 = (f32[64,1024]{1,0:T(8,128)}, f32[64,1024]{1,0:T(8,128)}, u32[]{:S(2)}, u32[]{:S(2)}) collective-permute-start(f32[64,1024]{1,0:T(8,128)} %refs_6_.1), channel_id=1, source_target_pairs={{0,4},{4,0},{8,12},{12,8},{16,20},{20,16},{24,28},{28,24},{1,5},{5... | collective-permute-start | bytes 786440 | tf_op jit(solution)/shard_map/ppermute | solution.py:535
  5.3 18.7 %collective-permute-start.8 = (f32[128,1024]{1,0:T(8,128)}, f32[128,1024]{1,0:T(8,128)}, u32[]{:S(2)}, u32[]{:S(2)}) collective-permute-start(f32[128,1024]{1,0:T(8,128)} %get-tuple-element.58), channel_id=1, source_target_pairs={{0,4},{4,0},{8,12},{12,8},{16,20},{20,16},{24,28},{28,24},{1,5},{5... | collective-permute-start | bytes 1572872 | tf_op jit(solution)/shard_map/ppermute | solution.py:536
  9.3 18.1 %collective-permute-start = (f32[88,1024]{1,0:T(8,128)}, f32[88,1024]{1,0:T(8,128)S(1)}, u32[]{:S(2)}, u32[]{:S(2)}) collective-permute-start(f32[88,1024]{1,0:T(8,128)} %get-tuple-element.32), channel_id=1, source_target_pairs={{1,0},{0,1},{3,2},{2,3},{5,4},{4,5},{7,6},{6,7},{9,8},{8,9},{11,10... | collective-permute-start | bytes 1081352 | tf_op jit(solution)/shard_map/ppermute | solution.py:539
  9.4 18.1 %collective-permute-start.1 = (f32[88,1024]{1,0:T(8,128)}, f32[88,1024]{1,0:T(8,128)S(1)}, u32[]{:S(2)}, u32[]{:S(2)}) collective-permute-start(f32[88,1024]{1,0:T(8,128)} %get-tuple-element.33), channel_id=1, source_target_pairs={{2,0},{3,1},{0,2},{1,3},{6,4},{7,5},{4,6},{5,7},{10,8},{11,9},{8,1... | collective-permute-start | bytes 1081352 | tf_op jit(solution)/shard_map/ppermute | solution.py:539
  11.5 16.7 %collective-permute-start.2 = (f32[88,1024]{1,0:T(8,128)}, f32[88,1024]{1,0:T(8,128)S(1)}, u32[]{:S(2)}, u32[]{:S(2)}) collective-permute-start(f32[88,1024]{1,0:T(8,128)} %get-tuple-element.34), channel_id=1, source_target_pairs={{3,0},{2,1},{1,2},{0,3},{7,4},{6,5},{5,6},{4,7},{11,8},{10,9},{9,1... | collective-permute-start | bytes 1081352 | tf_op jit(solution)/shard_map/ppermute | solution.py:539
  11.5 10.1 %collective-permute-start.7 = (f32[64,1024]{1,0:T(8,128)}, f32[64,1024]{1,0:T(8,128)S(1)}, u32[]{:S(2)}, u32[]{:S(2)}) collective-permute-start(f32[64,1024]{1,0:T(8,128)} %collective-permute-done.6.refs_6_), channel_id=1, source_target_pairs={{0,8},{8,16},{16,24},{12,4},{20,12},{28,20},{1,9},{9,17},{17,25},{... | collective-permute-start | bytes 786440 | tf_op jit(solution)/shard_map/ppermute | solution.py:543
  21.6 14.2 %collective-permute-start.10 = (f32[128,1024]{1,0:T(8,128)}, f32[128,1024]{1,0:T(8,128)S(1)}, u32[]{:S(2)}, u32[]{:S(2)}) collective-permute-start(f32[128,1024]{1,0:T(8,128)} %get-tuple-element.57), channel_id=1, source_target_pairs={{0,4},{4,0},{8,12},{12,8},{16,20},{20,16},{24,28},{28,24},{1,5},{5... | collective-permute-start | bytes 1572872 | tf_op jit(solution)/shard_map/ppermute | solution.py:536
  23.9 36.6 %collective-permute-start.9 = (f32[128,1024]{1,0:T(8,128)}, f32[128,1024]{1,0:T(8,128)S(1)}, u32[]{:S(2)}, u32[]{:S(2)}) collective-permute-start(f32[128,1024]{1,0:T(8,128)} %collective-permute-done.8.refs_7_), channel_id=1, source_target_pairs={{0,8},{8,16},{16,24},{12,4},{20,12},{28,20},{1,9},{9,17},{17,25},{... | collective-permute-start | bytes 1572872 | tf_op jit(solution)/shard_map/ppermute | solution.py:545
  29.8 14.2 %copy-start.2 = (f32[88,1024]{1,0:T(8,128)S(1)}, f32[88,1024]{1,0:T(8,128)}, u32[]{:S(2)}) copy-start(f32[88,1024]{1,0:T(8,128)} %get-tuple-element.31.refs_0_) | copy-start | bytes 1081348
  29.8 14.2 %copy-start.5 = (f32[64,1024]{1,0:T(8,128)S(1)}, f32[64,1024]{1,0:T(8,128)}, u32[]{:S(2)}) copy-start(f32[64,1024]{1,0:T(8,128)} %refs_6_.1) | copy-start | bytes 786436
  35.8 25.8 %collective-permute-start.12 = (f32[128,1024]{1,0:T(8,128)S(1)}, f32[128,1024]{1,0:T(8,128)S(1)}, u32[]{:S(2)}, u32[]{:S(2)}) collective-permute-start(f32[128,1024]{1,0:T(8,128)S(1)} %collective-permute-done.10.refs_8_), channel_id=1, source_target_pairs={{0,8},{8,16},{16,24},{12,4},{20,12},{28,20},{1,9},{9,17},{17,25},{... | collective-permute-start | bytes 1572872 | tf_op jit(solution)/shard_map/ppermute | solution.py:555
  39.5 22.0 %collective-permute-start.3 = (f32[128,256]{1,0:T(8,128)S(1)}, f32[128,256]{1,0:T(8,128)S(1)}, u32[]{:S(2)}, u32[]{:S(2)}) collective-permute-start(f32[128,256]{1,0:T(8,128)S(1)} %get-tuple-element.45.refs_0_), channel_id=1, source_target_pairs={{0,8},{4,12},{8,0},{12,4},{16,24},{20,28},{24,16},{28,20},{1,9},{5... | collective-permute-start | bytes 393224 | tf_op jit(solution)/shard_map/ppermute | solution.py:550
  41.1 20.4 %collective-permute-start.4 = (f32[128,256]{1,0:T(8,128)S(1)}, f32[128,256]{1,0:T(8,128)S(1)}, u32[]{:S(2)}, u32[]{:S(2)}) collective-permute-start(f32[128,256]{1,0:T(8,128)S(1)} %get-tuple-element.45.refs_0_), channel_id=1, source_target_pairs={{0,16},{4,20},{8,24},{12,28},{16,0},{20,4},{24,8},{28,12},{1,17},{... | collective-permute-start | bytes 393224 | tf_op jit(solution)/shard_map/ppermute | solution.py:550
  42.2 19.3 %collective-permute-start.5 = (f32[128,256]{1,0:T(8,128)S(1)}, f32[128,256]{1,0:T(8,128)S(1)}, u32[]{:S(2)}, u32[]{:S(2)}) collective-permute-start(f32[128,256]{1,0:T(8,128)S(1)} %get-tuple-element.45.refs_0_), channel_id=1, source_target_pairs={{0,24},{4,28},{8,16},{12,20},{16,8},{20,12},{24,0},{28,4},{1,25},{... | collective-permute-start | bytes 393224 | tf_op jit(solution)/shard_map/ppermute | solution.py:550
  61.4 6.2 %collective-permute-start.16 = (f32[128,1024]{1,0:T(8,128)S(1)}, f32[128,1024]{1,0:T(8,128)S(1)}, u32[]{:S(2)}, u32[]{:S(2)}) collective-permute-start(f32[128,1024]{1,0:T(8,128)S(1)} %get-tuple-element.44), channel_id=1, source_target_pairs={{1,0},{0,1},{3,2},{2,3},{5,4},{4,5},{7,6},{6,7},{9,8},{8,9},{11,10... | collective-permute-start | bytes 1572872 | tf_op jit(solution)/shard_map/ppermute | solution.py:521
  62.5 6.1 %collective-permute-start.13 = (f32[128,1024]{1,0:T(8,128)S(1)}, f32[128,1024]{1,0:T(8,128)S(1)}, u32[]{:S(2)}, u32[]{:S(2)}) collective-permute-start(f32[128,1024]{1,0:T(8,128)S(1)} %get-tuple-element.50), channel_id=1, source_target_pairs={{1,0},{0,1},{3,2},{2,3},{5,4},{4,5},{7,6},{6,7},{9,8},{8,9},{11,10... | collective-permute-start | bytes 1572872 | tf_op jit(solution)/shard_map/ppermute | solution.py:521
  63.1 17.0 %collective-permute-start.11 = (f32[4,128,256]{2,1,0:T(8,128)S(1)}, f32[4,128,256]{2,1,0:T(8,128)S(1)}, u32[]{:S(2)}, u32[]{:S(2)}) collective-permute-start(f32[4,128,256]{2,1,0:T(8,128)S(1)} %stack.2.refs_11_.alike_ref), channel_id=1, source_target_pairs={{0,4},{4,0},{8,12},{12,8},{16,20},{20,16},{24,28},{28,24},{1,5},{5... | collective-permute-start | bytes 1572872 | tf_op jit(solution)/shard_map/ppermute | solution.py:564
  67.6 21.2 %collective-permute-start.17 = (f32[128,1024]{1,0:T(8,128)S(1)}, f32[128,1024]{1,0:T(8,128)S(1)}, u32[]{:S(2)}, u32[]{:S(2)}) collective-permute-start(f32[128,1024]{1,0:T(8,128)S(1)} %add_parts.4), channel_id=1, source_target_pairs={{2,0},{3,1},{0,2},{1,3},{6,4},{7,5},{4,6},{5,7},{10,8},{11,9},{8,1... | collective-permute-start | bytes 1572872 | tf_op jit(solution)/shard_map/ppermute | solution.py:524
  68.7 25.0 %collective-permute-start.18 = (f32[128,1024]{1,0:T(8,128)S(1)}, f32[128,1024]{1,0:T(8,128)S(1)}, u32[]{:S(2)}, u32[]{:S(2)}) collective-permute-start(f32[128,1024]{1,0:T(8,128)S(1)} %add_parts.3.refs_14_), channel_id=1, source_target_pairs={{2,0},{3,1},{0,2},{1,3},{6,4},{7,5},{4,6},{5,7},{10,8},{11,9},{8,1... | collective-permute-start | bytes 1572872 | tf_op jit(solution)/shard_map/ppermute | solution.py:524
  77.4 18.4 %collective-permute-start.19 = (f32[128,1024]{1,0:T(8,128)S(1)}, f32[128,1024]{1,0:T(8,128)S(1)}, u32[]{:S(2)}, u32[]{:S(2)}) collective-permute-start(f32[128,1024]{1,0:T(8,128)S(1)} %get-tuple-element.55), channel_id=1, source_target_pairs={{1,0},{0,1},{3,2},{2,3},{5,4},{4,5},{7,6},{6,7},{9,8},{8,9},{11,10... | collective-permute-start | bytes 1572872 | tf_op jit(solution)/shard_map/ppermute | solution.py:521
  77.5 18.3 %collective-permute-start.20 = (f32[128,1024]{1,0:T(8,128)S(1)}, f32[128,1024]{1,0:T(8,128)S(1)}, u32[]{:S(2)}, u32[]{:S(2)}) collective-permute-start(f32[128,1024]{1,0:T(8,128)S(1)} %get-tuple-element.56), channel_id=1, source_target_pairs={{1,0},{0,1},{3,2},{2,3},{5,4},{4,5},{7,6},{6,7},{9,8},{8,9},{11,10... | collective-permute-start | bytes 1572872 | tf_op jit(solution)/shard_map/ppermute | solution.py:521
  80.1 15.6 %copy-start.3 = (f32[2,512,256]{2,1,0:T(8,128)S(1)}, f32[2,512,256]{2,1,0:T(8,128)}, u32[]{:S(2)}) copy-start(f32[2,512,256]{2,1,0:T(8,128)} %interp_ref.1) | copy-start | bytes 3145732
  86.5 1.3 %collective-permute-start.14 = (f32[64,256]{1,0:T(8,128)S(1)}, f32[64,256]{1,0:T(8,128)S(1)}, u32[]{:S(2)}, u32[]{:S(2)}) collective-permute-start(f32[64,256]{1,0:T(8,128)S(1)} %far.1.refs_0_), channel_id=1, source_target_pairs={{1,0},{0,1},{3,2},{2,3},{5,4},{4,5},{7,6},{6,7},{9,8},{8,9},{11,10... | collective-permute-start | bytes 196616 | tf_op jit(solution)/shard_map/ppermute | solution.py:521
  87.8 7.9 %collective-permute-start.15 = (f32[2,64,256]{2,1,0:T(8,128)S(1)}, f32[2,64,256]{2,1,0:T(8,128)S(1)}, u32[]{:S(2)}, u32[]{:S(2)}) collective-permute-start(f32[2,64,256]{2,1,0:T(8,128)S(1)} %stack.3.refs_0_), channel_id=1, source_target_pairs={{2,0},{3,1},{0,2},{1,3},{6,4},{7,5},{4,6},{5,7},{10,8},{11,9},{8,1... | collective-permute-start | bytes 393224 | tf_op jit(solution)/shard_map/ppermute | solution.py:521
  (6 other events, 50.0 us)

commit v4 on v3

--- a/solution.py
+++ b/solution.py
@@ -541,7 +541,7 @@
         if n
     ]
     pts_z = lax.ppermute(pts_y, "leaf", across)
-    pts_z, w_y[0] = together(pts_z, w_y[0])
+    pts_z, w_y[0], got[0] = together(pts_z, w_y[0], got[0])
     w_z = [lax.ppermute(w_y[0], "leaf", across)]
     msgs = [sent[0]] + [got[order.index((-dx % xs, dc)) - 1] for dx, dc in order[1:]]
     payload, targets = skel_call(xs, skel_group, msgs)

time: 97.8 us -> 95.4 us (0.975)
  Pallas kernels: 38.9 us -> 37 us
  waiting for transfers between devices: 22.4 us -> 21.4 us
    ppermute x2, waiting for transfers between devices: 5.21 us -> 1.4 us  [shards(): lax.ppermute(chunk, 'leaf', beside)]
    ppermute x2, starting transfers between devices: 2.32 us -> 0.07 us  [shards(): lax.ppermute(chunk, 'leaf', beside)]
    pallas_call x5, Pallas kernels: 25.3 us -> 23.4 us  [near_call(): pl.pallas_call(partial(near_body, len(msgs) // 2, sets, leaves_at, rows,...]
    ppermute x1, waiting for transfers between devices: 2.13 us -> 4.08 us  [shards(): side = lax.ppermute(alike, 'leaf', beside)]
    ppermute x1, starting transfers between devices: 4.48 us -> 6.05 us  [shards(): side = lax.ppermute(alike, 'leaf', beside)]
    ppermute x3, waiting for transfers between devices: 0.65 us -> 2.17 us  [shards(): lax.ppermute(sent[n], 'help', help_pairs(xs, -dx, dc))]
  transfers between devices with their start and end apart: 21 -> 21, of which waited for: 7 -> 7; matrix products, arithmetic and copies ran while one was open for 2% -> 2% of each run, Pallas kernels for 38% -> 37%
where the time goes in v4:
time: 95.4 us; the launch traced here: 95.1 us
  Pallas kernels  37 us (39%)
  starting transfers between devices  32.4 us (34%)
  waiting for transfers between devices  21.4 us (22%)
  local copies, waits for them, and re-layouts  3.99 us (4%)
    pallas_call x5, Pallas kernels, near_call(): pl.pallas_call(partial(near_body, len(msgs) // 2, sets, leaves_at, rows,...  23.4 us
    pallas_call x1, Pallas kernels, far_call(): pl.pallas_call(partial(far_body, groups, rows), name='far', out_shape=jax...  6.38 us
    ppermute x1, waiting for transfers between devices, shards(): pts_z = lax.ppermute(pts_y, 'leaf', across)  6.27 us
    ppermute x1, starting transfers between devices, shards(): side = lax.ppermute(alike, 'leaf', beside)  6.05 us
    ppermute x3, starting transfers between devices, shards(): lax.ppermute(payload, 'leaf', [(i, i ^ mask) for i in range(groups)])  4.45 us
    ppermute x2, waiting for transfers between devices, to_help(): return lax.ppermute(value, 'help', help_pairs(xs, -dx, 0))  4.3 us
    ppermute x1, starting transfers between devices, shards(): w_z = [lax.ppermute(w_y[0], 'leaf', across)]  4.28 us
    ppermute x1, waiting for transfers between devices, shards(): side = lax.ppermute(alike, 'leaf', beside)  4.08 us
  transfers between devices with their start and end apart: 21, of which 7 were waited for; matrix products, arithmetic and copies ran while one was open for 2% of the time, Pallas kernels for 37%

profile of v4, /device:TPU:0, one launch (start us, length us, event | category | flops | bytes accessed | tf_op | source)
XLA Modules:
  0.0 95.1 jit_solution(259542070282742240)
XLA Ops:
  0.0 3.0 %collective-permute-start = (f32[64,1024]{1,0:T(8,128)}, f32[64,1024]{1,0:T(8,128)}, u32[]{:S(2)}, u32[]{:S(2)}) collective-permute-start(f32[64,1024]{1,0:T(8,128)} %refs_6_.1), channel_id=1, source_target_pairs={{0,4},{4,0},{8,12},{12,8},{16,20},{20,16},{24,28},{28,24},{1,5},{5... | collective-permute-start | bytes 786440 | tf_op jit(solution)/shard_map/ppermute | solution.py:535
  3.0 2.3 %fusion = (f32[128,1024]{1,0:T(8,128)}, f32[128,1024]{1,0:T(8,128)}) fusion(f32[256,1024]{1,0:T(8,128)} %refs_7_.1), kind=kLoop, calls=%fused_computation | loop fusion | bytes 2097152 | tf_op jit(solution)/shard_map/slice | solution.py:536
  5.3 4.1 %leaf_up.1 = (f32[88,1024]{1,0:T(8,128)}, f32[88,1024]{1,0:T(8,128)}, f32[88,1024]{1,0:T(8,128)}, f32[88,1024]{1,0:T(8,128)}) custom-call(s32[1,2]{1,0:T(1,128)} %count_ref.1, s32[2,32]{1,0:T(2,128)} %src_ref.1, f32[64,1024]{1,0:T(8,128)} %refs_6_.1, f32[256,1024]{1,0:T(8,128)} %refs_7_.1, f32[2,512,256]{2,1,0:T(8,128)} %interp_ref.1), custom_call_target="tpu_custom_call" | custom-call | tf_op jit(solution)/shard_map/leaf_up/pallas_call | solution.py:297
  9.4 2.1 %collective-permute-start.4 = (f32[88,1024]{1,0:T(8,128)}, f32[88,1024]{1,0:T(8,128)S(1)}, u32[]{:S(2)}, u32[]{:S(2)}) collective-permute-start(f32[88,1024]{1,0:T(8,128)} %get-tuple-element.35), channel_id=1, source_target_pairs={{2,0},{3,1},{0,2},{1,3},{6,4},{7,5},{4,6},{5,7},{10,8},{11,9},{8,1... | collective-permute-start | bytes 1081352 | tf_op jit(solution)/shard_map/ppermute | solution.py:539
  11.5 3.7 %collective-permute-start.1 = (f32[64,1024]{1,0:T(8,128)}, f32[64,1024]{1,0:T(8,128)S(1)}, u32[]{:S(2)}, u32[]{:S(2)}) collective-permute-start(f32[64,1024]{1,0:T(8,128)} %collective-permute-done.refs_6_), channel_id=1, source_target_pairs={{0,8},{8,16},{16,24},{12,4},{20,12},{28,20},{1,9},{9,17},{17,25},{... | collective-permute-start | bytes 786440 | tf_op jit(solution)/shard_map/ppermute | solution.py:543
  15.4 6.3 %collective-permute-done.1.pts_ref = f32[64,1024]{1,0:T(8,128)S(1)} collective-permute-done((f32[64,1024]{1,0:T(8,128)}, f32[64,1024]{1,0:T(8,128)S(1)}, u32[]{:S(2)}, u32[]{:S(2)}) %collective-permute-start.1) | collective-permute-done | bytes 262176 | tf_op jit(solution)/shard_map/ppermute | solution.py:543
  21.6 4.3 %collective-permute-start.9 = (f32[128,1024]{1,0:T(8,128)}, f32[128,1024]{1,0:T(8,128)S(1)}, u32[]{:S(2)}, u32[]{:S(2)}) collective-permute-start(f32[128,1024]{1,0:T(8,128)} %collective-permute-done.2.refs_7_), channel_id=1, source_target_pairs={{0,8},{8,16},{16,24},{12,4},{20,12},{28,20},{1,9},{9,17},{17,25},{... | collective-permute-start | bytes 1572872 | tf_op jit(solution)/shard_map/ppermute | solution.py:545
  25.9 2.2 %collective-permute-done.5.refs_3_ = f32[88,1024]{1,0:T(8,128)S(1)} collective-permute-done((f32[88,1024]{1,0:T(8,128)}, f32[88,1024]{1,0:T(8,128)S(1)}, u32[]{:S(2)}, u32[]{:S(2)}) %collective-permute-start.5) | collective-permute-done | bytes 360480 | tf_op jit(solution)/shard_map/ppermute | solution.py:539
  30.6 1.4 %collective-permute-done.10.refs_8_ = f32[128,1024]{1,0:T(8,128)S(1)} collective-permute-done((f32[128,1024]{1,0:T(8,128)}, f32[128,1024]{1,0:T(8,128)S(1)}, u32[]{:S(2)}, u32[]{:S(2)}) %collective-permute-start.10) | collective-permute-done | bytes 524320 | tf_op jit(solution)/shard_map/ppermute | solution.py:536
  32.0 3.7 %collective-permute-start.12 = (f32[128,1024]{1,0:T(8,128)S(1)}, f32[128,1024]{1,0:T(8,128)S(1)}, u32[]{:S(2)}, u32[]{:S(2)}) collective-permute-start(f32[128,1024]{1,0:T(8,128)S(1)} %collective-permute-done.10.refs_8_), channel_id=1, source_target_pairs={{0,8},{8,16},{16,24},{12,4},{20,12},{28,20},{1,9},{9,17},{17,25},{... | collective-permute-start | bytes 1572872 | tf_op jit(solution)/shard_map/ppermute | solution.py:555
  35.7 1.6 %collective-permute-start.6 = (f32[128,256]{1,0:T(8,128)S(1)}, f32[128,256]{1,0:T(8,128)S(1)}, u32[]{:S(2)}, u32[]{:S(2)}) collective-permute-start(f32[128,256]{1,0:T(8,128)S(1)} %get-tuple-element.47.refs_0_), channel_id=1, source_target_pairs={{0,8},{4,12},{8,0},{12,4},{16,24},{20,28},{24,16},{28,20},{1,9},{5... | collective-permute-start | bytes 393224 | tf_op jit(solution)/shard_map/ppermute | solution.py:550
  38.4 1.7 %collective-permute-start.8 = (f32[128,256]{1,0:T(8,128)S(1)}, f32[128,256]{1,0:T(8,128)S(1)}, u32[]{:S(2)}, u32[]{:S(2)}) collective-permute-start(f32[128,256]{1,0:T(8,128)S(1)} %get-tuple-element.47.refs_0_), channel_id=1, source_target_pairs={{0,24},{4,28},{8,16},{12,20},{16,8},{20,12},{24,0},{28,4},{1,25},{... | collective-permute-start | bytes 393224 | tf_op jit(solution)/shard_map/ppermute | solution.py:550
  40.7 9.3 %near_own.1.refs_9_.refs_13_ = f32[8,256,512]{2,1,0:T(8,128)S(1)} custom-call(f32[88,1024]{1,0:T(8,128)S(1)} %copy-done.2, f32[88,1024]{1,0:T(8,128)S(1)} %collective-permute-done.3.refs_1_, f32[88,1024]{1,0:T(8,128)S(1)} %collective-permute-done.4.refs_2_, f32[88,1024]{1,0:T(8,128)S(1)} %collective-permute-done.5.refs_3_, ...), custom_call_target="tpu_custom_call" | custom-call | tf_op jit(solution)/shard_map/near_own/pallas_call | solution.py:206
  50.0 6.8 %near_pair.1.refs_10_.refs_11_ = f32[4,256,512]{2,1,0:T(8,128)S(1)} custom-call(f32[88,1024]{1,0:T(8,128)S(1)} %copy-done.2, f32[88,1024]{1,0:T(8,128)S(1)} %collective-permute-done.3.refs_1_, f32[88,1024]{1,0:T(8,128)S(1)} %collective-permute-done.4.refs_2_, f32[88,1024]{1,0:T(8,128)S(1)} %collective-permute-done.5.refs_3_, ...), custom_call_target="tpu_custom_call" | custom-call | tf_op jit(solution)/shard_map/near_pair/pallas_call | solution.py:206
  59.3 6.0 %collective-permute-start.11 = (f32[4,128,256]{2,1,0:T(8,128)S(1)}, f32[4,128,256]{2,1,0:T(8,128)S(1)}, u32[]{:S(2)}, u32[]{:S(2)}) collective-permute-start(f32[4,128,256]{2,1,0:T(8,128)S(1)} %stack.2.refs_11_.alike_ref), channel_id=1, source_target_pairs={{0,4},{4,0},{8,12},{12,8},{16,20},{20,16},{24,28},{28,24},{1,5},{5... | collective-permute-start | bytes 1572872 | tf_op jit(solution)/shard_map/ppermute | solution.py:564
  65.4 1.6 %collective-permute-start.17 = (f32[128,1024]{1,0:T(8,128)S(1)}, f32[128,1024]{1,0:T(8,128)S(1)}, u32[]{:S(2)}, u32[]{:S(2)}) collective-permute-start(f32[128,1024]{1,0:T(8,128)S(1)} %add_parts.4), channel_id=1, source_target_pairs={{2,0},{3,1},{0,2},{1,3},{6,4},{7,5},{4,6},{5,7},{10,8},{11,9},{8,1... | collective-permute-start | bytes 1572872 | tf_op jit(solution)/shard_map/ppermute | solution.py:524
  67.6 5.5 %near_home.1 = (f32[128,1024]{1,0:T(8,128)S(1)}, f32[128,1024]{1,0:T(8,128)S(1)}, f32[128,1024]{1,0:T(8,128)S(1)}, f32[128,1024]{1,0:T(8,128)S(1)}) custom-call(f32[88,1024]{1,0:T(8,128)S(1)} %copy-done.2, f32[88,1024]{1,0:T(8,128)S(1)} %collective-permute-done.3.refs_1_, f32[88,1024]{1,0:T(8,128)S(1)} %collective-permute-done.4.refs_2_, ...), custom_call_target="tpu_custom_call" | custom-call | tf_op jit(solution)/shard_map/near_home/pallas_call | solution.py:206
  73.8 4.1 %collective-permute-done.11.beside_ref = f32[4,128,256]{2,1,0:T(8,128)S(1)} collective-permute-done((f32[4,128,256]{2,1,0:T(8,128)S(1)}, f32[4,128,256]{2,1,0:T(8,128)S(1)}, u32[]{:S(2)}, u32[]{:S(2)}) %collective-permute-start.11) | collective-permute-done | bytes 524320 | tf_op jit(solution)/shard_map/ppermute | solution.py:564
  77.9 6.4 %far.1.refs_0_ = f32[64,256]{1,0:T(8,128)S(1)} custom-call(s32[4,14]{1,0:T(4,128)S(1)} %bitcast.1, s32[6,256]{1,0:T(8,128)S(1)} %copy-done.6, f32[6,512,256]{2,1,0:T(8,128)S(1)} %copy-done.4, f32[4,128,256]{2,1,0:T(8,128)S(1)} %stack.2.refs_11_.alike_ref, f32[4,128,256]{2,1,0:T(8,128)S(1)} %collective-permute-done.11.beside_ref, ...), custom_call_target="tpu_custom_call" | custom-call | tf_op jit(solution)/shard_map/far/pallas_call | solution.py:440
  84.3 1.2 %collective-permute-done.14.refs_1_ = f32[64,256]{1,0:T(8,128)S(1)} collective-permute-done((f32[64,256]{1,0:T(8,128)S(1)}, f32[64,256]{1,0:T(8,128)S(1)}, u32[]{:S(2)}, u32[]{:S(2)}) %collective-permute-start.14) | collective-permute-done | bytes 65568 | tf_op jit(solution)/shard_map/ppermute | solution.py:521
  85.6 1.6 %collective-permute-start.15 = (f32[2,64,256]{2,1,0:T(8,128)S(1)}, f32[2,64,256]{2,1,0:T(8,128)S(1)}, u32[]{:S(2)}, u32[]{:S(2)}) collective-permute-start(f32[2,64,256]{2,1,0:T(8,128)S(1)} %stack.3.refs_0_), channel_id=1, source_target_pairs={{2,0},{3,1},{0,2},{1,3},{6,4},{7,5},{4,6},{5,7},{10,8},{11,9},{8,1... | collective-permute-start | bytes 393224 | tf_op jit(solution)/shard_map/ppermute | solution.py:521
  87.2 4.3 %collective-permute-done.18.refs_3_ = f32[128,1024]{1,0:T(8,128)S(1)} collective-permute-done((f32[128,1024]{1,0:T(8,128)S(1)}, f32[128,1024]{1,0:T(8,128)S(1)}, u32[]{:S(2)}, u32[]{:S(2)}) %collective-permute-start.18) | collective-permute-done | bytes 524320 | tf_op jit(solution)/shard_map/ppermute | solution.py:524
  91.6 1.9 %collective-permute-done.15.refs_1_ = f32[2,64,256]{2,1,0:T(8,128)S(1)} collective-permute-done((f32[2,64,256]{2,1,0:T(8,128)S(1)}, f32[2,64,256]{2,1,0:T(8,128)S(1)}, u32[]{:S(2)}, u32[]{:S(2)}) %collective-permute-start.15) | collective-permute-done | bytes 131104 | tf_op jit(solution)/shard_map/ppermute | solution.py:521
  93.5 1.6 %join.1 = f32[256,1024]{1,0:T(8,128)} custom-call(f32[2,512,256]{2,1,0:T(8,128)S(1)} %copy-done.3, f32[2,64,256]{2,1,0:T(8,128)S(1)} %stack.3.refs_0_, f32[2,64,256]{2,1,0:T(8,128)S(1)} %collective-permute-done.15.refs_1_, f32[128,1024]{1,0:T(8,128)S(1)} %get-tuple-element.55.refs_2_, f32[128,1024]{1,0:T(8,128)S(1)} %get-tuple-element.56.refs_3_, ...), custom_call_target="tpu_custom_call" | custom-call | tf_op jit(solution)/shard_map/join/pallas_call | solution.py:497
  (52 shorter events, 8.3 us)
Async XLA Ops:
  0.0 11.5 %collective-permute-start = (f32[64,1024]{1,0:T(8,128)}, f32[64,1024]{1,0:T(8,128)}, u32[]{:S(2)}, u32[]{:S(2)}) collective-permute-start(f32[64,1024]{1,0:T(8,128)} %refs_6_.1), channel_id=1, source_target_pairs={{0,4},{4,0},{8,12},{12,8},{16,20},{20,16},{24,28},{28,24},{1,5},{5... | collective-permute-start | bytes 786440 | tf_op jit(solution)/shard_map/ppermute | solution.py:535
  5.3 16.4 %collective-permute-start.2 = (f32[128,1024]{1,0:T(8,128)}, f32[128,1024]{1,0:T(8,128)}, u32[]{:S(2)}, u32[]{:S(2)}) collective-permute-start(f32[128,1024]{1,0:T(8,128)} %get-tuple-element.60), channel_id=1, source_target_pairs={{0,4},{4,0},{8,12},{12,8},{16,20},{20,16},{24,28},{28,24},{1,5},{5... | collective-permute-start | bytes 1572872 | tf_op jit(solution)/shard_map/ppermute | solution.py:536
  9.3 5.9 %collective-permute-start.3 = (f32[88,1024]{1,0:T(8,128)}, f32[88,1024]{1,0:T(8,128)S(1)}, u32[]{:S(2)}, u32[]{:S(2)}) collective-permute-start(f32[88,1024]{1,0:T(8,128)} %get-tuple-element.33), channel_id=1, source_target_pairs={{1,0},{0,1},{3,2},{2,3},{5,4},{4,5},{7,6},{6,7},{9,8},{8,9},{11,10... | collective-permute-start | bytes 1081352 | tf_op jit(solution)/shard_map/ppermute | solution.py:539
  9.4 16.5 %collective-permute-start.4 = (f32[88,1024]{1,0:T(8,128)}, f32[88,1024]{1,0:T(8,128)S(1)}, u32[]{:S(2)}, u32[]{:S(2)}) collective-permute-start(f32[88,1024]{1,0:T(8,128)} %get-tuple-element.35), channel_id=1, source_target_pairs={{2,0},{3,1},{0,2},{1,3},{6,4},{7,5},{4,6},{5,7},{10,8},{11,9},{8,1... | collective-permute-start | bytes 1081352 | tf_op jit(solution)/shard_map/ppermute | solution.py:539
  11.5 16.7 %collective-permute-start.5 = (f32[88,1024]{1,0:T(8,128)}, f32[88,1024]{1,0:T(8,128)S(1)}, u32[]{:S(2)}, u32[]{:S(2)}) collective-permute-start(f32[88,1024]{1,0:T(8,128)} %get-tuple-element.36), channel_id=1, source_target_pairs={{3,0},{2,1},{1,2},{0,3},{7,4},{6,5},{5,6},{4,7},{11,8},{10,9},{9,1... | collective-permute-start | bytes 1081352 | tf_op jit(solution)/shard_map/ppermute | solution.py:539
  11.5 10.1 %collective-permute-start.1 = (f32[64,1024]{1,0:T(8,128)}, f32[64,1024]{1,0:T(8,128)S(1)}, u32[]{:S(2)}, u32[]{:S(2)}) collective-permute-start(f32[64,1024]{1,0:T(8,128)} %collective-permute-done.refs_6_), channel_id=1, source_target_pairs={{0,8},{8,16},{16,24},{12,4},{20,12},{28,20},{1,9},{9,17},{17,25},{... | collective-permute-start | bytes 786440 | tf_op jit(solution)/shard_map/ppermute | solution.py:543
  15.3 16.7 %collective-permute-start.10 = (f32[128,1024]{1,0:T(8,128)}, f32[128,1024]{1,0:T(8,128)S(1)}, u32[]{:S(2)}, u32[]{:S(2)}) collective-permute-start(f32[128,1024]{1,0:T(8,128)} %get-tuple-element.59), channel_id=1, source_target_pairs={{0,4},{4,0},{8,12},{12,8},{16,20},{20,16},{24,28},{28,24},{1,5},{5... | collective-permute-start | bytes 1572872 | tf_op jit(solution)/shard_map/ppermute | solution.py:536
  21.6 35.1 %collective-permute-start.9 = (f32[128,1024]{1,0:T(8,128)}, f32[128,1024]{1,0:T(8,128)S(1)}, u32[]{:S(2)}, u32[]{:S(2)}) collective-permute-start(f32[128,1024]{1,0:T(8,128)} %collective-permute-done.2.refs_7_), channel_id=1, source_target_pairs={{0,8},{8,16},{16,24},{12,4},{20,12},{28,20},{1,9},{9,17},{17,25},{... | collective-permute-start | bytes 1572872 | tf_op jit(solution)/shard_map/ppermute | solution.py:545
  29.8 10.9 %copy-start.2 = (f32[88,1024]{1,0:T(8,128)S(1)}, f32[88,1024]{1,0:T(8,128)}, u32[]{:S(2)}) copy-start(f32[88,1024]{1,0:T(8,128)} %get-tuple-element.32.refs_0_) | copy-start | bytes 1081348
  29.8 10.9 %copy-start.5 = (f32[64,1024]{1,0:T(8,128)S(1)}, f32[64,1024]{1,0:T(8,128)}, u32[]{:S(2)}) copy-start(f32[64,1024]{1,0:T(8,128)} %refs_6_.1) | copy-start | bytes 786436
  32.0 25.8 %collective-permute-start.12 = (f32[128,1024]{1,0:T(8,128)S(1)}, f32[128,1024]{1,0:T(8,128)S(1)}, u32[]{:S(2)}, u32[]{:S(2)}) collective-permute-start(f32[128,1024]{1,0:T(8,128)S(1)} %collective-permute-done.10.refs_8_), channel_id=1, source_target_pairs={{0,8},{8,16},{16,24},{12,4},{20,12},{28,20},{1,9},{9,17},{17,25},{... | collective-permute-start | bytes 1572872 | tf_op jit(solution)/shard_map/ppermute | solution.py:555
  35.7 22.0 %collective-permute-start.6 = (f32[128,256]{1,0:T(8,128)S(1)}, f32[128,256]{1,0:T(8,128)S(1)}, u32[]{:S(2)}, u32[]{:S(2)}) collective-permute-start(f32[128,256]{1,0:T(8,128)S(1)} %get-tuple-element.47.refs_0_), channel_id=1, source_target_pairs={{0,8},{4,12},{8,0},{12,4},{16,24},{20,28},{24,16},{28,20},{1,9},{5... | collective-permute-start | bytes 393224 | tf_op jit(solution)/shard_map/ppermute | solution.py:550
  37.3 20.4 %collective-permute-start.7 = (f32[128,256]{1,0:T(8,128)S(1)}, f32[128,256]{1,0:T(8,128)S(1)}, u32[]{:S(2)}, u32[]{:S(2)}) collective-permute-start(f32[128,256]{1,0:T(8,128)S(1)} %get-tuple-element.47.refs_0_), channel_id=1, source_target_pairs={{0,16},{4,20},{8,24},{12,28},{16,0},{20,4},{24,8},{28,12},{1,17},{... | collective-permute-start | bytes 393224 | tf_op jit(solution)/shard_map/ppermute | solution.py:550
  38.4 19.3 %collective-permute-start.8 = (f32[128,256]{1,0:T(8,128)S(1)}, f32[128,256]{1,0:T(8,128)S(1)}, u32[]{:S(2)}, u32[]{:S(2)}) collective-permute-start(f32[128,256]{1,0:T(8,128)S(1)} %get-tuple-element.47.refs_0_), channel_id=1, source_target_pairs={{0,24},{4,28},{8,16},{12,20},{16,8},{20,12},{24,0},{28,4},{1,25},{... | collective-permute-start | bytes 393224 | tf_op jit(solution)/shard_map/ppermute | solution.py:550
  57.6 7.8 %collective-permute-start.16 = (f32[128,1024]{1,0:T(8,128)S(1)}, f32[128,1024]{1,0:T(8,128)S(1)}, u32[]{:S(2)}, u32[]{:S(2)}) collective-permute-start(f32[128,1024]{1,0:T(8,128)S(1)} %get-tuple-element.46), channel_id=1, source_target_pairs={{1,0},{0,1},{3,2},{2,3},{5,4},{4,5},{7,6},{6,7},{9,8},{8,9},{11,10... | collective-permute-start | bytes 1572872 | tf_op jit(solution)/shard_map/ppermute | solution.py:521
  58.7 8.2 %collective-permute-start.13 = (f32[128,1024]{1,0:T(8,128)S(1)}, f32[128,1024]{1,0:T(8,128)S(1)}, u32[]{:S(2)}, u32[]{:S(2)}) collective-permute-start(f32[128,1024]{1,0:T(8,128)S(1)} %get-tuple-element.52), channel_id=1, source_target_pairs={{1,0},{0,1},{3,2},{2,3},{5,4},{4,5},{7,6},{6,7},{9,8},{8,9},{11,10... | collective-permute-start | bytes 1572872 | tf_op jit(solution)/shard_map/ppermute | solution.py:521
  59.3 18.6 %collective-permute-start.11 = (f32[4,128,256]{2,1,0:T(8,128)S(1)}, f32[4,128,256]{2,1,0:T(8,128)S(1)}, u32[]{:S(2)}, u32[]{:S(2)}) collective-permute-start(f32[4,128,256]{2,1,0:T(8,128)S(1)} %stack.2.refs_11_.alike_ref), channel_id=1, source_target_pairs={{0,4},{4,0},{8,12},{12,8},{16,20},{20,16},{24,28},{28,24},{1,5},{5... | collective-permute-start | bytes 1572872 | tf_op jit(solution)/shard_map/ppermute | solution.py:564
  65.4 21.8 %collective-permute-start.17 = (f32[128,1024]{1,0:T(8,128)S(1)}, f32[128,1024]{1,0:T(8,128)S(1)}, u32[]{:S(2)}, u32[]{:S(2)}) collective-permute-start(f32[128,1024]{1,0:T(8,128)S(1)} %add_parts.4), channel_id=1, source_target_pairs={{2,0},{3,1},{0,2},{1,3},{6,4},{7,5},{4,6},{5,7},{10,8},{11,9},{8,1... | collective-permute-start | bytes 1572872 | tf_op jit(solution)/shard_map/ppermute | solution.py:524
  67.0 24.4 %collective-permute-start.18 = (f32[128,1024]{1,0:T(8,128)S(1)}, f32[128,1024]{1,0:T(8,128)S(1)}, u32[]{:S(2)}, u32[]{:S(2)}) collective-permute-start(f32[128,1024]{1,0:T(8,128)S(1)} %add_parts.3.refs_14_), channel_id=1, source_target_pairs={{2,0},{3,1},{0,2},{1,3},{6,4},{7,5},{4,6},{5,7},{10,8},{11,9},{8,1... | collective-permute-start | bytes 1572872 | tf_op jit(solution)/shard_map/ppermute | solution.py:524
  73.2 20.3 %collective-permute-start.19 = (f32[128,1024]{1,0:T(8,128)S(1)}, f32[128,1024]{1,0:T(8,128)S(1)}, u32[]{:S(2)}, u32[]{:S(2)}) collective-permute-start(f32[128,1024]{1,0:T(8,128)S(1)} %get-tuple-element.57), channel_id=1, source_target_pairs={{1,0},{0,1},{3,2},{2,3},{5,4},{4,5},{7,6},{6,7},{9,8},{8,9},{11,10... | collective-permute-start | bytes 1572872 | tf_op jit(solution)/shard_map/ppermute | solution.py:521
  73.3 20.2 %collective-permute-start.20 = (f32[128,1024]{1,0:T(8,128)S(1)}, f32[128,1024]{1,0:T(8,128)S(1)}, u32[]{:S(2)}, u32[]{:S(2)}) collective-permute-start(f32[128,1024]{1,0:T(8,128)S(1)} %get-tuple-element.58), channel_id=1, source_target_pairs={{1,0},{0,1},{3,2},{2,3},{5,4},{4,5},{7,6},{6,7},{9,8},{8,9},{11,10... | collective-permute-start | bytes 1572872 | tf_op jit(solution)/shard_map/ppermute | solution.py:521
  77.9 15.6 %copy-start.3 = (f32[2,512,256]{2,1,0:T(8,128)S(1)}, f32[2,512,256]{2,1,0:T(8,128)}, u32[]{:S(2)}) copy-start(f32[2,512,256]{2,1,0:T(8,128)} %interp_ref.1) | copy-start | bytes 3145732
  84.3 1.3 %collective-permute-start.14 = (f32[64,256]{1,0:T(8,128)S(1)}, f32[64,256]{1,0:T(8,128)S(1)}, u32[]{:S(2)}, u32[]{:S(2)}) collective-permute-start(f32[64,256]{1,0:T(8,128)S(1)} %far.1.refs_0_), channel_id=1, source_target_pairs={{1,0},{0,1},{3,2},{2,3},{5,4},{4,5},{7,6},{6,7},{9,8},{8,9},{11,10... | collective-permute-start | bytes 196616 | tf_op jit(solution)/shard_map/ppermute | solution.py:521
  85.6 7.9 %collective-permute-start.15 = (f32[2,64,256]{2,1,0:T(8,128)S(1)}, f32[2,64,256]{2,1,0:T(8,128)S(1)}, u32[]{:S(2)}, u32[]{:S(2)}) collective-permute-start(f32[2,64,256]{2,1,0:T(8,128)S(1)} %stack.3.refs_0_), channel_id=1, source_target_pairs={{2,0},{3,1},{0,2},{1,3},{6,4},{7,5},{4,6},{5,7},{10,8},{11,9},{8,1... | collective-permute-start | bytes 393224 | tf_op jit(solution)/shard_map/ppermute | solution.py:521
  (6 other events, 45.0 us)

commit v5 on v4

--- a/solution.py
+++ b/solution.py
@@ -14,6 +14,7 @@
 SK = 256
 FL = 4
 EXTRA = 8
+HALF = F // 2
 SIZES = (128, 128)
 
 BF = jnp.bfloat16
@@ -312,7 +313,7 @@
 
 
 def skel_body(xs, index_ref, *refs):
-    msgs, (out_ref, side_ref, off_ref) = refs[:-3], refs[-3:]
+    msgs, (out_ref, side_ref, off_ref, scr) = refs[:-4], refs[-4:]
     rows = R // (2 * xs)
     tall = share_rows(xs)
     total = jnp.zeros((2 * F, SK), F32)
@@ -329,9 +330,10 @@
         hot = spot + helper * (2 * LEAF) == index_ref[...]
         total = total + dot(side[: 2 * F], hot.astype(F32).astype(BF))
         value = value + msg[F + EXTRA :, :]
-    out_ref[:F, :] = total[:F] + total[F:]
+    scr[...] = total[:F] + total[F:]
+    out_ref[:HALF, :] = scr[pl.ds(pl.multiple_of(core * HALF, HALF), HALF), :]
     for i in range(rows // tall):
-        out_ref[F + i * tall : F + (i + 1) * tall, :] = value[:, i * SK : (i + 1) * SK]
+        out_ref[HALF + i * tall : HALF + (i + 1) * tall, :] = value[:, i * SK : (i + 1) * SK]
 
 
 def skel_call(xs, index, msgs):
@@ -342,12 +344,13 @@
         partial(skel_body, xs),
         name="skeleton",
         out_shape=[
-            jax.ShapeDtypeStruct((F + rows, SK), F32),
+            jax.ShapeDtypeStruct((HALF + rows, SK), F32),
             jax.ShapeDtypeStruct((leaves, 4 * F, LEAF), BF),
             jax.ShapeDtypeStruct((leaves, 8, LEAF), F32),
         ],
         in_specs=[vmem] * (1 + len(msgs)),
         out_specs=[vmem] * 3,
+        scratch_shapes=[pltpu.VMEM((F, SK), F32)],
         compiler_params=pltpu.CompilerParams(vmem_limit_bytes=VMEM_LIMIT),
         cost_estimate=pl.CostEstimate(
             flops=5_000_000_000, bytes_accessed=8_000_000, transcendentals=0
@@ -373,6 +376,25 @@
     )(*pieces)
 
 
+def points_body(alike_ref, beside_ref, out_ref):
+    count = alike_ref.shape[0]
+    for n in range(count):
+        out_ref[n] = alike_ref[n, :HALF, :]
+        out_ref[count + n] = beside_ref[n, :HALF, :]
+
+
+def points_call(alike, beside):
+    vmem = pl.BlockSpec(memory_space=pltpu.VMEM)
+    return pl.pallas_call(
+        points_body,
+        name="points_of",
+        out_shape=jax.ShapeDtypeStruct((2 * alike.shape[0], HALF, SK), F32),
+        in_specs=[vmem, vmem],
+        out_specs=vmem,
+        compiler_params=pltpu.CompilerParams(vmem_limit_bytes=VMEM_LIMIT),
+    )(alike, beside)
+
+
 def upper_start(level, groups):
     return sum((groups >> step for step in range(1, level)))
 
@@ -381,17 +403,20 @@
     return sum((groups >> step for step in range(level)))
 
 
-def far_body(groups, rows, far_ref, node_ref, transfer_ref, alike_ref, beside_ref, *refs):
+def far_body(groups, rows, far_ref, node_ref, transfer_ref, alike_ref, beside_ref, mate_ref, *refs):
     out_ref, p_scr, u_scr, f_scr = refs[-4:]
     levels = groups.bit_length() - 1
     group = place()[2]
     start = [list_start(level, groups) for level in range(levels)]
-    for n in range(groups // 2):
-        same, other = group ^ (2 * n), group ^ (2 * n + 1)
-        p_scr[same] = alike_ref[n, :F, :]
-        u_scr[same] = alike_ref[n, F:, :]
-        p_scr[other] = beside_ref[n, :F, :]
-        u_scr[other] = beside_ref[n, F:, :]
+    core = place()[1]
+    here = pl.ds(pl.multiple_of(core * HALF, HALF), HALF)
+    there = pl.ds(pl.multiple_of((1 - core) * HALF, HALF), HALF)
+    for n in range(groups):
+        node = group ^ (2 * (n % (groups // 2)) + n // (groups // 2))
+        part = (alike_ref, beside_ref)[n // (groups // 2)]
+        p_scr[node, here, :] = part[n % (groups // 2), :HALF, :]
+        p_scr[node, there, :] = mate_ref[n]
+        u_scr[node] = part[n % (groups // 2), HALF:, :]
     spot = lax.broadcasted_iota(jnp.int32, (2 * SK, SK), 0)
     for level in range(1, levels):
         for n in range(groups >> level):
@@ -432,8 +457,8 @@
     out_ref[...] = local
 
 
-def far_call(groups, far_nodes, skel_node, transfer, alike, beside, after):
-    rows = alike.shape[1] - F
+def far_call(groups, far_nodes, skel_node, transfer, alike, beside, mate, after):
+    rows = alike.shape[1] - HALF
     vmem = pl.BlockSpec(memory_space=pltpu.VMEM)
     smem = pl.BlockSpec(memory_space=pltpu.SMEM)
     nodes = 2 * groups
@@ -441,7 +466,7 @@
         partial(far_body, groups, rows),
         name="far",
         out_shape=jax.ShapeDtypeStruct((rows, SK), F32),
-        in_specs=[smem, vmem, vmem, vmem, vmem]
+        in_specs=[smem, vmem, vmem, vmem, vmem, vmem]
         + [pl.BlockSpec(memory_space=pl.ANY)] * len(after),
         out_specs=vmem,
         scratch_shapes=[
@@ -450,7 +475,7 @@
             pltpu.VMEM((groups.bit_length(), rows, SK), F32),
         ],
         compiler_params=pltpu.CompilerParams(vmem_limit_bytes=VMEM_LIMIT),
-    )(far_nodes.T, skel_node, transfer, alike, beside, *after)
+    )(far_nodes.T, skel_node, transfer, alike, beside, mate, *after)
 
 
 def final_body(xs, interp_ref, *refs):
@@ -576,7 +601,8 @@
         parts.append([to_help(value, dx + 1) for dx, value in enumerate(both)])
     sources = [pair_src, ("next", z_side, w_z)]
     home = near_call("near_home", msgs, targets, home, sources, R, 0, [own], both[:1])
-    v_own = far_call(groups, far_nodes, skel_node, transfer, alike, side, home[:1])
+    swapped = from_help(points_call(alike, side), 0, 1)
+    v_own = far_call(groups, far_nodes, skel_node, transfer, alike, side, swapped, home[:1])
     v_pair = stack_call([v_own, from_help(v_own, 0, 1)])
     values = [v_pair] + [from_help(v_pair, dx, 0) for dx in range(1, xs)]
     mate = [from_help(value, 0, 1) for value in home[2:]]

time: 95.4 us -> 93.5 us (0.980)
    ppermute x1, waiting for transfers between devices: 4.08 us -> 0.01 us  [shards(): side = lax.ppermute(alike, 'leaf', beside)]
    ppermute x1, starting transfers between devices: 6.05 us -> 3.11 us  [shards(): side = lax.ppermute(alike, 'leaf', beside)]
    ppermute x6 -> x7, waiting for transfers between devices: 3.18 us -> 4.99 us  [from_help(): return lax.ppermute(value, 'help', help_pairs(xs, dx, dc))]
    ppermute x2, starting transfers between devices: 2.16 us -> 3.69 us  [to_help(): return lax.ppermute(value, 'help', help_pairs(xs, -dx, 0))]
    ppermute x2, waiting for transfers between devices: 4.3 us -> 5.77 us  [to_help(): return lax.ppermute(value, 'help', help_pairs(xs, -dx, 0))]
    ppermute x6 -> x7, starting transfers between devices: 2.82 us -> 3.34 us  [from_help(): return lax.ppermute(value, 'help', help_pairs(xs, dx, dc))]
  transfers between devices with their start and end apart: 21 -> 22, of which waited for: 7 -> 7; matrix products, arithmetic and copies ran while one was open for 2% -> 2% of each run, Pallas kernels for 37% -> 38%
where the time goes in v5:
time: 93.5 us; the launch traced here: 93.7 us
  Pallas kernels  37.2 us (40%)
  starting transfers between devices  31.6 us (34%)
  waiting for transfers between devices  20.6 us (22%)
  local copies, waits for them, and re-layouts  3.98 us (4%)
    pallas_call x5, Pallas kernels, near_call(): pl.pallas_call(partial(near_body, len(msgs) // 2, sets, leaves_at, rows,...  24 us
    ppermute x1, waiting for transfers between devices, shards(): pts_z = lax.ppermute(pts_y, 'leaf', across)  6.27 us
    pallas_call x1, Pallas kernels, far_call(): pl.pallas_call(partial(far_body, groups, rows), name='far', out_shape=jax...  5.94 us
    ppermute x2, waiting for transfers between devices, to_help(): return lax.ppermute(value, 'help', help_pairs(xs, -dx, 0))  5.77 us
    ppermute x7, waiting for transfers between devices, from_help(): return lax.ppermute(value, 'help', help_pairs(xs, dx, dc))  4.99 us
    ppermute x3, starting transfers between devices, shards(): lax.ppermute(payload, 'leaf', [(i, i ^ mask) for i in range(groups)])  4.45 us
    ppermute x1, starting transfers between devices, shards(): w_z = [lax.ppermute(w_y[0], 'leaf', across)]  4.27 us
    pallas_call x1, Pallas kernels, leaf_call(): pl.pallas_call(partial(leaf_body, xs), name='leaf_up', out_shape=[jax.Sha...  4.05 us
  transfers between devices with their start and end apart: 22, of which 7 were waited for; matrix products, arithmetic and copies ran while one was open for 2% of the time, Pallas kernels for 38%

profile of v5, /device:TPU:0, one launch (start us, length us, event | category | flops | bytes accessed | tf_op | source)
XLA Modules:
  0.0 93.7 jit_solution(18255457961442793341)
XLA Ops:
  0.0 3.0 %collective-permute-start = (f32[64,1024]{1,0:T(8,128)}, f32[64,1024]{1,0:T(8,128)}, u32[]{:S(2)}, u32[]{:S(2)}) collective-permute-start(f32[64,1024]{1,0:T(8,128)} %refs_6_.1), channel_id=1, source_target_pairs={{0,4},{4,0},{8,12},{12,8},{16,20},{20,16},{24,28},{28,24},{1,5},{5... | collective-permute-start | bytes 786440 | tf_op jit(solution)/shard_map/ppermute | solution.py:560
  3.0 2.3 %fusion = (f32[128,1024]{1,0:T(8,128)}, f32[128,1024]{1,0:T(8,128)}) fusion(f32[256,1024]{1,0:T(8,128)} %refs_7_.1), kind=kLoop, calls=%fused_computation | loop fusion | bytes 2097152 | tf_op jit(solution)/shard_map/slice | solution.py:561
  5.3 4.1 %leaf_up.1 = (f32[88,1024]{1,0:T(8,128)}, f32[88,1024]{1,0:T(8,128)}, f32[88,1024]{1,0:T(8,128)}, f32[88,1024]{1,0:T(8,128)}) custom-call(s32[1,2]{1,0:T(1,128)} %count_ref.1, s32[2,32]{1,0:T(2,128)} %src_ref.1, f32[64,1024]{1,0:T(8,128)} %refs_6_.1, f32[256,1024]{1,0:T(8,128)} %refs_7_.1, f32[2,512,256]{2,1,0:T(8,128)} %interp_ref.1), custom_call_target="tpu_custom_call" | custom-call | tf_op jit(solution)/shard_map/leaf_up/pallas_call | solution.py:298
  9.4 2.1 %collective-permute-start.4 = (f32[88,1024]{1,0:T(8,128)}, f32[88,1024]{1,0:T(8,128)S(1)}, u32[]{:S(2)}, u32[]{:S(2)}) collective-permute-start(f32[88,1024]{1,0:T(8,128)} %get-tuple-element.35), channel_id=1, source_target_pairs={{2,0},{3,1},{0,2},{1,3},{6,4},{7,5},{4,6},{5,7},{10,8},{11,9},{8,1... | collective-permute-start | bytes 1081352 | tf_op jit(solution)/shard_map/ppermute | solution.py:564
  11.5 3.7 %collective-permute-start.1 = (f32[64,1024]{1,0:T(8,128)}, f32[64,1024]{1,0:T(8,128)S(1)}, u32[]{:S(2)}, u32[]{:S(2)}) collective-permute-start(f32[64,1024]{1,0:T(8,128)} %collective-permute-done.refs_6_), channel_id=1, source_target_pairs={{0,8},{8,16},{16,24},{12,4},{20,12},{28,20},{1,9},{9,17},{17,25},{... | collective-permute-start | bytes 786440 | tf_op jit(solution)/shard_map/ppermute | solution.py:568
  15.3 6.3 %collective-permute-done.1.pts_ref = f32[64,1024]{1,0:T(8,128)S(1)} collective-permute-done((f32[64,1024]{1,0:T(8,128)}, f32[64,1024]{1,0:T(8,128)S(1)}, u32[]{:S(2)}, u32[]{:S(2)}) %collective-permute-start.1) | collective-permute-done | bytes 262176 | tf_op jit(solution)/shard_map/ppermute | solution.py:568
  21.6 4.3 %collective-permute-start.9 = (f32[128,1024]{1,0:T(8,128)}, f32[128,1024]{1,0:T(8,128)S(1)}, u32[]{:S(2)}, u32[]{:S(2)}) collective-permute-start(f32[128,1024]{1,0:T(8,128)} %collective-permute-done.2.refs_7_), channel_id=1, source_target_pairs={{0,8},{8,16},{16,24},{12,4},{20,12},{28,20},{1,9},{9,17},{17,25},{... | collective-permute-start | bytes 1572872 | tf_op jit(solution)/shard_map/ppermute | solution.py:570
  25.9 2.2 %collective-permute-done.5.refs_3_ = f32[88,1024]{1,0:T(8,128)S(1)} collective-permute-done((f32[88,1024]{1,0:T(8,128)}, f32[88,1024]{1,0:T(8,128)S(1)}, u32[]{:S(2)}, u32[]{:S(2)}) %collective-permute-start.5) | collective-permute-done | bytes 360480 | tf_op jit(solution)/shard_map/ppermute | solution.py:564
  30.6 1.4 %collective-permute-done.10.refs_8_ = f32[128,1024]{1,0:T(8,128)S(1)} collective-permute-done((f32[128,1024]{1,0:T(8,128)}, f32[128,1024]{1,0:T(8,128)S(1)}, u32[]{:S(2)}, u32[]{:S(2)}) %collective-permute-start.10) | collective-permute-done | bytes 524320 | tf_op jit(solution)/shard_map/ppermute | solution.py:561
  32.0 3.7 %collective-permute-start.13 = (f32[128,1024]{1,0:T(8,128)S(1)}, f32[128,1024]{1,0:T(8,128)S(1)}, u32[]{:S(2)}, u32[]{:S(2)}) collective-permute-start(f32[128,1024]{1,0:T(8,128)S(1)} %collective-permute-done.10.refs_8_), channel_id=1, source_target_pairs={{0,8},{8,16},{16,24},{12,4},{20,12},{28,20},{1,9},{9,17},{17,25},{... | collective-permute-start | bytes 1572872 | tf_op jit(solution)/shard_map/ppermute | solution.py:580
  35.7 1.6 %collective-permute-start.6 = (f32[96,256]{1,0:T(8,128)S(1)}, f32[96,256]{1,0:T(8,128)S(1)}, u32[]{:S(2)}, u32[]{:S(2)}) collective-permute-start(f32[96,256]{1,0:T(8,128)S(1)} %get-tuple-element.47.refs_0_), channel_id=1, source_target_pairs={{0,8},{4,12},{8,0},{12,4},{16,24},{20,28},{24,16},{28,20},{1,9},{5... | collective-permute-start | bytes 294920 | tf_op jit(solution)/shard_map/ppermute | solution.py:575
  37.3 1.1 %collective-permute-start.7 = (f32[96,256]{1,0:T(8,128)S(1)}, f32[96,256]{1,0:T(8,128)S(1)}, u32[]{:S(2)}, u32[]{:S(2)}) collective-permute-start(f32[96,256]{1,0:T(8,128)S(1)} %get-tuple-element.47.refs_0_), channel_id=1, source_target_pairs={{0,16},{4,20},{8,24},{12,28},{16,0},{20,4},{24,8},{28,12},{1,17},{... | collective-permute-start | bytes 294920 | tf_op jit(solution)/shard_map/ppermute | solution.py:575
  38.4 1.7 %collective-permute-start.8 = (f32[96,256]{1,0:T(8,128)S(1)}, f32[96,256]{1,0:T(8,128)S(1)}, u32[]{:S(2)}, u32[]{:S(2)}) collective-permute-start(f32[96,256]{1,0:T(8,128)S(1)} %get-tuple-element.47.refs_0_), channel_id=1, source_target_pairs={{0,24},{4,28},{8,16},{12,20},{16,8},{20,12},{24,0},{28,4},{1,25},{... | collective-permute-start | bytes 294920 | tf_op jit(solution)/shard_map/ppermute | solution.py:575
  40.7 10.1 %near_own.1.refs_9_.refs_13_ = f32[8,256,512]{2,1,0:T(8,128)S(1)} custom-call(f32[88,1024]{1,0:T(8,128)S(1)} %copy-done.2, f32[88,1024]{1,0:T(8,128)S(1)} %collective-permute-done.3.refs_1_, f32[88,1024]{1,0:T(8,128)S(1)} %collective-permute-done.4.refs_2_, f32[88,1024]{1,0:T(8,128)S(1)} %collective-permute-done.5.refs_3_, ...), custom_call_target="tpu_custom_call" | custom-call | tf_op jit(solution)/shard_map/near_own/pallas_call | solution.py:207
  50.8 6.0 %near_pair.1.refs_10_.refs_11_ = f32[4,256,512]{2,1,0:T(8,128)S(1)} custom-call(f32[88,1024]{1,0:T(8,128)S(1)} %copy-done.2, f32[88,1024]{1,0:T(8,128)S(1)} %collective-permute-done.3.refs_1_, f32[88,1024]{1,0:T(8,128)S(1)} %collective-permute-done.4.refs_2_, f32[88,1024]{1,0:T(8,128)S(1)} %collective-permute-done.5.refs_3_, ...), custom_call_target="tpu_custom_call" | custom-call | tf_op jit(solution)/shard_map/near_pair/pallas_call | solution.py:207
  59.3 3.1 %collective-permute-start.11 = (f32[4,96,256]{2,1,0:T(8,128)S(1)}, f32[4,96,256]{2,1,0:T(8,128)S(1)}, u32[]{:S(2)}, u32[]{:S(2)}) collective-permute-start(f32[4,96,256]{2,1,0:T(8,128)S(1)} %stack.2.alike_ref.refs_11_), channel_id=1, source_target_pairs={{0,4},{4,0},{8,12},{12,8},{16,20},{20,16},{24,28},{28,24},{1,5},{5... | collective-permute-start | bytes 1179656 | tf_op jit(solution)/shard_map/ppermute | solution.py:589
  62.5 3.6 %collective-permute-start.18 = (f32[128,1024]{1,0:T(8,128)S(1)}, f32[128,1024]{1,0:T(8,128)S(1)}, u32[]{:S(2)}, u32[]{:S(2)}) collective-permute-start(f32[128,1024]{1,0:T(8,128)S(1)} %add_parts.4), channel_id=1, source_target_pairs={{2,0},{3,1},{0,2},{1,3},{6,4},{7,5},{4,6},{5,7},{10,8},{11,9},{8,1... | collective-permute-start | bytes 1572872 | tf_op jit(solution)/shard_map/ppermute | solution.py:549
  66.3 6.1 %near_home.1 = (f32[128,1024]{1,0:T(8,128)S(1)}, f32[128,1024]{1,0:T(8,128)S(1)}, f32[128,1024]{1,0:T(8,128)S(1)}, f32[128,1024]{1,0:T(8,128)S(1)}) custom-call(f32[88,1024]{1,0:T(8,128)S(1)} %copy-done.2, f32[88,1024]{1,0:T(8,128)S(1)} %collective-permute-done.3.refs_1_, f32[88,1024]{1,0:T(8,128)S(1)} %collective-permute-done.4.refs_2_, ...), custom_call_target="tpu_custom_call" | custom-call | tf_op jit(solution)/shard_map/near_home/pallas_call | solution.py:207
  73.3 2.2 %collective-permute-done.12.mate_ref = f32[8,32,256]{2,1,0:T(8,128)S(1)} collective-permute-done((f32[8,32,256]{2,1,0:T(8,128)S(1)}, f32[8,32,256]{2,1,0:T(8,128)S(1)}, u32[]{:S(2)}, u32[]{:S(2)}) %collective-permute-start.12) | collective-permute-done | bytes 262176 | tf_op jit(solution)/shard_map/ppermute | solution.py:546
  75.5 5.9 %far.1.refs_0_ = f32[64,256]{1,0:T(8,128)S(1)} custom-call(s32[4,14]{1,0:T(4,128)S(1)} %bitcast.1, s32[6,256]{1,0:T(8,128)S(1)} %copy-done.6, f32[6,512,256]{2,1,0:T(8,128)S(1)} %copy-done.4, f32[4,96,256]{2,1,0:T(8,128)S(1)} %stack.2.alike_ref.refs_11_, f32[4,96,256]{2,1,0:T(8,128)S(1)} %collective-permute-done.11.beside_ref, ...), custom_call_target="tpu_custom_call" | custom-call | tf_op jit(solution)/shard_map/far/pallas_call | solution.py:465
  82.8 1.5 %collective-permute-start.16 = (f32[2,64,256]{2,1,0:T(8,128)S(1)}, f32[2,64,256]{2,1,0:T(8,128)S(1)}, u32[]{:S(2)}, u32[]{:S(2)}) collective-permute-start(f32[2,64,256]{2,1,0:T(8,128)S(1)} %stack.3.refs_0_), channel_id=1, source_target_pairs={{2,0},{3,1},{0,2},{1,3},{6,4},{7,5},{4,6},{5,7},{10,8},{11,9},{8,1... | collective-permute-start | bytes 393224 | tf_op jit(solution)/shard_map/ppermute | solution.py:546
  84.3 5.8 %collective-permute-done.19.refs_3_ = f32[128,1024]{1,0:T(8,128)S(1)} collective-permute-done((f32[128,1024]{1,0:T(8,128)S(1)}, f32[128,1024]{1,0:T(8,128)S(1)}, u32[]{:S(2)}, u32[]{:S(2)}) %collective-permute-start.19) | collective-permute-done | bytes 524320 | tf_op jit(solution)/shard_map/ppermute | solution.py:549
  90.2 1.8 %collective-permute-done.16.refs_1_ = f32[2,64,256]{2,1,0:T(8,128)S(1)} collective-permute-done((f32[2,64,256]{2,1,0:T(8,128)S(1)}, f32[2,64,256]{2,1,0:T(8,128)S(1)}, u32[]{:S(2)}, u32[]{:S(2)}) %collective-permute-start.16) | collective-permute-done | bytes 131104 | tf_op jit(solution)/shard_map/ppermute | solution.py:546
  92.0 1.6 %join.1 = f32[256,1024]{1,0:T(8,128)} custom-call(f32[2,512,256]{2,1,0:T(8,128)S(1)} %copy-done.3, f32[2,64,256]{2,1,0:T(8,128)S(1)} %stack.3.refs_0_, f32[2,64,256]{2,1,0:T(8,128)S(1)} %collective-permute-done.16.refs_1_, f32[128,1024]{1,0:T(8,128)S(1)} %get-tuple-element.55.refs_2_, f32[128,1024]{1,0:T(8,128)S(1)} %get-tuple-element.56.refs_3_, ...), custom_call_target="tpu_custom_call" | custom-call | tf_op jit(solution)/shard_map/join/pallas_call | solution.py:522
  (55 shorter events, 8.3 us)
Async XLA Ops:
  0.0 11.5 %collective-permute-start = (f32[64,1024]{1,0:T(8,128)}, f32[64,1024]{1,0:T(8,128)}, u32[]{:S(2)}, u32[]{:S(2)}) collective-permute-start(f32[64,1024]{1,0:T(8,128)} %refs_6_.1), channel_id=1, source_target_pairs={{0,4},{4,0},{8,12},{12,8},{16,20},{20,16},{24,28},{28,24},{1,5},{5... | collective-permute-start | bytes 786440 | tf_op jit(solution)/shard_map/ppermute | solution.py:560
  5.3 16.4 %collective-permute-start.2 = (f32[128,1024]{1,0:T(8,128)}, f32[128,1024]{1,0:T(8,128)}, u32[]{:S(2)}, u32[]{:S(2)}) collective-permute-start(f32[128,1024]{1,0:T(8,128)} %get-tuple-element.60), channel_id=1, source_target_pairs={{0,4},{4,0},{8,12},{12,8},{16,20},{20,16},{24,28},{28,24},{1,5},{5... | collective-permute-start | bytes 1572872 | tf_op jit(solution)/shard_map/ppermute | solution.py:561
  9.3 5.9 %collective-permute-start.3 = (f32[88,1024]{1,0:T(8,128)}, f32[88,1024]{1,0:T(8,128)S(1)}, u32[]{:S(2)}, u32[]{:S(2)}) collective-permute-start(f32[88,1024]{1,0:T(8,128)} %get-tuple-element.33), channel_id=1, source_target_pairs={{1,0},{0,1},{3,2},{2,3},{5,4},{4,5},{7,6},{6,7},{9,8},{8,9},{11,10... | collective-permute-start | bytes 1081352 | tf_op jit(solution)/shard_map/ppermute | solution.py:564
  9.4 16.5 %collective-permute-start.4 = (f32[88,1024]{1,0:T(8,128)}, f32[88,1024]{1,0:T(8,128)S(1)}, u32[]{:S(2)}, u32[]{:S(2)}) collective-permute-start(f32[88,1024]{1,0:T(8,128)} %get-tuple-element.35), channel_id=1, source_target_pairs={{2,0},{3,1},{0,2},{1,3},{6,4},{7,5},{4,6},{5,7},{10,8},{11,9},{8,1... | collective-permute-start | bytes 1081352 | tf_op jit(solution)/shard_map/ppermute | solution.py:564
  11.5 16.7 %collective-permute-start.5 = (f32[88,1024]{1,0:T(8,128)}, f32[88,1024]{1,0:T(8,128)S(1)}, u32[]{:S(2)}, u32[]{:S(2)}) collective-permute-start(f32[88,1024]{1,0:T(8,128)} %get-tuple-element.36), channel_id=1, source_target_pairs={{3,0},{2,1},{1,2},{0,3},{7,4},{6,5},{5,6},{4,7},{11,8},{10,9},{9,1... | collective-permute-start | bytes 1081352 | tf_op jit(solution)/shard_map/ppermute | solution.py:564
  11.5 10.1 %collective-permute-start.1 = (f32[64,1024]{1,0:T(8,128)}, f32[64,1024]{1,0:T(8,128)S(1)}, u32[]{:S(2)}, u32[]{:S(2)}) collective-permute-start(f32[64,1024]{1,0:T(8,128)} %collective-permute-done.refs_6_), channel_id=1, source_target_pairs={{0,8},{8,16},{16,24},{12,4},{20,12},{28,20},{1,9},{9,17},{17,25},{... | collective-permute-start | bytes 786440 | tf_op jit(solution)/shard_map/ppermute | solution.py:568
  15.3 16.7 %collective-permute-start.10 = (f32[128,1024]{1,0:T(8,128)}, f32[128,1024]{1,0:T(8,128)S(1)}, u32[]{:S(2)}, u32[]{:S(2)}) collective-permute-start(f32[128,1024]{1,0:T(8,128)} %get-tuple-element.59), channel_id=1, source_target_pairs={{0,4},{4,0},{8,12},{12,8},{16,20},{20,16},{24,28},{28,24},{1,5},{5... | collective-permute-start | bytes 1572872 | tf_op jit(solution)/shard_map/ppermute | solution.py:561
  21.6 35.1 %collective-permute-start.9 = (f32[128,1024]{1,0:T(8,128)}, f32[128,1024]{1,0:T(8,128)S(1)}, u32[]{:S(2)}, u32[]{:S(2)}) collective-permute-start(f32[128,1024]{1,0:T(8,128)} %collective-permute-done.2.refs_7_), channel_id=1, source_target_pairs={{0,8},{8,16},{16,24},{12,4},{20,12},{28,20},{1,9},{9,17},{17,25},{... | collective-permute-start | bytes 1572872 | tf_op jit(solution)/shard_map/ppermute | solution.py:570
  29.8 10.9 %copy-start.5 = (f32[64,1024]{1,0:T(8,128)S(1)}, f32[64,1024]{1,0:T(8,128)}, u32[]{:S(2)}) copy-start(f32[64,1024]{1,0:T(8,128)} %refs_6_.1) | copy-start | bytes 786436
  32.0 25.8 %collective-permute-start.13 = (f32[128,1024]{1,0:T(8,128)S(1)}, f32[128,1024]{1,0:T(8,128)S(1)}, u32[]{:S(2)}, u32[]{:S(2)}) collective-permute-start(f32[128,1024]{1,0:T(8,128)S(1)} %collective-permute-done.10.refs_8_), channel_id=1, source_target_pairs={{0,8},{8,16},{16,24},{12,4},{20,12},{28,20},{1,9},{9,17},{17,25},{... | collective-permute-start | bytes 1572872 | tf_op jit(solution)/shard_map/ppermute | solution.py:580
  35.7 22.0 %collective-permute-start.6 = (f32[96,256]{1,0:T(8,128)S(1)}, f32[96,256]{1,0:T(8,128)S(1)}, u32[]{:S(2)}, u32[]{:S(2)}) collective-permute-start(f32[96,256]{1,0:T(8,128)S(1)} %get-tuple-element.47.refs_0_), channel_id=1, source_target_pairs={{0,8},{4,12},{8,0},{12,4},{16,24},{20,28},{24,16},{28,20},{1,9},{5... | collective-permute-start | bytes 294920 | tf_op jit(solution)/shard_map/ppermute | solution.py:575
  37.3 20.4 %collective-permute-start.7 = (f32[96,256]{1,0:T(8,128)S(1)}, f32[96,256]{1,0:T(8,128)S(1)}, u32[]{:S(2)}, u32[]{:S(2)}) collective-permute-start(f32[96,256]{1,0:T(8,128)S(1)} %get-tuple-element.47.refs_0_), channel_id=1, source_target_pairs={{0,16},{4,20},{8,24},{12,28},{16,0},{20,4},{24,8},{28,12},{1,17},{... | collective-permute-start | bytes 294920 | tf_op jit(solution)/shard_map/ppermute | solution.py:575
  38.4 19.3 %collective-permute-start.8 = (f32[96,256]{1,0:T(8,128)S(1)}, f32[96,256]{1,0:T(8,128)S(1)}, u32[]{:S(2)}, u32[]{:S(2)}) collective-permute-start(f32[96,256]{1,0:T(8,128)S(1)} %get-tuple-element.47.refs_0_), channel_id=1, source_target_pairs={{0,24},{4,28},{8,16},{12,20},{16,8},{20,12},{24,0},{28,4},{1,25},{... | collective-permute-start | bytes 294920 | tf_op jit(solution)/shard_map/ppermute | solution.py:575
  57.6 4.8 %collective-permute-start.17 = (f32[128,1024]{1,0:T(8,128)S(1)}, f32[128,1024]{1,0:T(8,128)S(1)}, u32[]{:S(2)}, u32[]{:S(2)}) collective-permute-start(f32[128,1024]{1,0:T(8,128)S(1)} %get-tuple-element.46), channel_id=1, source_target_pairs={{1,0},{0,1},{3,2},{2,3},{5,4},{4,5},{7,6},{6,7},{9,8},{8,9},{11,10... | collective-permute-start | bytes 1572872 | tf_op jit(solution)/shard_map/ppermute | solution.py:546
  58.8 7.3 %collective-permute-start.14 = (f32[128,1024]{1,0:T(8,128)S(1)}, f32[128,1024]{1,0:T(8,128)S(1)}, u32[]{:S(2)}, u32[]{:S(2)}) collective-permute-start(f32[128,1024]{1,0:T(8,128)S(1)} %get-tuple-element.52), channel_id=1, source_target_pairs={{1,0},{0,1},{3,2},{2,3},{5,4},{4,5},{7,6},{6,7},{9,8},{8,9},{11,10... | collective-permute-start | bytes 1572872 | tf_op jit(solution)/shard_map/ppermute | solution.py:546
  59.3 13.7 %collective-permute-start.11 = (f32[4,96,256]{2,1,0:T(8,128)S(1)}, f32[4,96,256]{2,1,0:T(8,128)S(1)}, u32[]{:S(2)}, u32[]{:S(2)}) collective-permute-start(f32[4,96,256]{2,1,0:T(8,128)S(1)} %stack.2.alike_ref.refs_11_), channel_id=1, source_target_pairs={{0,4},{4,0},{8,12},{12,8},{16,20},{20,16},{24,28},{28,24},{1,5},{5... | collective-permute-start | bytes 1179656 | tf_op jit(solution)/shard_map/ppermute | solution.py:589
  62.5 21.8 %collective-permute-start.18 = (f32[128,1024]{1,0:T(8,128)S(1)}, f32[128,1024]{1,0:T(8,128)S(1)}, u32[]{:S(2)}, u32[]{:S(2)}) collective-permute-start(f32[128,1024]{1,0:T(8,128)S(1)} %add_parts.4), channel_id=1, source_target_pairs={{2,0},{3,1},{0,2},{1,3},{6,4},{7,5},{4,6},{5,7},{10,8},{11,9},{8,1... | collective-permute-start | bytes 1572872 | tf_op jit(solution)/shard_map/ppermute | solution.py:549
  66.2 23.9 %collective-permute-start.19 = (f32[128,1024]{1,0:T(8,128)S(1)}, f32[128,1024]{1,0:T(8,128)S(1)}, u32[]{:S(2)}, u32[]{:S(2)}) collective-permute-start(f32[128,1024]{1,0:T(8,128)S(1)} %add_parts.3.refs_14_), channel_id=1, source_target_pairs={{2,0},{3,1},{0,2},{1,3},{6,4},{7,5},{4,6},{5,7},{10,8},{11,9},{8,1... | collective-permute-start | bytes 1572872 | tf_op jit(solution)/shard_map/ppermute | solution.py:549
  72.4 19.6 %collective-permute-start.20 = (f32[128,1024]{1,0:T(8,128)S(1)}, f32[128,1024]{1,0:T(8,128)S(1)}, u32[]{:S(2)}, u32[]{:S(2)}) collective-permute-start(f32[128,1024]{1,0:T(8,128)S(1)} %get-tuple-element.57), channel_id=1, source_target_pairs={{1,0},{0,1},{3,2},{2,3},{5,4},{4,5},{7,6},{6,7},{9,8},{8,9},{11,10... | collective-permute-start | bytes 1572872 | tf_op jit(solution)/shard_map/ppermute | solution.py:546
  72.7 19.3 %collective-permute-start.21 = (f32[128,1024]{1,0:T(8,128)S(1)}, f32[128,1024]{1,0:T(8,128)S(1)}, u32[]{:S(2)}, u32[]{:S(2)}) collective-permute-start(f32[128,1024]{1,0:T(8,128)S(1)} %get-tuple-element.58), channel_id=1, source_target_pairs={{1,0},{0,1},{3,2},{2,3},{5,4},{4,5},{7,6},{6,7},{9,8},{8,9},{11,10... | collective-permute-start | bytes 1572872 | tf_op jit(solution)/shard_map/ppermute | solution.py:546
  73.0 2.5 %collective-permute-start.12 = (f32[8,32,256]{2,1,0:T(8,128)S(1)}, f32[8,32,256]{2,1,0:T(8,128)S(1)}, u32[]{:S(2)}, u32[]{:S(2)}) collective-permute-start(f32[8,32,256]{2,1,0:T(8,128)S(1)} %points_of.1), channel_id=1, source_target_pairs={{1,0},{0,1},{3,2},{2,3},{5,4},{4,5},{7,6},{6,7},{9,8},{8,9},{11,10... | collective-permute-start | bytes 786440 | tf_op jit(solution)/shard_map/ppermute | solution.py:546
  75.5 16.5 %copy-start.3 = (f32[2,512,256]{2,1,0:T(8,128)S(1)}, f32[2,512,256]{2,1,0:T(8,128)}, u32[]{:S(2)}) copy-start(f32[2,512,256]{2,1,0:T(8,128)} %interp_ref.1) | copy-start | bytes 3145732
  81.5 1.3 %collective-permute-start.15 = (f32[64,256]{1,0:T(8,128)S(1)}, f32[64,256]{1,0:T(8,128)S(1)}, u32[]{:S(2)}, u32[]{:S(2)}) collective-permute-start(f32[64,256]{1,0:T(8,128)S(1)} %far.1.refs_0_), channel_id=1, source_target_pairs={{1,0},{0,1},{3,2},{2,3},{5,4},{4,5},{7,6},{6,7},{9,8},{8,9},{11,10... | collective-permute-start | bytes 196616 | tf_op jit(solution)/shard_map/ppermute | solution.py:546
  82.8 9.2 %collective-permute-start.16 = (f32[2,64,256]{2,1,0:T(8,128)S(1)}, f32[2,64,256]{2,1,0:T(8,128)S(1)}, u32[]{:S(2)}, u32[]{:S(2)}) collective-permute-start(f32[2,64,256]{2,1,0:T(8,128)S(1)} %stack.3.refs_0_), channel_id=1, source_target_pairs={{2,0},{3,1},{0,2},{1,3},{6,4},{7,5},{4,6},{5,7},{10,8},{11,9},{8,1... | collective-permute-start | bytes 393224 | tf_op jit(solution)/shard_map/ppermute | solution.py:546
  (7 other events, 51.5 us)

commit v6 on v5

--- a/solution.py
+++ b/solution.py
@@ -62,12 +62,12 @@
 
 
 def near_body(
-    xs, sets, leaves_at, rows, row, nacc, nout, *refs
+    xs, sets, leaves_at, rows, row, nacc, nout, apart, *refs
 ):
     nset = len(sets)
     start, stop = leaves_at
     msgs, (t_ref, tb_ref), refs = refs[: 2 * xs], refs[2 * xs : 2 * xs + 2], refs[2 * xs + 2 :]
-    if nacc:
+    if apart:
         s_scr, sb_scr, w_scr, o_scr, k_scr, times_scr, list_ref, times_ref, sems = refs[-9:]
         outs = refs[-9 - nout : -9]
     else:
@@ -170,7 +170,7 @@
         return carry
 
     lax.fori_loop(0, (count + 1) // 2, pair, jnp.int32(0))
-    if nacc:
+    if apart:
         t, top = 0, 0
         for ref in outs:
             tall = ref.shape[0]
@@ -180,7 +180,7 @@
             t, top = (t, top + tall) if top + tall < rows else (t + 2, 0)
 
 
-def near_call(name, msgs, targets, leaves_at, sources, rows, row=0, acc=(), after=()):
+def near_call(name, msgs, targets, leaves_at, sources, rows, row=0, acc=(), after=(), apart=None):
     nset = len(sources)
     start, stop = leaves_at
     vmem = pl.BlockSpec(memory_space=pltpu.VMEM)
@@ -196,7 +196,8 @@
         pltpu.SMEM((len(msgs), EXTRA, 128), F32),
         pltpu.SemaphoreType.DMA((len(msgs),)),
     ]
-    if not acc:
+    apart = bool(acc) if apart is None else apart
+    if not apart:
         out = [jax.ShapeDtypeStruct((stop - start, rows, LEAF), F32)]
         scratch.pop(3)
     else:
@@ -206,7 +207,7 @@
     sets = tuple((kind, len(heads) - 1, len(chunks)) for kind, heads, chunks in sources)
     return pl.pallas_call(
         partial(
-            near_body, len(msgs) // 2, sets, leaves_at, rows, row, len(acc), len(out)
+            near_body, len(msgs) // 2, sets, leaves_at, rows, row, len(acc), len(out), apart
         ),
         name=name,
         out_shape=out,
@@ -575,8 +576,9 @@
         pieces.append(lax.ppermute(payload, "leaf", [(i, i ^ mask) for i in range(groups)]))
 
     payload, w_y[1] = together(payload, w_y[1])
-    every, away, home = (0, 2 * helpers), (4, 2 * helpers), (0, 4)
-    (own,) = near_call("near_own", msgs, targets, every, [("own", (points,), [weights])], R)
+    away, home = (4, 2 * helpers), (0, 4)
+    own_src = ("own", (points,), [weights])
+    (own,) = near_call("near_own", msgs, targets, away, [own_src], R)
     w_z.append(lax.ppermute(w_y[1], "leaf", across))
     pair_src = ("pair", (pts_y,), w_y)
     (pair,) = near_call("near_pair", msgs, targets, away, [pair_src], R, after=[own])
@@ -599,8 +601,8 @@
         kept, mates = sums[c]
         both = add_call(*zip(kept, mates))
         parts.append([to_help(value, dx + 1) for dx, value in enumerate(both)])
-    sources = [pair_src, ("next", z_side, w_z)]
-    home = near_call("near_home", msgs, targets, home, sources, R, 0, [own], both[:1])
+    sources = [own_src, pair_src, ("next", z_side, w_z)]
+    home = near_call("near_home", msgs, targets, home, sources, R, after=both[:1], apart=True)
     swapped = from_help(points_call(alike, side), 0, 1)
     v_own = far_call(groups, far_nodes, skel_node, transfer, alike, side, swapped, home[:1])
     v_pair = stack_call([v_own, from_help(v_own, 0, 1)])

time: 93.5 us -> 98.5 us (1.053)
  starting transfers between devices: 31.6 us -> 37.5 us
  waiting for transfers between devices: 20.6 us -> 17.1 us
  Pallas kernels: 37.2 us -> 39.9 us
    ppermute x2, waiting for transfers between devices: 5.77 us -> 0.01 us  [to_help(): return lax.ppermute(value, 'help', help_pairs(xs, -dx, 0))]
    ppermute x7, starting transfers between devices: 3.34 us -> 8.09 us  [from_help(): return lax.ppermute(value, 'help', help_pairs(xs, dx, dc))]
    ppermute x1, starting transfers between devices: 3.11 us -> 5.77 us  [shards(): side = lax.ppermute(alike, 'leaf', beside)]
    pallas_call x5, Pallas kernels: 24 us -> 26.3 us  [near_call(): pl.pallas_call(partial(near_body, len(msgs) // 2, sets, leaves_at, rows,...]
    ppermute x7, waiting for transfers between devices: 4.99 us -> 7.17 us  [from_help(): return lax.ppermute(value, 'help', help_pairs(xs, dx, dc))]
    ppermute x2, starting transfers between devices: 3.69 us -> 2.19 us  [to_help(): return lax.ppermute(value, 'help', help_pairs(xs, -dx, 0))]
  transfers between devices with their start and end apart: 22 -> 22, of which waited for: 7 -> 6; matrix products, arithmetic and copies ran while one was open for 2% -> 2% of each run, Pallas kernels for 38% -> 39%
where the time goes in v6:
time: 98.5 us; the launch traced here: 98.7 us
  Pallas kernels  39.9 us (41%)
  starting transfers between devices  37.5 us (38%)
  waiting for transfers between devices  17.1 us (17%)
  local copies, waits for them, and re-layouts  3.98 us (4%)
    pallas_call x5, Pallas kernels, near_call(): pl.pallas_call(partial(near_body, len(msgs) // 2, sets, leaves_at, rows,...  26.3 us
    ppermute x7, starting transfers between devices, from_help(): return lax.ppermute(value, 'help', help_pairs(xs, dx, dc))  8.09 us
    ppermute x7, waiting for transfers between devices, from_help(): return lax.ppermute(value, 'help', help_pairs(xs, dx, dc))  7.17 us
    pallas_call x1, Pallas kernels, far_call(): pl.pallas_call(partial(far_body, groups, rows), name='far', out_shape=jax...  6.39 us
    ppermute x1, waiting for transfers between devices, shards(): pts_z = lax.ppermute(pts_y, 'leaf', across)  6.27 us
    ppermute x1, starting transfers between devices, shards(): side = lax.ppermute(alike, 'leaf', beside)  5.77 us
    ppermute x3, starting transfers between devices, shards(): lax.ppermute(payload, 'leaf', [(i, i ^ mask) for i in range(groups)])  4.45 us
    ppermute x1, starting transfers between devices, shards(): w_z = [lax.ppermute(w_y[0], 'leaf', across)]  4.27 us
  transfers between devices with their start and end apart: 22, of which 6 were waited for; matrix products, arithmetic and copies ran while one was open for 2% of the time, Pallas kernels for 39%

profile of v6, /device:TPU:0, one launch (start us, length us, event | category | flops | bytes accessed | tf_op | source)
XLA Modules:
  0.0 98.7 jit_solution(1150817692875209709)
XLA Ops:
  0.0 3.0 %collective-permute-start = (f32[64,1024]{1,0:T(8,128)}, f32[64,1024]{1,0:T(8,128)}, u32[]{:S(2)}, u32[]{:S(2)}) collective-permute-start(f32[64,1024]{1,0:T(8,128)} %refs_6_.3), channel_id=1, source_target_pairs={{0,4},{4,0},{8,12},{12,8},{16,20},{20,16},{24,28},{28,24},{1,5},{5... | collective-permute-start | bytes 786440 | tf_op jit(solution)/shard_map/ppermute | solution.py:561
  3.0 2.3 %fusion = (f32[128,1024]{1,0:T(8,128)}, f32[128,1024]{1,0:T(8,128)}) fusion(f32[256,1024]{1,0:T(8,128)} %refs_7_.3), kind=kLoop, calls=%fused_computation | loop fusion | bytes 2097152 | tf_op jit(solution)/shard_map/slice | solution.py:562
  5.3 4.1 %leaf_up.1 = (f32[88,1024]{1,0:T(8,128)}, f32[88,1024]{1,0:T(8,128)}, f32[88,1024]{1,0:T(8,128)}, f32[88,1024]{1,0:T(8,128)}) custom-call(s32[1,2]{1,0:T(1,128)} %count_ref.1, s32[2,32]{1,0:T(2,128)} %src_ref.1, f32[64,1024]{1,0:T(8,128)} %refs_6_.3, f32[256,1024]{1,0:T(8,128)} %refs_7_.3, f32[2,512,256]{2,1,0:T(8,128)} %interp_ref.1), custom_call_target="tpu_custom_call" | custom-call | tf_op jit(solution)/shard_map/leaf_up/pallas_call | solution.py:299
  9.4 2.1 %collective-permute-start.4 = (f32[88,1024]{1,0:T(8,128)}, f32[88,1024]{1,0:T(8,128)S(1)}, u32[]{:S(2)}, u32[]{:S(2)}) collective-permute-start(f32[88,1024]{1,0:T(8,128)} %get-tuple-element.35), channel_id=1, source_target_pairs={{2,0},{3,1},{0,2},{1,3},{6,4},{7,5},{4,6},{5,7},{10,8},{11,9},{8,1... | collective-permute-start | bytes 1081352 | tf_op jit(solution)/shard_map/ppermute | solution.py:565
  11.5 3.7 %collective-permute-start.1 = (f32[64,1024]{1,0:T(8,128)}, f32[64,1024]{1,0:T(8,128)S(1)}, u32[]{:S(2)}, u32[]{:S(2)}) collective-permute-start(f32[64,1024]{1,0:T(8,128)} %collective-permute-done.refs_6_.refs_8_), channel_id=1, source_target_pairs={{0,8},{8,16},{16,24},{12,4},{20,12},{28,20},{1,9},{9,17},{17,25},{... | collective-permute-start | bytes 786440 | tf_op jit(solution)/shard_map/ppermute | solution.py:569
  15.3 6.3 %collective-permute-done.1.pts_ref = f32[64,1024]{1,0:T(8,128)S(1)} collective-permute-done((f32[64,1024]{1,0:T(8,128)}, f32[64,1024]{1,0:T(8,128)S(1)}, u32[]{:S(2)}, u32[]{:S(2)}) %collective-permute-start.1) | collective-permute-done | bytes 262176 | tf_op jit(solution)/shard_map/ppermute | solution.py:569
  21.6 4.3 %collective-permute-start.9 = (f32[128,1024]{1,0:T(8,128)}, f32[128,1024]{1,0:T(8,128)S(1)}, u32[]{:S(2)}, u32[]{:S(2)}) collective-permute-start(f32[128,1024]{1,0:T(8,128)} %collective-permute-done.2.refs_7_.refs_9_), channel_id=1, source_target_pairs={{0,8},{8,16},{16,24},{12,4},{20,12},{28,20},{1,9},{9,17},{17,25},{... | collective-permute-start | bytes 1572872 | tf_op jit(solution)/shard_map/ppermute | solution.py:571
  25.9 2.2 %collective-permute-done.5.refs_3_ = f32[88,1024]{1,0:T(8,128)S(1)} collective-permute-done((f32[88,1024]{1,0:T(8,128)}, f32[88,1024]{1,0:T(8,128)S(1)}, u32[]{:S(2)}, u32[]{:S(2)}) %collective-permute-start.5) | collective-permute-done | bytes 360480 | tf_op jit(solution)/shard_map/ppermute | solution.py:565
  30.6 1.4 %collective-permute-done.10.refs_8_.refs_10_ = f32[128,1024]{1,0:T(8,128)S(1)} collective-permute-done((f32[128,1024]{1,0:T(8,128)}, f32[128,1024]{1,0:T(8,128)S(1)}, u32[]{:S(2)}, u32[]{:S(2)}) %collective-permute-start.10) | collective-permute-done | bytes 524320 | tf_op jit(solution)/shard_map/ppermute | solution.py:562
  32.0 3.7 %collective-permute-start.13 = (f32[128,1024]{1,0:T(8,128)S(1)}, f32[128,1024]{1,0:T(8,128)S(1)}, u32[]{:S(2)}, u32[]{:S(2)}) collective-permute-start(f32[128,1024]{1,0:T(8,128)S(1)} %collective-permute-done.10.refs_8_.refs_10_), channel_id=1, source_target_pairs={{0,8},{8,16},{16,24},{12,4},{20,12},{28,20},{1,9},{9,17},{17,25},{... | collective-permute-start | bytes 1572872 | tf_op jit(solution)/shard_map/ppermute | solution.py:582
  35.7 1.6 %collective-permute-start.6 = (f32[96,256]{1,0:T(8,128)S(1)}, f32[96,256]{1,0:T(8,128)S(1)}, u32[]{:S(2)}, u32[]{:S(2)}) collective-permute-start(f32[96,256]{1,0:T(8,128)S(1)} %get-tuple-element.47.refs_0_), channel_id=1, source_target_pairs={{0,8},{4,12},{8,0},{12,4},{16,24},{20,28},{24,16},{28,20},{1,9},{5... | collective-permute-start | bytes 294920 | tf_op jit(solution)/shard_map/ppermute | solution.py:576
  37.3 1.1 %collective-permute-start.7 = (f32[96,256]{1,0:T(8,128)S(1)}, f32[96,256]{1,0:T(8,128)S(1)}, u32[]{:S(2)}, u32[]{:S(2)}) collective-permute-start(f32[96,256]{1,0:T(8,128)S(1)} %get-tuple-element.47.refs_0_), channel_id=1, source_target_pairs={{0,16},{4,20},{8,24},{12,28},{16,0},{20,4},{24,8},{28,12},{1,17},{... | collective-permute-start | bytes 294920 | tf_op jit(solution)/shard_map/ppermute | solution.py:576
  38.4 1.7 %collective-permute-start.8 = (f32[96,256]{1,0:T(8,128)S(1)}, f32[96,256]{1,0:T(8,128)S(1)}, u32[]{:S(2)}, u32[]{:S(2)}) collective-permute-start(f32[96,256]{1,0:T(8,128)S(1)} %get-tuple-element.47.refs_0_), channel_id=1, source_target_pairs={{0,24},{4,28},{8,16},{12,20},{16,8},{20,12},{24,0},{28,4},{1,25},{... | collective-permute-start | bytes 294920 | tf_op jit(solution)/shard_map/ppermute | solution.py:576
  40.7 5.9 %near_own.1.refs_9_ = f32[4,256,512]{2,1,0:T(8,128)S(1)} custom-call(f32[88,1024]{1,0:T(8,128)S(1)} %copy-done.2, f32[88,1024]{1,0:T(8,128)S(1)} %collective-permute-done.3.refs_1_, f32[88,1024]{1,0:T(8,128)S(1)} %collective-permute-done.4.refs_2_, f32[88,1024]{1,0:T(8,128)S(1)} %collective-permute-done.5.refs_3_, ...), custom_call_target="tpu_custom_call" | custom-call | tf_op jit(solution)/shard_map/near_own/pallas_call | solution.py:208
  46.6 7.5 %near_pair.1.refs_10_.refs_11_ = f32[4,256,512]{2,1,0:T(8,128)S(1)} custom-call(f32[88,1024]{1,0:T(8,128)S(1)} %copy-done.2, f32[88,1024]{1,0:T(8,128)S(1)} %collective-permute-done.3.refs_1_, f32[88,1024]{1,0:T(8,128)S(1)} %collective-permute-done.4.refs_2_, f32[88,1024]{1,0:T(8,128)S(1)} %collective-permute-done.5.refs_3_, ...), custom_call_target="tpu_custom_call" | custom-call | tf_op jit(solution)/shard_map/near_pair/pallas_call | solution.py:208
  56.6 5.8 %collective-permute-start.11 = (f32[4,96,256]{2,1,0:T(8,128)S(1)}, f32[4,96,256]{2,1,0:T(8,128)S(1)}, u32[]{:S(2)}, u32[]{:S(2)}) collective-permute-start(f32[4,96,256]{2,1,0:T(8,128)S(1)} %stack.2.alike_ref.refs_11_), channel_id=1, source_target_pairs={{0,4},{4,0},{8,12},{12,8},{16,20},{20,16},{24,28},{28,24},{1,5},{5... | collective-permute-start | bytes 1179656 | tf_op jit(solution)/shard_map/ppermute | solution.py:591
  62.5 2.1 %collective-permute-start.18 = (f32[128,1024]{1,0:T(8,128)S(1)}, f32[128,1024]{1,0:T(8,128)S(1)}, u32[]{:S(2)}, u32[]{:S(2)}) collective-permute-start(f32[128,1024]{1,0:T(8,128)S(1)} %add_parts.4), channel_id=1, source_target_pairs={{2,0},{3,1},{0,2},{1,3},{6,4},{7,5},{4,6},{5,7},{10,8},{11,9},{8,1... | collective-permute-start | bytes 1572872 | tf_op jit(solution)/shard_map/ppermute | solution.py:550
  64.8 11.1 %near_home.1 = (f32[128,1024]{1,0:T(8,128)S(1)}, f32[128,1024]{1,0:T(8,128)S(1)}, f32[128,1024]{1,0:T(8,128)S(1)}, f32[128,1024]{1,0:T(8,128)S(1)}) custom-call(f32[88,1024]{1,0:T(8,128)S(1)} %copy-done.2, f32[88,1024]{1,0:T(8,128)S(1)} %collective-permute-done.3.refs_1_, f32[88,1024]{1,0:T(8,128)S(1)} %collective-permute-done.4.refs_2_, ...), custom_call_target="tpu_custom_call" | custom-call | tf_op jit(solution)/shard_map/near_home/pallas_call | solution.py:208
  76.6 2.4 %collective-permute-done.12.mate_ref = f32[8,32,256]{2,1,0:T(8,128)S(1)} collective-permute-done((f32[8,32,256]{2,1,0:T(8,128)S(1)}, f32[8,32,256]{2,1,0:T(8,128)S(1)}, u32[]{:S(2)}, u32[]{:S(2)}) %collective-permute-start.12) | collective-permute-done | bytes 262176 | tf_op jit(solution)/shard_map/ppermute | solution.py:547
  79.0 6.4 %far.1.refs_0_ = f32[64,256]{1,0:T(8,128)S(1)} custom-call(s32[4,14]{1,0:T(4,128)S(1)} %bitcast.1, s32[6,256]{1,0:T(8,128)S(1)} %copy-done.6, f32[6,512,256]{2,1,0:T(8,128)S(1)} %copy-done.4, f32[4,96,256]{2,1,0:T(8,128)S(1)} %stack.2.alike_ref.refs_11_, f32[4,96,256]{2,1,0:T(8,128)S(1)} %collective-permute-done.11.beside_ref, ...), custom_call_target="tpu_custom_call" | custom-call | tf_op jit(solution)/shard_map/far/pallas_call | solution.py:466
  85.6 1.1 %collective-permute-done.15.refs_1_ = f32[64,256]{1,0:T(8,128)S(1)} collective-permute-done((f32[64,256]{1,0:T(8,128)S(1)}, f32[64,256]{1,0:T(8,128)S(1)}, u32[]{:S(2)}, u32[]{:S(2)}) %collective-permute-start.15) | collective-permute-done | bytes 65568 | tf_op jit(solution)/shard_map/ppermute | solution.py:547
  86.7 6.6 %collective-permute-start.16 = (f32[2,64,256]{2,1,0:T(8,128)S(1)}, f32[2,64,256]{2,1,0:T(8,128)S(1)}, u32[]{:S(2)}, u32[]{:S(2)}) collective-permute-start(f32[2,64,256]{2,1,0:T(8,128)S(1)} %stack.3.refs_0_), channel_id=1, source_target_pairs={{2,0},{3,1},{0,2},{1,3},{6,4},{7,5},{4,6},{5,7},{10,8},{11,9},{8,1... | collective-permute-start | bytes 393224 | tf_op jit(solution)/shard_map/ppermute | solution.py:547
  93.4 3.7 %collective-permute-done.16.refs_1_ = f32[2,64,256]{2,1,0:T(8,128)S(1)} collective-permute-done((f32[2,64,256]{2,1,0:T(8,128)S(1)}, f32[2,64,256]{2,1,0:T(8,128)S(1)}, u32[]{:S(2)}, u32[]{:S(2)}) %collective-permute-start.16) | collective-permute-done | bytes 131104 | tf_op jit(solution)/shard_map/ppermute | solution.py:547
  97.1 1.6 %join.1 = f32[256,1024]{1,0:T(8,128)} custom-call(f32[2,512,256]{2,1,0:T(8,128)S(1)} %copy-done.3, f32[2,64,256]{2,1,0:T(8,128)S(1)} %stack.3.refs_0_, f32[2,64,256]{2,1,0:T(8,128)S(1)} %collective-permute-done.16.refs_1_, f32[128,1024]{1,0:T(8,128)S(1)} %get-tuple-element.55.refs_2_, f32[128,1024]{1,0:T(8,128)S(1)} %get-tuple-element.56.refs_3_, ...), custom_call_target="tpu_custom_call" | custom-call | tf_op jit(solution)/shard_map/join/pallas_call | solution.py:523
  (55 shorter events, 7.0 us)
Async XLA Ops:
  0.0 11.5 %collective-permute-start = (f32[64,1024]{1,0:T(8,128)}, f32[64,1024]{1,0:T(8,128)}, u32[]{:S(2)}, u32[]{:S(2)}) collective-permute-start(f32[64,1024]{1,0:T(8,128)} %refs_6_.3), channel_id=1, source_target_pairs={{0,4},{4,0},{8,12},{12,8},{16,20},{20,16},{24,28},{28,24},{1,5},{5... | collective-permute-start | bytes 786440 | tf_op jit(solution)/shard_map/ppermute | solution.py:561
  5.3 16.4 %collective-permute-start.2 = (f32[128,1024]{1,0:T(8,128)}, f32[128,1024]{1,0:T(8,128)}, u32[]{:S(2)}, u32[]{:S(2)}) collective-permute-start(f32[128,1024]{1,0:T(8,128)} %get-tuple-element.60), channel_id=1, source_target_pairs={{0,4},{4,0},{8,12},{12,8},{16,20},{20,16},{24,28},{28,24},{1,5},{5... | collective-permute-start | bytes 1572872 | tf_op jit(solution)/shard_map/ppermute | solution.py:562
  9.3 5.9 %collective-permute-start.3 = (f32[88,1024]{1,0:T(8,128)}, f32[88,1024]{1,0:T(8,128)S(1)}, u32[]{:S(2)}, u32[]{:S(2)}) collective-permute-start(f32[88,1024]{1,0:T(8,128)} %get-tuple-element.33), channel_id=1, source_target_pairs={{1,0},{0,1},{3,2},{2,3},{5,4},{4,5},{7,6},{6,7},{9,8},{8,9},{11,10... | collective-permute-start | bytes 1081352 | tf_op jit(solution)/shard_map/ppermute | solution.py:565
  9.4 16.5 %collective-permute-start.4 = (f32[88,1024]{1,0:T(8,128)}, f32[88,1024]{1,0:T(8,128)S(1)}, u32[]{:S(2)}, u32[]{:S(2)}) collective-permute-start(f32[88,1024]{1,0:T(8,128)} %get-tuple-element.35), channel_id=1, source_target_pairs={{2,0},{3,1},{0,2},{1,3},{6,4},{7,5},{4,6},{5,7},{10,8},{11,9},{8,1... | collective-permute-start | bytes 1081352 | tf_op jit(solution)/shard_map/ppermute | solution.py:565
  11.5 16.7 %collective-permute-start.5 = (f32[88,1024]{1,0:T(8,128)}, f32[88,1024]{1,0:T(8,128)S(1)}, u32[]{:S(2)}, u32[]{:S(2)}) collective-permute-start(f32[88,1024]{1,0:T(8,128)} %get-tuple-element.36), channel_id=1, source_target_pairs={{3,0},{2,1},{1,2},{0,3},{7,4},{6,5},{5,6},{4,7},{11,8},{10,9},{9,1... | collective-permute-start | bytes 1081352 | tf_op jit(solution)/shard_map/ppermute | solution.py:565
  11.5 10.1 %collective-permute-start.1 = (f32[64,1024]{1,0:T(8,128)}, f32[64,1024]{1,0:T(8,128)S(1)}, u32[]{:S(2)}, u32[]{:S(2)}) collective-permute-start(f32[64,1024]{1,0:T(8,128)} %collective-permute-done.refs_6_.refs_8_), channel_id=1, source_target_pairs={{0,8},{8,16},{16,24},{12,4},{20,12},{28,20},{1,9},{9,17},{17,25},{... | collective-permute-start | bytes 786440 | tf_op jit(solution)/shard_map/ppermute | solution.py:569
  15.3 16.7 %collective-permute-start.10 = (f32[128,1024]{1,0:T(8,128)}, f32[128,1024]{1,0:T(8,128)S(1)}, u32[]{:S(2)}, u32[]{:S(2)}) collective-permute-start(f32[128,1024]{1,0:T(8,128)} %get-tuple-element.59), channel_id=1, source_target_pairs={{0,4},{4,0},{8,12},{12,8},{16,20},{20,16},{24,28},{28,24},{1,5},{5... | collective-permute-start | bytes 1572872 | tf_op jit(solution)/shard_map/ppermute | solution.py:562
  21.6 32.5 %collective-permute-start.9 = (f32[128,1024]{1,0:T(8,128)}, f32[128,1024]{1,0:T(8,128)S(1)}, u32[]{:S(2)}, u32[]{:S(2)}) collective-permute-start(f32[128,1024]{1,0:T(8,128)} %collective-permute-done.2.refs_7_.refs_9_), channel_id=1, source_target_pairs={{0,8},{8,16},{16,24},{12,4},{20,12},{28,20},{1,9},{9,17},{17,25},{... | collective-permute-start | bytes 1572872 | tf_op jit(solution)/shard_map/ppermute | solution.py:571
  32.0 23.1 %collective-permute-start.13 = (f32[128,1024]{1,0:T(8,128)S(1)}, f32[128,1024]{1,0:T(8,128)S(1)}, u32[]{:S(2)}, u32[]{:S(2)}) collective-permute-start(f32[128,1024]{1,0:T(8,128)S(1)} %collective-permute-done.10.refs_8_.refs_10_), channel_id=1, source_target_pairs={{0,8},{8,16},{16,24},{12,4},{20,12},{28,20},{1,9},{9,17},{17,25},{... | collective-permute-start | bytes 1572872 | tf_op jit(solution)/shard_map/ppermute | solution.py:582
  35.7 19.3 %collective-permute-start.6 = (f32[96,256]{1,0:T(8,128)S(1)}, f32[96,256]{1,0:T(8,128)S(1)}, u32[]{:S(2)}, u32[]{:S(2)}) collective-permute-start(f32[96,256]{1,0:T(8,128)S(1)} %get-tuple-element.47.refs_0_), channel_id=1, source_target_pairs={{0,8},{4,12},{8,0},{12,4},{16,24},{20,28},{24,16},{28,20},{1,9},{5... | collective-permute-start | bytes 294920 | tf_op jit(solution)/shard_map/ppermute | solution.py:576
  37.3 17.7 %collective-permute-start.7 = (f32[96,256]{1,0:T(8,128)S(1)}, f32[96,256]{1,0:T(8,128)S(1)}, u32[]{:S(2)}, u32[]{:S(2)}) collective-permute-start(f32[96,256]{1,0:T(8,128)S(1)} %get-tuple-element.47.refs_0_), channel_id=1, source_target_pairs={{0,16},{4,20},{8,24},{12,28},{16,0},{20,4},{24,8},{28,12},{1,17},{... | collective-permute-start | bytes 294920 | tf_op jit(solution)/shard_map/ppermute | solution.py:576
  38.4 16.7 %collective-permute-start.8 = (f32[96,256]{1,0:T(8,128)S(1)}, f32[96,256]{1,0:T(8,128)S(1)}, u32[]{:S(2)}, u32[]{:S(2)}) collective-permute-start(f32[96,256]{1,0:T(8,128)S(1)} %get-tuple-element.47.refs_0_), channel_id=1, source_target_pairs={{0,24},{4,28},{8,16},{12,20},{16,8},{20,12},{24,0},{28,4},{1,25},{... | collective-permute-start | bytes 294920 | tf_op jit(solution)/shard_map/ppermute | solution.py:576
  54.9 7.5 %collective-permute-start.17 = (f32[128,1024]{1,0:T(8,128)S(1)}, f32[128,1024]{1,0:T(8,128)S(1)}, u32[]{:S(2)}, u32[]{:S(2)}) collective-permute-start(f32[128,1024]{1,0:T(8,128)S(1)} %get-tuple-element.46), channel_id=1, source_target_pairs={{1,0},{0,1},{3,2},{2,3},{5,4},{4,5},{7,6},{6,7},{9,8},{8,9},{11,10... | collective-permute-start | bytes 1572872 | tf_op jit(solution)/shard_map/ppermute | solution.py:547
  56.1 8.5 %collective-permute-start.14 = (f32[128,1024]{1,0:T(8,128)S(1)}, f32[128,1024]{1,0:T(8,128)S(1)}, u32[]{:S(2)}, u32[]{:S(2)}) collective-permute-start(f32[128,1024]{1,0:T(8,128)S(1)} %get-tuple-element.52), channel_id=1, source_target_pairs={{1,0},{0,1},{3,2},{2,3},{5,4},{4,5},{7,6},{6,7},{9,8},{8,9},{11,10... | collective-permute-start | bytes 1572872 | tf_op jit(solution)/shard_map/ppermute | solution.py:547
  56.6 19.8 %collective-permute-start.11 = (f32[4,96,256]{2,1,0:T(8,128)S(1)}, f32[4,96,256]{2,1,0:T(8,128)S(1)}, u32[]{:S(2)}, u32[]{:S(2)}) collective-permute-start(f32[4,96,256]{2,1,0:T(8,128)S(1)} %stack.2.alike_ref.refs_11_), channel_id=1, source_target_pairs={{0,4},{4,0},{8,12},{12,8},{16,20},{20,16},{24,28},{28,24},{1,5},{5... | collective-permute-start | bytes 1179656 | tf_op jit(solution)/shard_map/ppermute | solution.py:591
  62.5 30.8 %collective-permute-start.18 = (f32[128,1024]{1,0:T(8,128)S(1)}, f32[128,1024]{1,0:T(8,128)S(1)}, u32[]{:S(2)}, u32[]{:S(2)}) collective-permute-start(f32[128,1024]{1,0:T(8,128)S(1)} %add_parts.4), channel_id=1, source_target_pairs={{2,0},{3,1},{0,2},{1,3},{6,4},{7,5},{4,6},{5,7},{10,8},{11,9},{8,1... | collective-permute-start | bytes 1572872 | tf_op jit(solution)/shard_map/ppermute | solution.py:550
  64.6 14.4 %copy-start.6 = (s32[6,256]{1,0:T(8,128)S(1)}, s32[6,256]{1,0:T(8,128)}, u32[]{:S(2)}) copy-start(s32[6,256]{1,0:T(8,128)} %node_ref.1) | copy-start | bytes 18436
  64.7 14.3 %copy-start.7 = (s32[14,4]{0,1:T(4,128)S(1)}, s32[14,4]{0,1:T(4,128)}, u32[]{:S(2)}) copy-start(s32[14,4]{0,1:T(4,128)} %param.17) | copy-start | bytes 676
  64.7 28.6 %collective-permute-start.19 = (f32[128,1024]{1,0:T(8,128)S(1)}, f32[128,1024]{1,0:T(8,128)S(1)}, u32[]{:S(2)}, u32[]{:S(2)}) collective-permute-start(f32[128,1024]{1,0:T(8,128)S(1)} %add_parts.3.refs_15_), channel_id=1, source_target_pairs={{2,0},{3,1},{0,2},{1,3},{6,4},{7,5},{4,6},{5,7},{10,8},{11,9},{8,1... | collective-permute-start | bytes 1572872 | tf_op jit(solution)/shard_map/ppermute | solution.py:550
  75.9 21.2 %collective-permute-start.20 = (f32[128,1024]{1,0:T(8,128)S(1)}, f32[128,1024]{1,0:T(8,128)S(1)}, u32[]{:S(2)}, u32[]{:S(2)}) collective-permute-start(f32[128,1024]{1,0:T(8,128)S(1)} %get-tuple-element.57), channel_id=1, source_target_pairs={{1,0},{0,1},{3,2},{2,3},{5,4},{4,5},{7,6},{6,7},{9,8},{8,9},{11,10... | collective-permute-start | bytes 1572872 | tf_op jit(solution)/shard_map/ppermute | solution.py:547
  76.0 21.2 %collective-permute-start.21 = (f32[128,1024]{1,0:T(8,128)S(1)}, f32[128,1024]{1,0:T(8,128)S(1)}, u32[]{:S(2)}, u32[]{:S(2)}) collective-permute-start(f32[128,1024]{1,0:T(8,128)S(1)} %get-tuple-element.58), channel_id=1, source_target_pairs={{1,0},{0,1},{3,2},{2,3},{5,4},{4,5},{7,6},{6,7},{9,8},{8,9},{11,10... | collective-permute-start | bytes 1572872 | tf_op jit(solution)/shard_map/ppermute | solution.py:547
  76.5 2.5 %collective-permute-start.12 = (f32[8,32,256]{2,1,0:T(8,128)S(1)}, f32[8,32,256]{2,1,0:T(8,128)S(1)}, u32[]{:S(2)}, u32[]{:S(2)}) collective-permute-start(f32[8,32,256]{2,1,0:T(8,128)S(1)} %points_of.1), channel_id=1, source_target_pairs={{1,0},{0,1},{3,2},{2,3},{5,4},{4,5},{7,6},{6,7},{9,8},{8,9},{11,10... | collective-permute-start | bytes 786440 | tf_op jit(solution)/shard_map/ppermute | solution.py:547
  85.4 1.3 %collective-permute-start.15 = (f32[64,256]{1,0:T(8,128)S(1)}, f32[64,256]{1,0:T(8,128)S(1)}, u32[]{:S(2)}, u32[]{:S(2)}) collective-permute-start(f32[64,256]{1,0:T(8,128)S(1)} %far.1.refs_0_), channel_id=1, source_target_pairs={{1,0},{0,1},{3,2},{2,3},{5,4},{4,5},{7,6},{6,7},{9,8},{8,9},{11,10... | collective-permute-start | bytes 196616 | tf_op jit(solution)/shard_map/ppermute | solution.py:547
  86.7 10.4 %collective-permute-start.16 = (f32[2,64,256]{2,1,0:T(8,128)S(1)}, f32[2,64,256]{2,1,0:T(8,128)S(1)}, u32[]{:S(2)}, u32[]{:S(2)}) collective-permute-start(f32[2,64,256]{2,1,0:T(8,128)S(1)} %stack.3.refs_0_), channel_id=1, source_target_pairs={{2,0},{3,1},{0,2},{1,3},{6,4},{7,5},{4,6},{5,7},{10,8},{11,9},{8,1... | collective-permute-start | bytes 393224 | tf_op jit(solution)/shard_map/ppermute | solution.py:547
  (7 other events, 60.4 us)

commit v7 on v5

--- a/solution.py
+++ b/solution.py
@@ -150,9 +150,10 @@
         factor = times_scr[index]
         for half in range(2):
             cols = slice(half * 256, (half + 1) * 256)
-            both = dot(w_scr[j], k_scr[slot, :LEAF, cols])
-            low = dot(w_scr[j, :rows, :], k_scr[slot, LEAF:, cols])
-            o_scr[t, :, cols] = o_scr[t, :, cols] + factor * (both[:rows] + both[rows:] + low)
+            high = w_scr[j, :rows, :]
+            both = dot(jnp.concatenate([high, high], axis=1), k_scr[slot, :, cols])
+            low = dot(w_scr[j, rows:, :], k_scr[slot, :LEAF, cols])
+            o_scr[t, :, cols] = o_scr[t, :, cols] + factor * (both + low)
 
     @pl.when(count > 0)
     def _():

time: 93.5 us -> 96 us (1.027); the launches traced: 93.7 us -> 94.2 us
  Pallas kernels: 37.2 us -> 38.5 us
    ppermute x2, waiting for transfers between devices: 5.77 us -> 4.78 us  [to_help(): return lax.ppermute(value, 'help', help_pairs(xs, -dx, 0))]
  transfers between devices with their start and end apart: 22 -> 22, of which waited for: 7 -> 8; matrix products, arithmetic and copies ran while one was open for 2% -> 2% of each run, Pallas kernels for 38% -> 39%
where the time goes in v7:
time: 96 us; the launch traced here: 94.2 us
  Pallas kernels  38.5 us (40%)
  starting transfers between devices  31 us (32%)
  waiting for transfers between devices  20.5 us (21%)
  local copies, waits for them, and re-layouts  3.98 us (4%)
    pallas_call x5, Pallas kernels, near_call(): pl.pallas_call(partial(near_body, len(msgs) // 2, sets, leaves_at, rows,...  24.7 us
    pallas_call x1, Pallas kernels, far_call(): pl.pallas_call(partial(far_body, groups, rows), name='far', out_shape=jax...  6.53 us
    ppermute x1, waiting for transfers between devices, shards(): pts_z = lax.ppermute(pts_y, 'leaf', across)  6.27 us
    ppermute x7, waiting for transfers between devices, from_help(): return lax.ppermute(value, 'help', help_pairs(xs, dx, dc))  5.72 us
    ppermute x2, waiting for transfers between devices, to_help(): return lax.ppermute(value, 'help', help_pairs(xs, -dx, 0))  4.78 us
    ppermute x3, starting transfers between devices, shards(): lax.ppermute(payload, 'leaf', [(i, i ^ mask) for i in range(groups)])  4.45 us
    ppermute x1, starting transfers between devices, shards(): w_z = [lax.ppermute(w_y[0], 'leaf', across)]  4.27 us
    pallas_call x1, Pallas kernels, leaf_call(): pl.pallas_call(partial(leaf_body, xs), name='leaf_up', out_shape=[jax.Sha...  4.05 us
  transfers between devices with their start and end apart: 22, of which 8 were waited for; matrix products, arithmetic and copies ran while one was open for 2% of the time, Pallas kernels for 39%

profile of v7, /device:TPU:0, one launch (start us, length us, event | category | flops | bytes accessed | tf_op | source)
XLA Modules:
  0.0 94.2 jit_solution(16666009424802670193)
XLA Ops:
  0.0 3.0 %collective-permute-start = (f32[64,1024]{1,0:T(8,128)}, f32[64,1024]{1,0:T(8,128)}, u32[]{:S(2)}, u32[]{:S(2)}) collective-permute-start(f32[64,1024]{1,0:T(8,128)} %refs_6_.1), channel_id=1, source_target_pairs={{0,4},{4,0},{8,12},{12,8},{16,20},{20,16},{24,28},{28,24},{1,5},{5... | collective-permute-start | bytes 786440 | tf_op jit(solution)/shard_map/ppermute | solution.py:561
  3.0 2.3 %fusion = (f32[128,1024]{1,0:T(8,128)}, f32[128,1024]{1,0:T(8,128)}) fusion(f32[256,1024]{1,0:T(8,128)} %refs_7_.1), kind=kLoop, calls=%fused_computation | loop fusion | bytes 2097152 | tf_op jit(solution)/shard_map/slice | solution.py:562
  5.3 4.1 %leaf_up.1 = (f32[88,1024]{1,0:T(8,128)}, f32[88,1024]{1,0:T(8,128)}, f32[88,1024]{1,0:T(8,128)}, f32[88,1024]{1,0:T(8,128)}) custom-call(s32[1,2]{1,0:T(1,128)} %count_ref.1, s32[2,32]{1,0:T(2,128)} %src_ref.1, f32[64,1024]{1,0:T(8,128)} %refs_6_.1, f32[256,1024]{1,0:T(8,128)} %refs_7_.1, f32[2,512,256]{2,1,0:T(8,128)} %interp_ref.1), custom_call_target="tpu_custom_call" | custom-call | tf_op jit(solution)/shard_map/leaf_up/pallas_call | solution.py:299
  9.4 2.1 %collective-permute-start.4 = (f32[88,1024]{1,0:T(8,128)}, f32[88,1024]{1,0:T(8,128)S(1)}, u32[]{:S(2)}, u32[]{:S(2)}) collective-permute-start(f32[88,1024]{1,0:T(8,128)} %get-tuple-element.35), channel_id=1, source_target_pairs={{2,0},{3,1},{0,2},{1,3},{6,4},{7,5},{4,6},{5,7},{10,8},{11,9},{8,1... | collective-permute-start | bytes 1081352 | tf_op jit(solution)/shard_map/ppermute | solution.py:565
  11.5 3.7 %collective-permute-start.1 = (f32[64,1024]{1,0:T(8,128)}, f32[64,1024]{1,0:T(8,128)S(1)}, u32[]{:S(2)}, u32[]{:S(2)}) collective-permute-start(f32[64,1024]{1,0:T(8,128)} %collective-permute-done.refs_6_), channel_id=1, source_target_pairs={{0,8},{8,16},{16,24},{12,4},{20,12},{28,20},{1,9},{9,17},{17,25},{... | collective-permute-start | bytes 786440 | tf_op jit(solution)/shard_map/ppermute | solution.py:569
  15.3 6.3 %collective-permute-done.1.pts_ref = f32[64,1024]{1,0:T(8,128)S(1)} collective-permute-done((f32[64,1024]{1,0:T(8,128)}, f32[64,1024]{1,0:T(8,128)S(1)}, u32[]{:S(2)}, u32[]{:S(2)}) %collective-permute-start.1) | collective-permute-done | bytes 262176 | tf_op jit(solution)/shard_map/ppermute | solution.py:569
  21.6 4.3 %collective-permute-start.9 = (f32[128,1024]{1,0:T(8,128)}, f32[128,1024]{1,0:T(8,128)S(1)}, u32[]{:S(2)}, u32[]{:S(2)}) collective-permute-start(f32[128,1024]{1,0:T(8,128)} %collective-permute-done.2.refs_7_), channel_id=1, source_target_pairs={{0,8},{8,16},{16,24},{12,4},{20,12},{28,20},{1,9},{9,17},{17,25},{... | collective-permute-start | bytes 1572872 | tf_op jit(solution)/shard_map/ppermute | solution.py:571
  25.9 2.2 %collective-permute-done.5.refs_3_ = f32[88,1024]{1,0:T(8,128)S(1)} collective-permute-done((f32[88,1024]{1,0:T(8,128)}, f32[88,1024]{1,0:T(8,128)S(1)}, u32[]{:S(2)}, u32[]{:S(2)}) %collective-permute-start.5) | collective-permute-done | bytes 360480 | tf_op jit(solution)/shard_map/ppermute | solution.py:565
  30.6 1.4 %collective-permute-done.10.refs_8_ = f32[128,1024]{1,0:T(8,128)S(1)} collective-permute-done((f32[128,1024]{1,0:T(8,128)}, f32[128,1024]{1,0:T(8,128)S(1)}, u32[]{:S(2)}, u32[]{:S(2)}) %collective-permute-start.10) | collective-permute-done | bytes 524320 | tf_op jit(solution)/shard_map/ppermute | solution.py:562
  32.0 3.7 %collective-permute-start.13 = (f32[128,1024]{1,0:T(8,128)S(1)}, f32[128,1024]{1,0:T(8,128)S(1)}, u32[]{:S(2)}, u32[]{:S(2)}) collective-permute-start(f32[128,1024]{1,0:T(8,128)S(1)} %collective-permute-done.10.refs_8_), channel_id=1, source_target_pairs={{0,8},{8,16},{16,24},{12,4},{20,12},{28,20},{1,9},{9,17},{17,25},{... | collective-permute-start | bytes 1572872 | tf_op jit(solution)/shard_map/ppermute | solution.py:581
  35.7 1.6 %collective-permute-start.6 = (f32[96,256]{1,0:T(8,128)S(1)}, f32[96,256]{1,0:T(8,128)S(1)}, u32[]{:S(2)}, u32[]{:S(2)}) collective-permute-start(f32[96,256]{1,0:T(8,128)S(1)} %get-tuple-element.47.refs_0_), channel_id=1, source_target_pairs={{0,8},{4,12},{8,0},{12,4},{16,24},{20,28},{24,16},{28,20},{1,9},{5... | collective-permute-start | bytes 294920 | tf_op jit(solution)/shard_map/ppermute | solution.py:576
  38.4 1.7 %collective-permute-start.8 = (f32[96,256]{1,0:T(8,128)S(1)}, f32[96,256]{1,0:T(8,128)S(1)}, u32[]{:S(2)}, u32[]{:S(2)}) collective-permute-start(f32[96,256]{1,0:T(8,128)S(1)} %get-tuple-element.47.refs_0_), channel_id=1, source_target_pairs={{0,24},{4,28},{8,16},{12,20},{16,8},{20,12},{24,0},{28,4},{1,25},{... | collective-permute-start | bytes 294920 | tf_op jit(solution)/shard_map/ppermute | solution.py:576
  40.7 11.5 %near_own.1.refs_9_.refs_13_ = f32[8,256,512]{2,1,0:T(8,128)S(1)} custom-call(f32[88,1024]{1,0:T(8,128)S(1)} %copy-done.2, f32[88,1024]{1,0:T(8,128)S(1)} %collective-permute-done.3.refs_1_, f32[88,1024]{1,0:T(8,128)S(1)} %collective-permute-done.4.refs_2_, f32[88,1024]{1,0:T(8,128)S(1)} %collective-permute-done.5.refs_3_, ...), custom_call_target="tpu_custom_call" | custom-call | tf_op jit(solution)/shard_map/near_own/pallas_call | solution.py:208
  52.2 5.3 %near_pair.1.refs_10_.refs_11_ = f32[4,256,512]{2,1,0:T(8,128)S(1)} custom-call(f32[88,1024]{1,0:T(8,128)S(1)} %copy-done.2, f32[88,1024]{1,0:T(8,128)S(1)} %collective-permute-done.3.refs_1_, f32[88,1024]{1,0:T(8,128)S(1)} %collective-permute-done.4.refs_2_, f32[88,1024]{1,0:T(8,128)S(1)} %collective-permute-done.5.refs_3_, ...), custom_call_target="tpu_custom_call" | custom-call | tf_op jit(solution)/shard_map/near_pair/pallas_call | solution.py:208
  60.0 3.5 %collective-permute-start.11 = (f32[4,96,256]{2,1,0:T(8,128)S(1)}, f32[4,96,256]{2,1,0:T(8,128)S(1)}, u32[]{:S(2)}, u32[]{:S(2)}) collective-permute-start(f32[4,96,256]{2,1,0:T(8,128)S(1)} %stack.2.alike_ref.refs_11_), channel_id=1, source_target_pairs={{0,4},{4,0},{8,12},{12,8},{16,20},{20,16},{24,28},{28,24},{1,5},{5... | collective-permute-start | bytes 1179656 | tf_op jit(solution)/shard_map/ppermute | solution.py:590
  63.6 2.7 %collective-permute-start.18 = (f32[128,1024]{1,0:T(8,128)S(1)}, f32[128,1024]{1,0:T(8,128)S(1)}, u32[]{:S(2)}, u32[]{:S(2)}) collective-permute-start(f32[128,1024]{1,0:T(8,128)S(1)} %add_parts.4), channel_id=1, source_target_pairs={{2,0},{3,1},{0,2},{1,3},{6,4},{7,5},{4,6},{5,7},{10,8},{11,9},{8,1... | collective-permute-start | bytes 1572872 | tf_op jit(solution)/shard_map/ppermute | solution.py:550
  66.4 6.1 %near_home.1 = (f32[128,1024]{1,0:T(8,128)S(1)}, f32[128,1024]{1,0:T(8,128)S(1)}, f32[128,1024]{1,0:T(8,128)S(1)}, f32[128,1024]{1,0:T(8,128)S(1)}) custom-call(f32[88,1024]{1,0:T(8,128)S(1)} %copy-done.2, f32[88,1024]{1,0:T(8,128)S(1)} %collective-permute-done.3.refs_1_, f32[88,1024]{1,0:T(8,128)S(1)} %collective-permute-done.4.refs_2_, ...), custom_call_target="tpu_custom_call" | custom-call | tf_op jit(solution)/shard_map/near_home/pallas_call | solution.py:208
  73.3 2.3 %collective-permute-done.12.mate_ref = f32[8,32,256]{2,1,0:T(8,128)S(1)} collective-permute-done((f32[8,32,256]{2,1,0:T(8,128)S(1)}, f32[8,32,256]{2,1,0:T(8,128)S(1)}, u32[]{:S(2)}, u32[]{:S(2)}) %collective-permute-start.12) | collective-permute-done | bytes 262176 | tf_op jit(solution)/shard_map/ppermute | solution.py:547
  75.7 6.5 %far.1.refs_0_ = f32[64,256]{1,0:T(8,128)S(1)} custom-call(s32[4,14]{1,0:T(4,128)S(1)} %bitcast.1, s32[6,256]{1,0:T(8,128)S(1)} %copy-done.6, f32[6,512,256]{2,1,0:T(8,128)S(1)} %copy-done.4, f32[4,96,256]{2,1,0:T(8,128)S(1)} %stack.2.alike_ref.refs_11_, f32[4,96,256]{2,1,0:T(8,128)S(1)} %collective-permute-done.11.beside_ref, ...), custom_call_target="tpu_custom_call" | custom-call | tf_op jit(solution)/shard_map/far/pallas_call | solution.py:466
  82.4 1.1 %collective-permute-done.15.refs_1_ = f32[64,256]{1,0:T(8,128)S(1)} collective-permute-done((f32[64,256]{1,0:T(8,128)S(1)}, f32[64,256]{1,0:T(8,128)S(1)}, u32[]{:S(2)}, u32[]{:S(2)}) %collective-permute-start.15) | collective-permute-done | bytes 65568 | tf_op jit(solution)/shard_map/ppermute | solution.py:547
  83.6 1.8 %collective-permute-start.16 = (f32[2,64,256]{2,1,0:T(8,128)S(1)}, f32[2,64,256]{2,1,0:T(8,128)S(1)}, u32[]{:S(2)}, u32[]{:S(2)}) collective-permute-start(f32[2,64,256]{2,1,0:T(8,128)S(1)} %stack.3.refs_0_), channel_id=1, source_target_pairs={{2,0},{3,1},{0,2},{1,3},{6,4},{7,5},{4,6},{5,7},{10,8},{11,9},{8,1... | collective-permute-start | bytes 393224 | tf_op jit(solution)/shard_map/ppermute | solution.py:547
  85.4 4.8 %collective-permute-done.19.refs_3_ = f32[128,1024]{1,0:T(8,128)S(1)} collective-permute-done((f32[128,1024]{1,0:T(8,128)S(1)}, f32[128,1024]{1,0:T(8,128)S(1)}, u32[]{:S(2)}, u32[]{:S(2)}) %collective-permute-start.19) | collective-permute-done | bytes 524320 | tf_op jit(solution)/shard_map/ppermute | solution.py:550
  90.3 2.2 %collective-permute-done.16.refs_1_ = f32[2,64,256]{2,1,0:T(8,128)S(1)} collective-permute-done((f32[2,64,256]{2,1,0:T(8,128)S(1)}, f32[2,64,256]{2,1,0:T(8,128)S(1)}, u32[]{:S(2)}, u32[]{:S(2)}) %collective-permute-start.16) | collective-permute-done | bytes 131104 | tf_op jit(solution)/shard_map/ppermute | solution.py:547
  92.6 1.6 %join.1 = f32[256,1024]{1,0:T(8,128)} custom-call(f32[2,512,256]{2,1,0:T(8,128)S(1)} %copy-done.3, f32[2,64,256]{2,1,0:T(8,128)S(1)} %stack.3.refs_0_, f32[2,64,256]{2,1,0:T(8,128)S(1)} %collective-permute-done.16.refs_1_, f32[128,1024]{1,0:T(8,128)S(1)} %get-tuple-element.55.refs_2_, f32[128,1024]{1,0:T(8,128)S(1)} %get-tuple-element.56.refs_3_, ...), custom_call_target="tpu_custom_call" | custom-call | tf_op jit(solution)/shard_map/join/pallas_call | solution.py:523
  (55 shorter events, 8.1 us)
Async XLA Ops:
  0.0 11.5 %collective-permute-start = (f32[64,1024]{1,0:T(8,128)}, f32[64,1024]{1,0:T(8,128)}, u32[]{:S(2)}, u32[]{:S(2)}) collective-permute-start(f32[64,1024]{1,0:T(8,128)} %refs_6_.1), channel_id=1, source_target_pairs={{0,4},{4,0},{8,12},{12,8},{16,20},{20,16},{24,28},{28,24},{1,5},{5... | collective-permute-start | bytes 786440 | tf_op jit(solution)/shard_map/ppermute | solution.py:561
  5.3 16.4 %collective-permute-start.2 = (f32[128,1024]{1,0:T(8,128)}, f32[128,1024]{1,0:T(8,128)}, u32[]{:S(2)}, u32[]{:S(2)}) collective-permute-start(f32[128,1024]{1,0:T(8,128)} %get-tuple-element.60), channel_id=1, source_target_pairs={{0,4},{4,0},{8,12},{12,8},{16,20},{20,16},{24,28},{28,24},{1,5},{5... | collective-permute-start | bytes 1572872 | tf_op jit(solution)/shard_map/ppermute | solution.py:562
  9.3 5.9 %collective-permute-start.3 = (f32[88,1024]{1,0:T(8,128)}, f32[88,1024]{1,0:T(8,128)S(1)}, u32[]{:S(2)}, u32[]{:S(2)}) collective-permute-start(f32[88,1024]{1,0:T(8,128)} %get-tuple-element.33), channel_id=1, source_target_pairs={{1,0},{0,1},{3,2},{2,3},{5,4},{4,5},{7,6},{6,7},{9,8},{8,9},{11,10... | collective-permute-start | bytes 1081352 | tf_op jit(solution)/shard_map/ppermute | solution.py:565
  9.4 16.5 %collective-permute-start.4 = (f32[88,1024]{1,0:T(8,128)}, f32[88,1024]{1,0:T(8,128)S(1)}, u32[]{:S(2)}, u32[]{:S(2)}) collective-permute-start(f32[88,1024]{1,0:T(8,128)} %get-tuple-element.35), channel_id=1, source_target_pairs={{2,0},{3,1},{0,2},{1,3},{6,4},{7,5},{4,6},{5,7},{10,8},{11,9},{8,1... | collective-permute-start | bytes 1081352 | tf_op jit(solution)/shard_map/ppermute | solution.py:565
  11.5 16.7 %collective-permute-start.5 = (f32[88,1024]{1,0:T(8,128)}, f32[88,1024]{1,0:T(8,128)S(1)}, u32[]{:S(2)}, u32[]{:S(2)}) collective-permute-start(f32[88,1024]{1,0:T(8,128)} %get-tuple-element.36), channel_id=1, source_target_pairs={{3,0},{2,1},{1,2},{0,3},{7,4},{6,5},{5,6},{4,7},{11,8},{10,9},{9,1... | collective-permute-start | bytes 1081352 | tf_op jit(solution)/shard_map/ppermute | solution.py:565
  11.5 10.1 %collective-permute-start.1 = (f32[64,1024]{1,0:T(8,128)}, f32[64,1024]{1,0:T(8,128)S(1)}, u32[]{:S(2)}, u32[]{:S(2)}) collective-permute-start(f32[64,1024]{1,0:T(8,128)} %collective-permute-done.refs_6_), channel_id=1, source_target_pairs={{0,8},{8,16},{16,24},{12,4},{20,12},{28,20},{1,9},{9,17},{17,25},{... | collective-permute-start | bytes 786440 | tf_op jit(solution)/shard_map/ppermute | solution.py:569
  15.3 16.7 %collective-permute-start.10 = (f32[128,1024]{1,0:T(8,128)}, f32[128,1024]{1,0:T(8,128)S(1)}, u32[]{:S(2)}, u32[]{:S(2)}) collective-permute-start(f32[128,1024]{1,0:T(8,128)} %get-tuple-element.59), channel_id=1, source_target_pairs={{0,4},{4,0},{8,12},{12,8},{16,20},{20,16},{24,28},{28,24},{1,5},{5... | collective-permute-start | bytes 1572872 | tf_op jit(solution)/shard_map/ppermute | solution.py:562
  21.6 35.9 %collective-permute-start.9 = (f32[128,1024]{1,0:T(8,128)}, f32[128,1024]{1,0:T(8,128)S(1)}, u32[]{:S(2)}, u32[]{:S(2)}) collective-permute-start(f32[128,1024]{1,0:T(8,128)} %collective-permute-done.2.refs_7_), channel_id=1, source_target_pairs={{0,8},{8,16},{16,24},{12,4},{20,12},{28,20},{1,9},{9,17},{17,25},{... | collective-permute-start | bytes 1572872 | tf_op jit(solution)/shard_map/ppermute | solution.py:571
  29.8 10.9 %copy-start.5 = (f32[64,1024]{1,0:T(8,128)S(1)}, f32[64,1024]{1,0:T(8,128)}, u32[]{:S(2)}) copy-start(f32[64,1024]{1,0:T(8,128)} %refs_6_.1) | copy-start | bytes 786436
  32.0 26.5 %collective-permute-start.13 = (f32[128,1024]{1,0:T(8,128)S(1)}, f32[128,1024]{1,0:T(8,128)S(1)}, u32[]{:S(2)}, u32[]{:S(2)}) collective-permute-start(f32[128,1024]{1,0:T(8,128)S(1)} %collective-permute-done.10.refs_8_), channel_id=1, source_target_pairs={{0,8},{8,16},{16,24},{12,4},{20,12},{28,20},{1,9},{9,17},{17,25},{... | collective-permute-start | bytes 1572872 | tf_op jit(solution)/shard_map/ppermute | solution.py:581
  35.7 22.7 %collective-permute-start.6 = (f32[96,256]{1,0:T(8,128)S(1)}, f32[96,256]{1,0:T(8,128)S(1)}, u32[]{:S(2)}, u32[]{:S(2)}) collective-permute-start(f32[96,256]{1,0:T(8,128)S(1)} %get-tuple-element.47.refs_0_), channel_id=1, source_target_pairs={{0,8},{4,12},{8,0},{12,4},{16,24},{20,28},{24,16},{28,20},{1,9},{5... | collective-permute-start | bytes 294920 | tf_op jit(solution)/shard_map/ppermute | solution.py:576
  37.3 21.1 %collective-permute-start.7 = (f32[96,256]{1,0:T(8,128)S(1)}, f32[96,256]{1,0:T(8,128)S(1)}, u32[]{:S(2)}, u32[]{:S(2)}) collective-permute-start(f32[96,256]{1,0:T(8,128)S(1)} %get-tuple-element.47.refs_0_), channel_id=1, source_target_pairs={{0,16},{4,20},{8,24},{12,28},{16,0},{20,4},{24,8},{28,12},{1,17},{... | collective-permute-start | bytes 294920 | tf_op jit(solution)/shard_map/ppermute | solution.py:576
  38.4 20.0 %collective-permute-start.8 = (f32[96,256]{1,0:T(8,128)S(1)}, f32[96,256]{1,0:T(8,128)S(1)}, u32[]{:S(2)}, u32[]{:S(2)}) collective-permute-start(f32[96,256]{1,0:T(8,128)S(1)} %get-tuple-element.47.refs_0_), channel_id=1, source_target_pairs={{0,24},{4,28},{8,16},{12,20},{16,8},{20,12},{24,0},{28,4},{1,25},{... | collective-permute-start | bytes 294920 | tf_op jit(solution)/shard_map/ppermute | solution.py:576
  58.3 5.2 %collective-permute-start.17 = (f32[128,1024]{1,0:T(8,128)S(1)}, f32[128,1024]{1,0:T(8,128)S(1)}, u32[]{:S(2)}, u32[]{:S(2)}) collective-permute-start(f32[128,1024]{1,0:T(8,128)S(1)} %get-tuple-element.46), channel_id=1, source_target_pairs={{1,0},{0,1},{3,2},{2,3},{5,4},{4,5},{7,6},{6,7},{9,8},{8,9},{11,10... | collective-permute-start | bytes 1572872 | tf_op jit(solution)/shard_map/ppermute | solution.py:547
  59.5 6.8 %collective-permute-start.14 = (f32[128,1024]{1,0:T(8,128)S(1)}, f32[128,1024]{1,0:T(8,128)S(1)}, u32[]{:S(2)}, u32[]{:S(2)}) collective-permute-start(f32[128,1024]{1,0:T(8,128)S(1)} %get-tuple-element.52), channel_id=1, source_target_pairs={{1,0},{0,1},{3,2},{2,3},{5,4},{4,5},{7,6},{6,7},{9,8},{8,9},{11,10... | collective-permute-start | bytes 1572872 | tf_op jit(solution)/shard_map/ppermute | solution.py:547
  60.0 13.2 %collective-permute-start.11 = (f32[4,96,256]{2,1,0:T(8,128)S(1)}, f32[4,96,256]{2,1,0:T(8,128)S(1)}, u32[]{:S(2)}, u32[]{:S(2)}) collective-permute-start(f32[4,96,256]{2,1,0:T(8,128)S(1)} %stack.2.alike_ref.refs_11_), channel_id=1, source_target_pairs={{0,4},{4,0},{8,12},{12,8},{16,20},{20,16},{24,28},{28,24},{1,5},{5... | collective-permute-start | bytes 1179656 | tf_op jit(solution)/shard_map/ppermute | solution.py:590
  63.6 21.8 %collective-permute-start.18 = (f32[128,1024]{1,0:T(8,128)S(1)}, f32[128,1024]{1,0:T(8,128)S(1)}, u32[]{:S(2)}, u32[]{:S(2)}) collective-permute-start(f32[128,1024]{1,0:T(8,128)S(1)} %add_parts.4), channel_id=1, source_target_pairs={{2,0},{3,1},{0,2},{1,3},{6,4},{7,5},{4,6},{5,7},{10,8},{11,9},{8,1... | collective-permute-start | bytes 1572872 | tf_op jit(solution)/shard_map/ppermute | solution.py:550
  66.3 23.9 %collective-permute-start.19 = (f32[128,1024]{1,0:T(8,128)S(1)}, f32[128,1024]{1,0:T(8,128)S(1)}, u32[]{:S(2)}, u32[]{:S(2)}) collective-permute-start(f32[128,1024]{1,0:T(8,128)S(1)} %add_parts.3.refs_14_), channel_id=1, source_target_pairs={{2,0},{3,1},{0,2},{1,3},{6,4},{7,5},{4,6},{5,7},{10,8},{11,9},{8,1... | collective-permute-start | bytes 1572872 | tf_op jit(solution)/shard_map/ppermute | solution.py:550
  72.6 20.0 %collective-permute-start.20 = (f32[128,1024]{1,0:T(8,128)S(1)}, f32[128,1024]{1,0:T(8,128)S(1)}, u32[]{:S(2)}, u32[]{:S(2)}) collective-permute-start(f32[128,1024]{1,0:T(8,128)S(1)} %get-tuple-element.57), channel_id=1, source_target_pairs={{1,0},{0,1},{3,2},{2,3},{5,4},{4,5},{7,6},{6,7},{9,8},{8,9},{11,10... | collective-permute-start | bytes 1572872 | tf_op jit(solution)/shard_map/ppermute | solution.py:547
  72.7 19.9 %collective-permute-start.21 = (f32[128,1024]{1,0:T(8,128)S(1)}, f32[128,1024]{1,0:T(8,128)S(1)}, u32[]{:S(2)}, u32[]{:S(2)}) collective-permute-start(f32[128,1024]{1,0:T(8,128)S(1)} %get-tuple-element.58), channel_id=1, source_target_pairs={{1,0},{0,1},{3,2},{2,3},{5,4},{4,5},{7,6},{6,7},{9,8},{8,9},{11,10... | collective-permute-start | bytes 1572872 | tf_op jit(solution)/shard_map/ppermute | solution.py:547
  73.3 2.4 %collective-permute-start.12 = (f32[8,32,256]{2,1,0:T(8,128)S(1)}, f32[8,32,256]{2,1,0:T(8,128)S(1)}, u32[]{:S(2)}, u32[]{:S(2)}) collective-permute-start(f32[8,32,256]{2,1,0:T(8,128)S(1)} %points_of.1), channel_id=1, source_target_pairs={{1,0},{0,1},{3,2},{2,3},{5,4},{4,5},{7,6},{6,7},{9,8},{8,9},{11,10... | collective-permute-start | bytes 786440 | tf_op jit(solution)/shard_map/ppermute | solution.py:547
  75.7 16.9 %copy-start.3 = (f32[2,512,256]{2,1,0:T(8,128)S(1)}, f32[2,512,256]{2,1,0:T(8,128)}, u32[]{:S(2)}) copy-start(f32[2,512,256]{2,1,0:T(8,128)} %interp_ref.1) | copy-start | bytes 3145732
  82.2 1.3 %collective-permute-start.15 = (f32[64,256]{1,0:T(8,128)S(1)}, f32[64,256]{1,0:T(8,128)S(1)}, u32[]{:S(2)}, u32[]{:S(2)}) collective-permute-start(f32[64,256]{1,0:T(8,128)S(1)} %far.1.refs_0_), channel_id=1, source_target_pairs={{1,0},{0,1},{3,2},{2,3},{5,4},{4,5},{7,6},{6,7},{9,8},{8,9},{11,10... | collective-permute-start | bytes 196616 | tf_op jit(solution)/shard_map/ppermute | solution.py:547
  83.6 9.0 %collective-permute-start.16 = (f32[2,64,256]{2,1,0:T(8,128)S(1)}, f32[2,64,256]{2,1,0:T(8,128)S(1)}, u32[]{:S(2)}, u32[]{:S(2)}) collective-permute-start(f32[2,64,256]{2,1,0:T(8,128)S(1)} %stack.3.refs_0_), channel_id=1, source_target_pairs={{2,0},{3,1},{0,2},{1,3},{6,4},{7,5},{4,6},{5,7},{10,8},{11,9},{8,1... | collective-permute-start | bytes 393224 | tf_op jit(solution)/shard_map/ppermute | solution.py:547
  (7 other events, 51.4 us)

commit v8 on v5

--- a/solution.py
+++ b/solution.py
@@ -566,7 +566,8 @@
         if n
     ]
     pts_z = lax.ppermute(pts_y, "leaf", across)
-    pts_z, w_y[0], got[0] = together(pts_z, w_y[0], got[0])
+    sides = [source_call(points), source_call(pts_y)]
+    pts_z, w_y[0], got[0], (own_side, pair_side) = together(pts_z, w_y[0], got[0], sides)
     w_z = [lax.ppermute(w_y[0], "leaf", across)]
     msgs = [sent[0]] + [got[order.index((-dx % xs, dc)) - 1] for dx, dc in order[1:]]
     payload, targets = skel_call(xs, skel_group, msgs)
@@ -576,9 +577,9 @@
 
     payload, w_y[1] = together(payload, w_y[1])
     every, away, home = (0, 2 * helpers), (4, 2 * helpers), (0, 4)
-    (own,) = near_call("near_own", msgs, targets, every, [("own", (points,), [weights])], R)
+    (own,) = near_call("near_own", msgs, targets, every, [("own", own_side, [weights])], R)
     w_z.append(lax.ppermute(w_y[1], "leaf", across))
-    pair_src = ("pair", (pts_y,), w_y)
+    pair_src = ("pair", pair_side, w_y)
     (pair,) = near_call("near_pair", msgs, targets, away, [pair_src], R, after=[own])
     z_side = source_call(pts_z)
     sums, part = [], [pair]

time: 93.5 us -> 102 us (1.091)
  waiting for transfers between devices: 20.6 us -> 28.7 us
  Pallas kernels: 37.2 us -> 33.2 us
  starting transfers between devices: 31.6 us -> 34.7 us
    ppermute x1, waiting for transfers between devices: 0.01 us -> 11.6 us  [shards(): pts_y = lax.ppermute(points, 'leaf', beside)]
    pallas_call x5, Pallas kernels: 24 us -> 17.5 us  [near_call(): pl.pallas_call(partial(near_body, len(msgs) // 2, sets, leaves_at, rows,...]
    ppermute x1, starting transfers between devices: 3.11 us -> 7.71 us  [shards(): side = lax.ppermute(alike, 'leaf', beside)]
    ppermute x1, waiting for transfers between devices: 6.27 us -> 1.9 us  [shards(): pts_z = lax.ppermute(pts_y, 'leaf', across)]
    ppermute x1, waiting for transfers between devices: 0.01 us -> 3.57 us  [shards(): side = lax.ppermute(alike, 'leaf', beside)]
    ppermute x2, starting transfers between devices: 0.07 us -> 3.04 us  [shards(): lax.ppermute(chunk, 'leaf', beside)]
    ppermute x1, starting transfers between devices: 2.97 us -> 0.03 us  [shards(): pts_y = lax.ppermute(points, 'leaf', beside)]
    ppermute x3, waiting for transfers between devices: 2.18 us -> 0.01 us  [shards(): lax.ppermute(sent[n], 'help', help_pairs(xs, -dx, dc))]
  transfers between devices with their start and end apart: 22 -> 22, of which waited for: 7 -> 10; matrix products, arithmetic and copies ran while one was open for 2% -> 0% of each run, Pallas kernels for 38% -> 31%
where the time goes in v8:
time: 102 us
  starting transfers between devices  34.7 us (34%)
  Pallas kernels  33.2 us (33%)
  waiting for transfers between devices  28.7 us (28%)
  local copies, waits for them, and re-layouts  4.92 us (5%)
    pallas_call x5, Pallas kernels, near_call(): pl.pallas_call(partial(near_body, len(msgs) // 2, sets, leaves_at, rows,...  17.5 us
    ppermute x1, waiting for transfers between devices, shards(): pts_y = lax.ppermute(points, 'leaf', beside)  11.6 us
    ppermute x1, starting transfers between devices, shards(): side = lax.ppermute(alike, 'leaf', beside)  7.71 us
    pallas_call x1, Pallas kernels, far_call(): pl.pallas_call(partial(far_body, groups, rows), name='far', out_shape=jax...  6.4 us
    ppermute x2, waiting for transfers between devices, to_help(): return lax.ppermute(value, 'help', help_pairs(xs, -dx, 0))  4.74 us
    ppermute x7, waiting for transfers between devices, from_help(): return lax.ppermute(value, 'help', help_pairs(xs, dx, dc))  4.58 us
    ppermute x3, starting transfers between devices, shards(): lax.ppermute(payload, 'leaf', [(i, i ^ mask) for i in range(groups)])  4.45 us
    ppermute x1, starting transfers between devices, shards(): w_z = [lax.ppermute(w_y[0], 'leaf', across)]  4.3 us
  transfers between devices with their start and end apart: 22, of which 10 were waited for; matrix products, arithmetic and copies ran while one was open for 0% of the time, Pallas kernels for 31%

profile of v8, /device:TPU:0, one launch (start us, length us, event | category | flops | bytes accessed | tf_op | source)
XLA Modules:
  0.0 101.9 jit_solution(12688357613397408808)
XLA Ops:
  0.0 2.3 %fusion = (f32[128,1024]{1,0:T(8,128)}, f32[128,1024]{1,0:T(8,128)}) fusion(f32[256,1024]{1,0:T(8,128)} %refs_8_.1), kind=kLoop, calls=%fused_computation | loop fusion | bytes 2097152 | tf_op jit(solution)/shard_map/slice | solution.py:561
  2.3 3.0 %collective-permute-start.2 = (f32[128,1024]{1,0:T(8,128)}, f32[128,1024]{1,0:T(8,128)}, u32[]{:S(2)}, u32[]{:S(2)}) collective-permute-start(f32[128,1024]{1,0:T(8,128)} %get-tuple-element.76), channel_id=1, source_target_pairs={{0,4},{4,0},{8,12},{12,8},{16,20},{20,16},{24,28},{28,24},{1,5},{5... | collective-permute-start | bytes 1572872 | tf_op jit(solution)/shard_map/ppermute | solution.py:561
  5.3 4.1 %leaf_up.1 = (f32[88,1024]{1,0:T(8,128)}, f32[88,1024]{1,0:T(8,128)}, f32[88,1024]{1,0:T(8,128)}, f32[88,1024]{1,0:T(8,128)}) custom-call(s32[1,2]{1,0:T(1,128)} %count_ref.1, s32[2,32]{1,0:T(2,128)} %src_ref.1, f32[64,1024]{1,0:T(8,128)} %pts_ref.1, f32[256,1024]{1,0:T(8,128)} %refs_8_.1, f32[2,512,256]{2,1,0:T(8,128)} %interp_ref.1), custom_call_target="tpu_custom_call" | custom-call | tf_op jit(solution)/shard_map/leaf_up/pallas_call | solution.py:298
  9.5 2.0 %collective-permute-start.4 = (f32[88,1024]{1,0:T(8,128)}, f32[88,1024]{1,0:T(8,128)S(1)}, u32[]{:S(2)}, u32[]{:S(2)}) collective-permute-start(f32[88,1024]{1,0:T(8,128)} %get-tuple-element.47), channel_id=1, source_target_pairs={{2,0},{3,1},{0,2},{1,3},{6,4},{7,5},{4,6},{5,7},{10,8},{11,9},{8,1... | collective-permute-start | bytes 1081352 | tf_op jit(solution)/shard_map/ppermute | solution.py:564
  11.6 11.6 %collective-permute-done.pts_ref = f32[64,1024]{1,0:T(8,128)} collective-permute-done((f32[64,1024]{1,0:T(8,128)}, f32[64,1024]{1,0:T(8,128)}, u32[]{:S(2)}, u32[]{:S(2)}) %collective-permute-start) | collective-permute-done | bytes 262176 | tf_op jit(solution)/shard_map/ppermute | solution.py:560
  23.1 3.7 %collective-permute-start.1 = (f32[64,1024]{1,0:T(8,128)}, f32[64,1024]{1,0:T(8,128)S(1)}, u32[]{:S(2)}, u32[]{:S(2)}) collective-permute-start(f32[64,1024]{1,0:T(8,128)} %collective-permute-done.pts_ref), channel_id=1, source_target_pairs={{0,8},{8,16},{16,24},{12,4},{20,12},{28,20},{1,9},{9,17},{17,25},{... | collective-permute-start | bytes 786440 | tf_op jit(solution)/shard_map/ppermute | solution.py:568
  28.4 1.5 %source_side.4 = (bf16[2,512,256]{2,1,0:T(8,128)(2,1)S(1)}, f32[2,512,128]{2,1,0:T(8,128)S(1)}) custom-call(f32[64,1024]{1,0:T(8,128)} %collective-permute-done.pts_ref), custom_call_target="tpu_custom_call" | custom-call | tf_op jit(solution)/shard_map/source_side/pallas_call | solution.py:232
  29.9 1.9 %collective-permute-done.1.pts_ref = f32[64,1024]{1,0:T(8,128)S(1)} collective-permute-done((f32[64,1024]{1,0:T(8,128)}, f32[64,1024]{1,0:T(8,128)S(1)}, u32[]{:S(2)}, u32[]{:S(2)}) %collective-permute-start.1) | collective-permute-done | bytes 262176 | tf_op jit(solution)/shard_map/ppermute | solution.py:568
  31.8 4.3 %collective-permute-start.9 = (f32[128,1024]{1,0:T(8,128)}, f32[128,1024]{1,0:T(8,128)S(1)}, u32[]{:S(2)}, u32[]{:S(2)}) collective-permute-start(f32[128,1024]{1,0:T(8,128)} %collective-permute-done.2.refs_8_), channel_id=1, source_target_pairs={{0,8},{8,16},{16,24},{12,4},{20,12},{28,20},{1,9},{9,17},{17,25},{... | collective-permute-start | bytes 1572872 | tf_op jit(solution)/shard_map/ppermute | solution.py:571
  39.6 3.5 %collective-permute-start.13 = (f32[128,1024]{1,0:T(8,128)S(1)}, f32[128,1024]{1,0:T(8,128)S(1)}, u32[]{:S(2)}, u32[]{:S(2)}) collective-permute-start(f32[128,1024]{1,0:T(8,128)S(1)} %collective-permute-done.10.refs_9_), channel_id=1, source_target_pairs={{0,8},{8,16},{16,24},{12,4},{20,12},{28,20},{1,9},{9,17},{17,25},{... | collective-permute-start | bytes 1572872 | tf_op jit(solution)/shard_map/ppermute | solution.py:581
  43.1 1.6 %collective-permute-start.6 = (f32[96,256]{1,0:T(8,128)S(1)}, f32[96,256]{1,0:T(8,128)S(1)}, u32[]{:S(2)}, u32[]{:S(2)}) collective-permute-start(f32[96,256]{1,0:T(8,128)S(1)} %get-tuple-element.63.refs_0_), channel_id=1, source_target_pairs={{0,8},{4,12},{8,0},{12,4},{16,24},{20,28},{24,16},{28,20},{1,9},{5... | collective-permute-start | bytes 294920 | tf_op jit(solution)/shard_map/ppermute | solution.py:576
  44.7 2.8 %collective-permute-start.8 = (f32[96,256]{1,0:T(8,128)S(1)}, f32[96,256]{1,0:T(8,128)S(1)}, u32[]{:S(2)}, u32[]{:S(2)}) collective-permute-start(f32[96,256]{1,0:T(8,128)S(1)} %get-tuple-element.63.refs_0_), channel_id=1, source_target_pairs={{0,24},{4,28},{8,16},{12,20},{16,8},{20,12},{24,0},{28,4},{1,25},{... | collective-permute-start | bytes 294920 | tf_op jit(solution)/shard_map/ppermute | solution.py:576
  48.1 8.1 %near_own.1.refs_10_.refs_9_.refs_14_ = f32[8,256,512]{2,1,0:T(8,128)S(1)} custom-call(f32[88,1024]{1,0:T(8,128)S(1)} %copy-done.2, f32[88,1024]{1,0:T(8,128)S(1)} %collective-permute-done.3.refs_1_, f32[88,1024]{1,0:T(8,128)S(1)} %collective-permute-done.4.refs_2_, f32[88,1024]{1,0:T(8,128)S(1)} %collective-permute-done.5.refs_3_, ...), custom_call_target="tpu_custom_call" | custom-call | tf_op jit(solution)/shard_map/near_own/pallas_call | solution.py:207
  56.2 4.4 %near_pair.1.refs_10_.refs_11_ = f32[4,256,512]{2,1,0:T(8,128)S(1)} custom-call(f32[88,1024]{1,0:T(8,128)S(1)} %copy-done.2, f32[88,1024]{1,0:T(8,128)S(1)} %collective-permute-done.3.refs_1_, f32[88,1024]{1,0:T(8,128)S(1)} %collective-permute-done.4.refs_2_, f32[88,1024]{1,0:T(8,128)S(1)} %collective-permute-done.5.refs_3_, ...), custom_call_target="tpu_custom_call" | custom-call | tf_op jit(solution)/shard_map/near_pair/pallas_call | solution.py:207
  64.4 7.7 %collective-permute-start.11 = (f32[4,96,256]{2,1,0:T(8,128)S(1)}, f32[4,96,256]{2,1,0:T(8,128)S(1)}, u32[]{:S(2)}, u32[]{:S(2)}) collective-permute-start(f32[4,96,256]{2,1,0:T(8,128)S(1)} %stack.2.alike_ref.refs_11_), channel_id=1, source_target_pairs={{0,4},{4,0},{8,12},{12,8},{16,20},{20,16},{24,28},{28,24},{1,5},{5... | collective-permute-start | bytes 1179656 | tf_op jit(solution)/shard_map/ppermute | solution.py:590
  72.7 1.7 %collective-permute-start.19 = (f32[128,1024]{1,0:T(8,128)S(1)}, f32[128,1024]{1,0:T(8,128)S(1)}, u32[]{:S(2)}, u32[]{:S(2)}) collective-permute-start(f32[128,1024]{1,0:T(8,128)S(1)} %add_parts.3.refs_15_), channel_id=1, source_target_pairs={{2,0},{3,1},{0,2},{1,3},{6,4},{7,5},{4,6},{5,7},{10,8},{11,9},{8,1... | collective-permute-start | bytes 1572872 | tf_op jit(solution)/shard_map/ppermute | solution.py:549
  74.4 3.2 %near_home.1 = (f32[128,1024]{1,0:T(8,128)S(1)}, f32[128,1024]{1,0:T(8,128)S(1)}, f32[128,1024]{1,0:T(8,128)S(1)}, f32[128,1024]{1,0:T(8,128)S(1)}) custom-call(f32[88,1024]{1,0:T(8,128)S(1)} %copy-done.2, f32[88,1024]{1,0:T(8,128)S(1)} %collective-permute-done.3.refs_1_, f32[88,1024]{1,0:T(8,128)S(1)} %collective-permute-done.4.refs_2_, ...), custom_call_target="tpu_custom_call" | custom-call | tf_op jit(solution)/shard_map/near_home/pallas_call | solution.py:207
  78.2 3.6 %collective-permute-done.11.beside_ref = f32[4,96,256]{2,1,0:T(8,128)S(1)} collective-permute-done((f32[4,96,256]{2,1,0:T(8,128)S(1)}, f32[4,96,256]{2,1,0:T(8,128)S(1)}, u32[]{:S(2)}, u32[]{:S(2)}) %collective-permute-start.11) | collective-permute-done | bytes 393248 | tf_op jit(solution)/shard_map/ppermute | solution.py:590
  81.9 1.5 %collective-permute-done.12.mate_ref = f32[8,32,256]{2,1,0:T(8,128)S(1)} collective-permute-done((f32[8,32,256]{2,1,0:T(8,128)S(1)}, f32[8,32,256]{2,1,0:T(8,128)S(1)}, u32[]{:S(2)}, u32[]{:S(2)}) %collective-permute-start.12) | collective-permute-done | bytes 262176 | tf_op jit(solution)/shard_map/ppermute | solution.py:546
  83.4 6.4 %far.1.refs_0_ = f32[64,256]{1,0:T(8,128)S(1)} custom-call(s32[4,14]{1,0:T(4,128)S(1)} %bitcast.1, s32[6,256]{1,0:T(8,128)S(1)} %copy-done.6, f32[6,512,256]{2,1,0:T(8,128)S(1)} %copy-done.4, f32[4,96,256]{2,1,0:T(8,128)S(1)} %stack.2.alike_ref.refs_11_, f32[4,96,256]{2,1,0:T(8,128)S(1)} %collective-permute-done.11.beside_ref, ...), custom_call_target="tpu_custom_call" | custom-call | tf_op jit(solution)/shard_map/far/pallas_call | solution.py:465
  91.2 2.3 %collective-permute-start.16 = (f32[2,64,256]{2,1,0:T(8,128)S(1)}, f32[2,64,256]{2,1,0:T(8,128)S(1)}, u32[]{:S(2)}, u32[]{:S(2)}) collective-permute-start(f32[2,64,256]{2,1,0:T(8,128)S(1)} %stack.3.refs_0_), channel_id=1, source_target_pairs={{2,0},{3,1},{0,2},{1,3},{6,4},{7,5},{4,6},{5,7},{10,8},{11,9},{8,1... | collective-permute-start | bytes 393224 | tf_op jit(solution)/shard_map/ppermute | solution.py:546
  93.5 4.7 %collective-permute-done.19.refs_3_ = f32[128,1024]{1,0:T(8,128)S(1)} collective-permute-done((f32[128,1024]{1,0:T(8,128)S(1)}, f32[128,1024]{1,0:T(8,128)S(1)}, u32[]{:S(2)}, u32[]{:S(2)}) %collective-permute-start.19) | collective-permute-done | bytes 524320 | tf_op jit(solution)/shard_map/ppermute | solution.py:549
  98.3 1.9 %collective-permute-done.16.refs_1_ = f32[2,64,256]{2,1,0:T(8,128)S(1)} collective-permute-done((f32[2,64,256]{2,1,0:T(8,128)S(1)}, f32[2,64,256]{2,1,0:T(8,128)S(1)}, u32[]{:S(2)}, u32[]{:S(2)}) %collective-permute-start.16) | collective-permute-done | bytes 131104 | tf_op jit(solution)/shard_map/ppermute | solution.py:546
  100.3 1.6 %join.1 = f32[256,1024]{1,0:T(8,128)} custom-call(f32[2,512,256]{2,1,0:T(8,128)S(1)} %copy-done.3, f32[2,64,256]{2,1,0:T(8,128)S(1)} %stack.3.refs_0_, f32[2,64,256]{2,1,0:T(8,128)S(1)} %collective-permute-done.16.refs_1_, f32[128,1024]{1,0:T(8,128)S(1)} %get-tuple-element.71.refs_2_, f32[128,1024]{1,0:T(8,128)S(1)} %get-tuple-element.72.refs_3_, ...), custom_call_target="tpu_custom_call" | custom-call | tf_op jit(solution)/shard_map/join/pallas_call | solution.py:522
  (57 shorter events, 12.1 us)
Async XLA Ops:
  2.3 27.6 %collective-permute-start.2 = (f32[128,1024]{1,0:T(8,128)}, f32[128,1024]{1,0:T(8,128)}, u32[]{:S(2)}, u32[]{:S(2)}) collective-permute-start(f32[128,1024]{1,0:T(8,128)} %get-tuple-element.76), channel_id=1, source_target_pairs={{0,4},{4,0},{8,12},{12,8},{16,20},{20,16},{24,28},{28,24},{1,5},{5... | collective-permute-start | bytes 1572872 | tf_op jit(solution)/shard_map/ppermute | solution.py:561
  5.3 17.9 %collective-permute-start = (f32[64,1024]{1,0:T(8,128)}, f32[64,1024]{1,0:T(8,128)}, u32[]{:S(2)}, u32[]{:S(2)}) collective-permute-start(f32[64,1024]{1,0:T(8,128)} %pts_ref.1), channel_id=1, source_target_pairs={{0,4},{4,0},{8,12},{12,8},{16,20},{20,16},{24,28},{28,24},{1,5},{5... | collective-permute-start | bytes 786440 | tf_op jit(solution)/shard_map/ppermute | solution.py:560
  9.4 17.5 %collective-permute-start.3 = (f32[88,1024]{1,0:T(8,128)}, f32[88,1024]{1,0:T(8,128)S(1)}, u32[]{:S(2)}, u32[]{:S(2)}) collective-permute-start(f32[88,1024]{1,0:T(8,128)} %get-tuple-element.41), channel_id=1, source_target_pairs={{1,0},{0,1},{3,2},{2,3},{5,4},{4,5},{7,6},{6,7},{9,8},{8,9},{11,10... | collective-permute-start | bytes 1081352 | tf_op jit(solution)/shard_map/ppermute | solution.py:564
  9.5 26.7 %collective-permute-start.4 = (f32[88,1024]{1,0:T(8,128)}, f32[88,1024]{1,0:T(8,128)S(1)}, u32[]{:S(2)}, u32[]{:S(2)}) collective-permute-start(f32[88,1024]{1,0:T(8,128)} %get-tuple-element.47), channel_id=1, source_target_pairs={{2,0},{3,1},{0,2},{1,3},{6,4},{7,5},{4,6},{5,7},{10,8},{11,9},{8,1... | collective-permute-start | bytes 1081352 | tf_op jit(solution)/shard_map/ppermute | solution.py:564
  11.5 24.6 %collective-permute-start.5 = (f32[88,1024]{1,0:T(8,128)}, f32[88,1024]{1,0:T(8,128)S(1)}, u32[]{:S(2)}, u32[]{:S(2)}) collective-permute-start(f32[88,1024]{1,0:T(8,128)} %get-tuple-element.48), channel_id=1, source_target_pairs={{3,0},{2,1},{1,2},{0,3},{7,4},{6,5},{5,6},{4,7},{11,8},{10,9},{9,1... | collective-permute-start | bytes 1081352 | tf_op jit(solution)/shard_map/ppermute | solution.py:564
  23.1 8.7 %collective-permute-start.1 = (f32[64,1024]{1,0:T(8,128)}, f32[64,1024]{1,0:T(8,128)S(1)}, u32[]{:S(2)}, u32[]{:S(2)}) collective-permute-start(f32[64,1024]{1,0:T(8,128)} %collective-permute-done.pts_ref), channel_id=1, source_target_pairs={{0,8},{8,16},{16,24},{12,4},{20,12},{28,20},{1,9},{9,17},{17,25},{... | collective-permute-start | bytes 786440 | tf_op jit(solution)/shard_map/ppermute | solution.py:568
  26.8 12.8 %collective-permute-start.10 = (f32[128,1024]{1,0:T(8,128)}, f32[128,1024]{1,0:T(8,128)S(1)}, u32[]{:S(2)}, u32[]{:S(2)}) collective-permute-start(f32[128,1024]{1,0:T(8,128)} %get-tuple-element.75), channel_id=1, source_target_pairs={{0,4},{4,0},{8,12},{12,8},{16,20},{20,16},{24,28},{28,24},{1,5},{5... | collective-permute-start | bytes 1572872 | tf_op jit(solution)/shard_map/ppermute | solution.py:561
  31.8 28.8 %collective-permute-start.9 = (f32[128,1024]{1,0:T(8,128)}, f32[128,1024]{1,0:T(8,128)S(1)}, u32[]{:S(2)}, u32[]{:S(2)}) collective-permute-start(f32[128,1024]{1,0:T(8,128)} %collective-permute-done.2.refs_8_), channel_id=1, source_target_pairs={{0,8},{8,16},{16,24},{12,4},{20,12},{28,20},{1,9},{9,17},{17,25},{... | collective-permute-start | bytes 1572872 | tf_op jit(solution)/shard_map/ppermute | solution.py:571
  39.6 23.7 %collective-permute-start.13 = (f32[128,1024]{1,0:T(8,128)S(1)}, f32[128,1024]{1,0:T(8,128)S(1)}, u32[]{:S(2)}, u32[]{:S(2)}) collective-permute-start(f32[128,1024]{1,0:T(8,128)S(1)} %collective-permute-done.10.refs_9_), channel_id=1, source_target_pairs={{0,8},{8,16},{16,24},{12,4},{20,12},{28,20},{1,9},{9,17},{17,25},{... | collective-permute-start | bytes 1572872 | tf_op jit(solution)/shard_map/ppermute | solution.py:581
  43.1 18.8 %collective-permute-start.6 = (f32[96,256]{1,0:T(8,128)S(1)}, f32[96,256]{1,0:T(8,128)S(1)}, u32[]{:S(2)}, u32[]{:S(2)}) collective-permute-start(f32[96,256]{1,0:T(8,128)S(1)} %get-tuple-element.63.refs_0_), channel_id=1, source_target_pairs={{0,8},{4,12},{8,0},{12,4},{16,24},{20,28},{24,16},{28,20},{1,9},{5... | collective-permute-start | bytes 294920 | tf_op jit(solution)/shard_map/ppermute | solution.py:576
  44.7 17.5 %collective-permute-start.7 = (f32[96,256]{1,0:T(8,128)S(1)}, f32[96,256]{1,0:T(8,128)S(1)}, u32[]{:S(2)}, u32[]{:S(2)}) collective-permute-start(f32[96,256]{1,0:T(8,128)S(1)} %get-tuple-element.63.refs_0_), channel_id=1, source_target_pairs={{0,16},{4,20},{8,24},{12,28},{16,0},{20,4},{24,8},{28,12},{1,17},{... | collective-permute-start | bytes 294920 | tf_op jit(solution)/shard_map/ppermute | solution.py:576
  44.7 18.5 %collective-permute-start.8 = (f32[96,256]{1,0:T(8,128)S(1)}, f32[96,256]{1,0:T(8,128)S(1)}, u32[]{:S(2)}, u32[]{:S(2)}) collective-permute-start(f32[96,256]{1,0:T(8,128)S(1)} %get-tuple-element.63.refs_0_), channel_id=1, source_target_pairs={{0,24},{4,28},{8,16},{12,20},{16,8},{20,12},{24,0},{28,4},{1,25},{... | collective-permute-start | bytes 294920 | tf_op jit(solution)/shard_map/ppermute | solution.py:576
  61.5 10.6 %collective-permute-start.17 = (f32[128,1024]{1,0:T(8,128)S(1)}, f32[128,1024]{1,0:T(8,128)S(1)}, u32[]{:S(2)}, u32[]{:S(2)}) collective-permute-start(f32[128,1024]{1,0:T(8,128)S(1)} %get-tuple-element.62), channel_id=1, source_target_pairs={{1,0},{0,1},{3,2},{2,3},{5,4},{4,5},{7,6},{6,7},{9,8},{8,9},{11,10... | collective-permute-start | bytes 1572872 | tf_op jit(solution)/shard_map/ppermute | solution.py:546
  64.3 8.3 %collective-permute-start.14 = (f32[128,1024]{1,0:T(8,128)S(1)}, f32[128,1024]{1,0:T(8,128)S(1)}, u32[]{:S(2)}, u32[]{:S(2)}) collective-permute-start(f32[128,1024]{1,0:T(8,128)S(1)} %get-tuple-element.68), channel_id=1, source_target_pairs={{1,0},{0,1},{3,2},{2,3},{5,4},{4,5},{7,6},{6,7},{9,8},{8,9},{11,10... | collective-permute-start | bytes 1572872 | tf_op jit(solution)/shard_map/ppermute | solution.py:546
  64.4 17.4 %collective-permute-start.11 = (f32[4,96,256]{2,1,0:T(8,128)S(1)}, f32[4,96,256]{2,1,0:T(8,128)S(1)}, u32[]{:S(2)}, u32[]{:S(2)}) collective-permute-start(f32[4,96,256]{2,1,0:T(8,128)S(1)} %stack.2.alike_ref.refs_11_), channel_id=1, source_target_pairs={{0,4},{4,0},{8,12},{12,8},{16,20},{20,16},{24,28},{28,24},{1,5},{5... | collective-permute-start | bytes 1179656 | tf_op jit(solution)/shard_map/ppermute | solution.py:590
  72.1 21.3 %collective-permute-start.18 = (f32[128,1024]{1,0:T(8,128)S(1)}, f32[128,1024]{1,0:T(8,128)S(1)}, u32[]{:S(2)}, u32[]{:S(2)}) collective-permute-start(f32[128,1024]{1,0:T(8,128)S(1)} %add_parts.4), channel_id=1, source_target_pairs={{2,0},{3,1},{0,2},{1,3},{6,4},{7,5},{4,6},{5,7},{10,8},{11,9},{8,1... | collective-permute-start | bytes 1572872 | tf_op jit(solution)/shard_map/ppermute | solution.py:549
  72.7 10.7 %copy-start.6 = (s32[6,256]{1,0:T(8,128)S(1)}, s32[6,256]{1,0:T(8,128)}, u32[]{:S(2)}) copy-start(s32[6,256]{1,0:T(8,128)} %node_ref.1) | copy-start | bytes 18436
  72.7 25.5 %collective-permute-start.19 = (f32[128,1024]{1,0:T(8,128)S(1)}, f32[128,1024]{1,0:T(8,128)S(1)}, u32[]{:S(2)}, u32[]{:S(2)}) collective-permute-start(f32[128,1024]{1,0:T(8,128)S(1)} %add_parts.3.refs_15_), channel_id=1, source_target_pairs={{2,0},{3,1},{0,2},{1,3},{6,4},{7,5},{4,6},{5,7},{10,8},{11,9},{8,1... | collective-permute-start | bytes 1572872 | tf_op jit(solution)/shard_map/ppermute | solution.py:549
  77.6 22.6 %collective-permute-start.20 = (f32[128,1024]{1,0:T(8,128)S(1)}, f32[128,1024]{1,0:T(8,128)S(1)}, u32[]{:S(2)}, u32[]{:S(2)}) collective-permute-start(f32[128,1024]{1,0:T(8,128)S(1)} %get-tuple-element.73), channel_id=1, source_target_pairs={{1,0},{0,1},{3,2},{2,3},{5,4},{4,5},{7,6},{6,7},{9,8},{8,9},{11,10... | collective-permute-start | bytes 1572872 | tf_op jit(solution)/shard_map/ppermute | solution.py:546
  77.7 22.5 %collective-permute-start.21 = (f32[128,1024]{1,0:T(8,128)S(1)}, f32[128,1024]{1,0:T(8,128)S(1)}, u32[]{:S(2)}, u32[]{:S(2)}) collective-permute-start(f32[128,1024]{1,0:T(8,128)S(1)} %get-tuple-element.74), channel_id=1, source_target_pairs={{1,0},{0,1},{3,2},{2,3},{5,4},{4,5},{7,6},{6,7},{9,8},{8,9},{11,10... | collective-permute-start | bytes 1572872 | tf_op jit(solution)/shard_map/ppermute | solution.py:546
  81.8 1.6 %collective-permute-start.12 = (f32[8,32,256]{2,1,0:T(8,128)S(1)}, f32[8,32,256]{2,1,0:T(8,128)S(1)}, u32[]{:S(2)}, u32[]{:S(2)}) collective-permute-start(f32[8,32,256]{2,1,0:T(8,128)S(1)} %points_of.1), channel_id=1, source_target_pairs={{1,0},{0,1},{3,2},{2,3},{5,4},{4,5},{7,6},{6,7},{9,8},{8,9},{11,10... | collective-permute-start | bytes 786440 | tf_op jit(solution)/shard_map/ppermute | solution.py:546
  83.4 16.8 %copy-start.3 = (f32[2,512,256]{2,1,0:T(8,128)S(1)}, f32[2,512,256]{2,1,0:T(8,128)}, u32[]{:S(2)}) copy-start(f32[2,512,256]{2,1,0:T(8,128)} %interp_ref.1) | copy-start | bytes 3145732
  89.8 1.3 %collective-permute-start.15 = (f32[64,256]{1,0:T(8,128)S(1)}, f32[64,256]{1,0:T(8,128)S(1)}, u32[]{:S(2)}, u32[]{:S(2)}) collective-permute-start(f32[64,256]{1,0:T(8,128)S(1)} %far.1.refs_0_), channel_id=1, source_target_pairs={{1,0},{0,1},{3,2},{2,3},{5,4},{4,5},{7,6},{6,7},{9,8},{8,9},{11,10... | collective-permute-start | bytes 196616 | tf_op jit(solution)/shard_map/ppermute | solution.py:546
  91.2 9.1 %collective-permute-start.16 = (f32[2,64,256]{2,1,0:T(8,128)S(1)}, f32[2,64,256]{2,1,0:T(8,128)S(1)}, u32[]{:S(2)}, u32[]{:S(2)}) collective-permute-start(f32[2,64,256]{2,1,0:T(8,128)S(1)} %stack.3.refs_0_), channel_id=1, source_target_pairs={{2,0},{3,1},{0,2},{1,3},{6,4},{7,5},{4,6},{5,7},{10,8},{11,9},{8,1... | collective-permute-start | bytes 393224 | tf_op jit(solution)/shard_map/ppermute | solution.py:546
  (7 other events, 43.0 us)
